TPU v7x, 512 devices: a whole 4x4x16 slice. The times are simulated.
512 devices in a mesh: slab: 64 (over y, z), pencil: 8 (over x, core).
Axes of the slice: x: 4, y: 4, z: 16, core: 2. Of those that a mesh axis runs over, the one named last changes fastest.
Arguments:
- coefficients: bfloat16 [32768, 128], P(('slab', 'pencil')), may hold values from -6 to 6
- projection: bfloat16 [32768, 64, 128], P(('slab', 'pencil')), may hold values from -0.5 to 0.5
- near_blocks: bfloat16 [32768, 1, 128, 128], P(('slab', 'pencil')), may hold values from -0.5 to 0.5
- near_ids: int32 [32768, 1], P(('slab', 'pencil')), may hold values from 0 to 32767, as said below
- grid_slab: int32 [32768, 1], P(('slab', 'pencil')), may hold values from 0 to 63; in each aligned block of 64 rows (0 to 63, 64 to 127, ...) at most 2 rows name the same one
- anchors: int32 [3, 32768], P(None, ('slab', 'pencil')), may hold values from 0 to 124, as said below
- spectrum: float32 [512, 128, 1024], P('pencil', 'slab'), may hold values from 0.3 to 13500, as said below
Outputs:
- fields: float32 [32768, 128], P(('slab', 'pencil'))
Inputs may be any that keep to these rules, and one draw needn't show every extreme that they name: `grid_slab`: among the rows of one device at most 2 boxes name the same slab; in every draw some device names one slab exactly 2 times. `anchors`: row 0 lies in 0 to 4, row 1 in 0 to 124, row 2 in 0 to 124, so a stencil stays inside one device's block of the grid; each bound is reached. `near_ids`: box b's near ids name boxes of its own slab group, from 512 * (b // 512) to 512 * (b // 512) + 511. `spectrum`: the kernel is real and even: kernel at frequency (kx, kz, ky) equals kernel at ((512 - kx) % 512, (128 - kz) % 128, (1024 - ky) % 1024).
All inputs are finite; a program needn't handle non-finite values.
Results may differ from a plain program's by a relative error of at most 0.006.
Values may be sent and summed in bfloat16 or wider, within the bound.
No kernel may reach another device: no remote copies, remote signals or barrier semaphores. Data moves between devices by JAX's collectives and lax.ppermute only.
A program may use at most 64 MiB of HBM per device.

v0:
```python
import math

import jax
import jax.numpy as jnp
from jax import lax
from jax.sharding import PartitionSpec as P

STENCIL = 64


HIGH = lax.Precision.HIGHEST


def angles(rows, cols, length, sign):
    left = lax.broadcasted_iota(jnp.int32, (rows, cols), 0)
    right = lax.broadcasted_iota(jnp.int32, (rows, cols), 1)
    phase = jnp.mod(left * right, length).astype(jnp.float32) * (2.0 * math.pi / length)
    return (jnp.cos(phase), sign * jnp.sin(phase))


def slot_table(depth):
    slots = jnp.arange(depth, dtype=jnp.int32)
    pair = slots // 2
    frequency = jnp.where(slots % 2 == 0, pair, jnp.where(pair == 0, depth // 2, depth - pair))
    cells = jnp.arange(depth, dtype=jnp.int32)
    phase = jnp.mod(frequency[:, None] * cells[None, :], depth).astype(jnp.float32) * (
        2.0 * math.pi / depth
    )
    return (jnp.cos(phase), jnp.sin(phase))


def complex_apply(form, table_re, table_im, real_part, imag_part):
    first = jnp.einsum(form, table_re, real_part, precision=HIGH) - jnp.einsum(
        form, table_im, imag_part, precision=HIGH
    )
    second = jnp.einsum(form, table_re, imag_part, precision=HIGH) + jnp.einsum(
        form, table_im, real_part, precision=HIGH
    )
    return (first, second)


def twiddle(real_part, imag_part, table_re, table_im):
    return (
        real_part * table_re - imag_part * table_im,
        real_part * table_im + imag_part * table_re,
    )


def lead_dft(real_part, imag_part, sign):
    shape = real_part.shape
    length = shape[0]
    factor_one = max(
        (divisor for divisor in range(1, math.isqrt(length) + 1) if length % divisor == 0)
    )
    factor_two = length // factor_one
    real_part = real_part.reshape(factor_one, factor_two, -1)
    imag_part = imag_part.reshape(factor_one, factor_two, -1)
    step_re, step_im = angles(factor_one, factor_one, factor_one, sign)
    real_part, imag_part = complex_apply("pa,abr->pbr", step_re, step_im, real_part, imag_part)
    turn_re, turn_im = angles(factor_one, factor_two, length, sign)
    real_part, imag_part = twiddle(real_part, imag_part, turn_re[:, :, None], turn_im[:, :, None])
    last_re, last_im = angles(factor_two, factor_two, factor_two, sign)
    real_part, imag_part = complex_apply("qb,pbr->qpr", last_re, last_im, real_part, imag_part)
    return (real_part.reshape(shape), imag_part.reshape(shape))


def tail_split(length):
    inner = min(length, 128)
    return (length // inner, inner)


def tail_forward(real_part, imag_part):
    shape = real_part.shape
    length = shape[-1]
    outer, inner = tail_split(length)
    real_part = real_part.reshape(shape[:-1] + (outer, inner))
    imag_part = imag_part.reshape(shape[:-1] + (outer, inner))
    step_re, step_im = angles(outer, outer, outer, -1.0)
    real_part, imag_part = complex_apply("pa,...ab->...pb", step_re, step_im, real_part, imag_part)
    turn_re, turn_im = angles(outer, inner, length, -1.0)
    real_part, imag_part = twiddle(real_part, imag_part, turn_re, turn_im)
    last_re, last_im = angles(inner, inner, inner, -1.0)
    real_part, imag_part = complex_apply("qb,...pb->...pq", last_re, last_im, real_part, imag_part)
    return (real_part.reshape(shape), imag_part.reshape(shape))


def tail_inverse(real_part, imag_part):
    shape = real_part.shape
    length = shape[-1]
    outer, inner = tail_split(length)
    real_part = real_part.reshape(shape[:-1] + (outer, inner))
    imag_part = imag_part.reshape(shape[:-1] + (outer, inner))
    step_re, step_im = angles(inner, inner, inner, 1.0)
    real_part, imag_part = complex_apply("tq,...pq->...pt", step_re, step_im, real_part, imag_part)
    turn_re, turn_im = angles(outer, inner, length, 1.0)
    real_part, imag_part = twiddle(real_part, imag_part, turn_re, turn_im)
    last_re, last_im = angles(outer, outer, outer, 1.0)
    real_part, imag_part = complex_apply("sp,...pt->...st", last_re, last_im, real_part, imag_part)
    return (real_part.reshape(shape), imag_part.reshape(shape))


def per_device(coefficients, projection, near_blocks, near_ids, grid_slab, anchors, spectrum):
    box_count, funcs = coefficients.shape
    slab_count = lax.axis_size("slab")
    pencil_count = lax.axis_size("pencil")
    capacity = max(2, (2 * box_count + slab_count - 1) // slab_count)
    slot_count = slab_count * capacity
    depth = spectrum.shape[1] * slab_count
    lines_y = spectrum.shape[2]
    lines_x = spectrum.shape[0] * pencil_count
    cells_y = lines_y // pencil_count
    cells_x = lines_x // slab_count
    projected = jnp.einsum(
        "bnf,bf->bn", projection, coefficients, preferred_element_type=jnp.float32
    )
    target = grid_slab[:, 0]
    order = jnp.arange(box_count, dtype=jnp.int32)
    earlier = jnp.sum(
        ((target[:, None] == target[None, :]) & (order[:, None] > order[None, :])).astype(
            jnp.int32
        ),
        axis=1,
    )
    position = target * capacity + earlier
    picks = (
        lax.broadcasted_iota(jnp.int32, (slot_count, box_count), 0) == position[None, :]
    ).astype(jnp.float32)
    corner = (anchors[0] * (depth * cells_y) + anchors[2] * cells_y + anchors[1]).astype(
        jnp.float32
    )
    send_values = jnp.dot(picks, projected, precision=HIGH)
    send_corner = jnp.dot(picks, corner, precision=HIGH)
    recv_values, recv_corner = (
        lax.all_to_all(send_values, "slab", split_axis=0, concat_axis=0, tiled=True),
        lax.all_to_all(send_corner, "slab", split_axis=0, concat_axis=0, tiled=True),
    )
    node = jnp.arange(STENCIL, dtype=jnp.int32)
    offsets = node // 16 * (depth * cells_y) + node % 4 * cells_y + node // 4 % 4
    cells = recv_corner.astype(jnp.int32)[:, None] + offsets[None, :]
    grid = (
        jnp.zeros((cells_x * depth * cells_y,), jnp.float32)
        .at[cells.reshape(-1)]
        .add(recv_values.reshape(-1))
    )
    grid = grid.reshape(cells_x, depth, cells_y)
    cosine, sine = slot_table(depth)
    wave_re = jnp.einsum("kz,xzy->xky", cosine, grid, precision=HIGH)
    wave_im = jnp.einsum("kz,xzy->xky", -sine, grid, precision=HIGH)
    wave_re, wave_im = (
        lax.all_to_all(wave_re, "slab", split_axis=1, concat_axis=0, tiled=True),
        lax.all_to_all(wave_im, "slab", split_axis=1, concat_axis=0, tiled=True),
    )
    wave_re, wave_im = lead_dft(wave_re, wave_im, -1.0)
    wave_re, wave_im = (
        lax.all_to_all(wave_re, "pencil", split_axis=0, concat_axis=2, tiled=True),
        lax.all_to_all(wave_im, "pencil", split_axis=0, concat_axis=2, tiled=True),
    )
    wave_re, wave_im = tail_forward(wave_re, wave_im)
    outer, inner = tail_split(lines_y)
    local_shape = spectrum.shape
    arranged = (
        spectrum.reshape(local_shape[:2] + (inner, outer)).swapaxes(2, 3).reshape(local_shape)
    )
    arranged = arranged * (1.0 / (lines_x * lines_y * depth))
    wave_re = wave_re * arranged
    wave_im = wave_im * arranged
    wave_re, wave_im = tail_inverse(wave_re, wave_im)
    wave_re, wave_im = (
        lax.all_to_all(
            wave_re.astype(jnp.bfloat16), "pencil", split_axis=2, concat_axis=0, tiled=True
        ).astype(wave_re.dtype),
        lax.all_to_all(
            wave_im.astype(jnp.bfloat16), "pencil", split_axis=2, concat_axis=0, tiled=True
        ).astype(wave_im.dtype),
    )
    wave_re, wave_im = lead_dft(wave_re, wave_im, 1.0)
    back_re = cosine.T
    back_im = sine.T
    wave_re, wave_im = (
        lax.all_to_all(wave_re, "slab", split_axis=0, concat_axis=1, tiled=True),
        lax.all_to_all(wave_im, "slab", split_axis=0, concat_axis=1, tiled=True),
    )
    potential = jnp.einsum("zk,xky->xzy", back_re, wave_re, precision=HIGH) - jnp.einsum(
        "zk,xky->xzy", back_im, wave_im, precision=HIGH
    )
    sampled = potential.reshape(-1)[cells].astype(jnp.bfloat16)
    returned = lax.all_to_all(sampled, "slab", split_axis=0, concat_axis=0, tiled=True)
    unpick = (
        lax.broadcasted_iota(jnp.int32, (box_count, slot_count), 1) == position[:, None]
    ).astype(jnp.bfloat16)
    gathered_values = jnp.dot(unpick, returned, preferred_element_type=jnp.float32).astype(
        jnp.bfloat16
    )
    interp = jnp.einsum(
        "bnf,bn->bf", projection, gathered_values, preferred_element_type=jnp.float32
    )
    group_size = box_count * pencil_count
    local_ids = near_ids % group_size
    group_values = lax.all_gather(coefficients, "pencil", axis=0, tiled=True)
    partner = group_values[local_ids]
    close = jnp.einsum("bmgf,bmf->bg", near_blocks, partner, preferred_element_type=jnp.float32)
    return interp + close


def solution(mesh):
    placed = (
        P(("slab", "pencil"), None),
        P(("slab", "pencil"), None, None),
        P(("slab", "pencil"), None, None, None),
        P(("slab", "pencil"), None),
        P(("slab", "pencil"), None),
        P(None, ("slab", "pencil")),
        P("pencil", "slab", None),
    )
    return jax.shard_map(
        per_device,
        mesh=mesh,
        in_specs=placed,
        out_specs=P(("slab", "pencil"), None),
        check_vma=False,
    )
```

profile of v0, /device:TPU:1, one launch (start us, length us, event | category | flops | bytes accessed | tf_op | source)
XLA Modules:
  0.0 421.2 jit_solution(9777301345347023964)
XLA Ops:
  3.5 19.3 %all-to-all-start = ((f32[64,2,1]{1,2,0:T(1,128)}), f32[64,2,1]{1,2,0:T(1,128)S(1)}, u32[]{:S(2)}, u32[]{:S(2)}) async-start(f32[64,2,1]{1,2,0:T(1,128)} %copy.144), calls=%async_computation | async-start | bytes 65536 | tf_op jit(solution)/shard_map/all_to_all | solution.py:135
  22.9 1.9 fusion.90
  25.6 10.4 %all-to-all-done = f32[64,2,1]{1,2,0:T(1,128)S(1)} async-done(((f32[64,2,1]{1,2,0:T(1,128)}), f32[64,2,1]{1,2,0:T(1,128)S(1)}, u32[]{:S(2)}, u32[]{:S(2)}) %all-to-all-start) | async-done | bytes 544 | tf_op jit(solution)/shard_map/all_to_all | solution.py:135
  36.1 4.6 %all-to-all-start.1 = ((f32[64,1,128]{2,1,0:T(1,128)}), f32[64,1,128]{2,1,0:T(1,128)S(1)}, u32[]{:S(2)}, u32[]{:S(2)}) async-start(f32[64,1,128]{2,1,0:T(1,128)} %reshape.391), calls=%async_computation.1 | async-start | bytes 65536 | tf_op jit(solution)/shard_map/all_to_all | solution.py:134
  41.1 12.8 %all-to-all-done.1 = f32[64,1,128]{2,1,0:T(1,128)S(1)} async-done(((f32[64,1,128]{2,1,0:T(1,128)}), f32[64,1,128]{2,1,0:T(1,128)S(1)}, u32[]{:S(2)}, u32[]{:S(2)}) %all-to-all-start.1) | async-done | bytes 32800 | tf_op jit(solution)/shard_map/all_to_all | solution.py:134
  55.4 53.5 %scatter_custom_fusion = f32[131072]{0:T(1024)S(1)} fusion(s32[8192]{0:T(1024)S(1)} %bitcast.239, f32[8192]{0:T(1024)S(1)} %reshape.350, f32[]{:T(128)} %constant.204.clone.1), kind=kCustom, calls=%fused_computation.77 | custom fusion | flops 8192 | bytes 524292 | tf_op jit(solution)/shard_map/scatter-add | solution.py:143
  111.0 4.6 %all-to-all-start.2 = ((f32[8,128,128]{2,0,1:T(8,128)}), f32[8,128,128]{2,0,1:T(8,128)S(1)}, u32[]{:S(2)}, u32[]{:S(2)}) async-start(f32[8,128,128]{2,0,1:T(8,128)} %copy.147), calls=%async_computation.2 | async-start | bytes 1048576 | tf_op jit(solution)/shard_map/all_to_all | solution.py:150
  115.6 1.9 convolution_bitcast_fusion
  117.6 2.0 copy.150
  119.6 23.0 %all-to-all-done.2 = f32[8,128,128]{2,0,1:T(8,128)S(1)} async-done(((f32[8,128,128]{2,0,1:T(8,128)}), f32[8,128,128]{2,0,1:T(8,128)S(1)}, u32[]{:S(2)}, u32[]{:S(2)}) %all-to-all-start.2) | async-done | bytes 524320 | tf_op jit(solution)/shard_map/all_to_all | solution.py:150
  142.6 9.6 %all-to-all-start.3 = ((f32[8,128,128]{2,0,1:T(8,128)}), f32[8,128,128]{2,0,1:T(8,128)S(1)}, u32[]{:S(2)}, u32[]{:S(2)}) async-start(f32[8,128,128]{2,0,1:T(8,128)} %copy.150), calls=%async_computation.3 | async-start | bytes 1048576 | tf_op jit(solution)/shard_map/all_to_all | solution.py:151
  152.2 2.1 broadcast_multiply_fusion
  154.3 2.4 copy.164
  156.7 1.6 copy.165
  158.4 2.7 fusion.41
  161.1 18.8 %all-to-all-done.3 = f32[8,128,128]{2,0,1:T(8,128)S(1)} async-done(((f32[8,128,128]{2,0,1:T(8,128)}), f32[8,128,128]{2,0,1:T(8,128)S(1)}, u32[]{:S(2)}, u32[]{:S(2)}) %all-to-all-start.3) | async-done | bytes 524320 | tf_op jit(solution)/shard_map/all_to_all | solution.py:151
  180.7 1.9 convolution_subtract_fusion.8
  187.6 8.2 %all-to-all-start.4 = ((f32[512,2,128]{2,1,0:T(2,128)}), f32[512,2,128]{2,1,0:T(2,128)S(1)}, u32[]{:S(2)}, u32[]{:S(2)}) async-start(f32[512,2,128]{2,1,0:T(2,128)} %reshape.321), calls=%async_computation.4 | async-start | bytes 1048576 | tf_op jit(solution)/shard_map/all_to_all | solution.py:155
  195.8 1.9 fusion.31
  197.8 1.9 convolution_add_fusion.6
  200.8 2.1 reshape.322
  202.9 2.4 all-to-all-done.4
  205.3 5.1 %all-to-all-start.5 = ((f32[512,2,128]{2,1,0:T(2,128)}), f32[512,2,128]{2,1,0:T(2,128)}, u32[]{:S(2)}, u32[]{:S(2)}) async-start(f32[512,2,128]{2,1,0:T(2,128)} %reshape.322), calls=%async_computation.5 | async-start | bytes 1048576 | tf_op jit(solution)/shard_map/all_to_all | solution.py:156
  210.5 1.7 fusion.16
  212.2 7.6 %all-to-all-done.5 = f32[512,2,128]{2,1,0:T(2,128)} async-done(((f32[512,2,128]{2,1,0:T(2,128)}), f32[512,2,128]{2,1,0:T(2,128)}, u32[]{:S(2)}, u32[]{:S(2)}) %all-to-all-start.5) | async-done | bytes 524320 | tf_op jit(solution)/shard_map/all_to_all | solution.py:156
  219.8 1.9 fusion.12
  221.7 2.1 fusion.6
  232.0 1.4 fusion.53
  235.7 2.1 reshape.393
  237.8 4.8 %all-to-all-start.7 = ((bf16[8,2,8192]{2,1,0:T(2,128)(2,1)}), bf16[8,2,8192]{2,1,0:T(2,128)(2,1)}, u32[]{:S(2)}, u32[]{:S(2)}) async-start(bf16[8,2,8192]{2,1,0:T(2,128)(2,1)} %reshape.393), calls=%async_computation.7 | async-start | bytes 524288 | tf_op jit(solution)/shard_map/all_to_all | solution.py:172
  242.6 1.7 fusion.10
  245.7 3.5 all-to-all-done.7
  249.2 4.4 %all-to-all-start.6 = ((bf16[8,2,8192]{2,1,0:T(2,128)(2,1)}), bf16[8,2,8192]{2,1,0:T(2,128)(2,1)S(1)}, u32[]{:S(2)}, u32[]{:S(2)}) async-start(bf16[8,2,8192]{2,1,0:T(2,128)(2,1)} %reshape.395), calls=%async_computation.6 | async-start | bytes 524288 | tf_op jit(solution)/shard_map/all_to_all | solution.py:169
  253.6 1.3 reshape.394
  255.7 4.4 %all-to-all-done.6 = bf16[8,2,8192]{2,1,0:T(2,128)(2,1)S(1)} async-done(((bf16[8,2,8192]{2,1,0:T(2,128)(2,1)}), bf16[8,2,8192]{2,1,0:T(2,128)(2,1)S(1)}, u32[]{:S(2)}, u32[]{:S(2)}) %all-to-all-start.6) | async-done | bytes 262176 | tf_op jit(solution)/shard_map/all_to_all | solution.py:169
  266.0 2.1 reshape.326
  268.2 7.3 %all-to-all-start.9 = ((f32[512,2,128]{2,1,0:T(2,128)}), f32[512,2,128]{2,1,0:T(2,128)}, u32[]{:S(2)}, u32[]{:S(2)}) async-start(f32[512,2,128]{2,1,0:T(2,128)} %reshape.326), calls=%async_computation.9 | async-start | bytes 1048576 | tf_op jit(solution)/shard_map/all_to_all | solution.py:181
  278.6 25.6 %all-to-all-done.9 = f32[512,2,128]{2,1,0:T(2,128)} async-done(((f32[512,2,128]{2,1,0:T(2,128)}), f32[512,2,128]{2,1,0:T(2,128)}, u32[]{:S(2)}, u32[]{:S(2)}) %all-to-all-start.9) | async-done | bytes 524320 | tf_op jit(solution)/shard_map/all_to_all | solution.py:181
  304.2 9.0 %all-to-all-start.8 = ((f32[512,2,128]{2,1,0:T(2,128)}), f32[512,2,128]{2,1,0:T(2,128)S(1)}, u32[]{:S(2)}, u32[]{:S(2)}) async-start(f32[512,2,128]{2,1,0:T(2,128)} %reshape.325), calls=%async_computation.8 | async-start | bytes 1048576 | tf_op jit(solution)/shard_map/all_to_all | solution.py:180
  313.2 13.9 %all_gather.3 = bf16[512,128]{1,0:T(8,128)(2,1)S(1)} all-gather(bf16[64,128]{1,0:T(8,128)(2,1)S(1)} %copy-done.5), channel_id=1, replica_groups=mesh['slab'=64,'pencil'=8] {'pencil'}, dimensions={0}, use_global_device_ids=true | all-gather | bytes 147456 | tf_op jit(solution)/shard_map/all_gather | solution.py:199
  327.8 1.2 fusion
  330.3 12.0 %all-to-all-done.8 = f32[512,2,128]{2,1,0:T(2,128)S(1)} async-done(((f32[512,2,128]{2,1,0:T(2,128)}), f32[512,2,128]{2,1,0:T(2,128)S(1)}, u32[]{:S(2)}, u32[]{:S(2)}) %all-to-all-start.8) | async-done | bytes 524320 | tf_op jit(solution)/shard_map/all_to_all | solution.py:180
  342.4 1.2 fusion.19
  343.6 1.2 fusion.2
  345.0 50.7 %gather_fusion = bf16[8192]{0:T(1024)(128)(2,1)S(1)} fusion(bf16[131072]{0:T(1024)(128)(2,1)S(1)} %bitcast.214, s32[8192]{0:T(1024)S(1)} %broadcast_clamp_fusion), kind=kCustom, calls=%fused_computation | custom fusion | bytes 65536 | tf_op jit(solution)/shard_map/gather | solution.py:186
  396.5 8.9 %all-to-all-start.10 = ((bf16[64,2,64]{2,1,0:T(2,128)(2,1)}), bf16[64,2,64]{2,1,0:T(2,128)(2,1)S(1)}, u32[]{:S(2)}, u32[]{:S(2)}) async-start(bf16[64,2,64]{2,1,0:T(2,128)(2,1)} %convert_element_type.204), calls=%async_computation.10 | async-start | bytes 65536 | tf_op jit(solution)/shard_map/all_to_all | solution.py:187
  405.4 13.2 %all-to-all-done.10 = bf16[64,2,64]{2,1,0:T(2,128)(2,1)S(1)} async-done(((bf16[64,2,64]{2,1,0:T(2,128)(2,1)}), bf16[64,2,64]{2,1,0:T(2,128)(2,1)S(1)}, u32[]{:S(2)}, u32[]{:S(2)}) %all-to-all-start.10) | async-done | bytes 16416 | tf_op jit(solution)/shard_map/all_to_all | solution.py:187
  418.8 1.6 fusion.88
  (95 shorter events, 40.9 us)
Async XLA Ops:
  0.0 327.8 %copy-start = (bf16[64,1,128,128]{3,2,1,0:T(8,128)(2,1)S(1)}, bf16[64,1,128,128]{3,2,1,0:T(8,128)(2,1)}, u32[]{:S(2)}) copy-start(bf16[64,1,128,128]{3,2,1,0:T(8,128)(2,1)} %param.9) | copy-start | bytes 6291460
  3.5 32.5 %all-to-all-start = ((f32[64,2,1]{1,2,0:T(1,128)}), f32[64,2,1]{1,2,0:T(1,128)S(1)}, u32[]{:S(2)}, u32[]{:S(2)}) async-start(f32[64,2,1]{1,2,0:T(1,128)} %copy.144), calls=%async_computation | async-start | bytes 65536 | tf_op jit(solution)/shard_map/all_to_all | solution.py:135
  36.1 17.9 %all-to-all-start.1 = ((f32[64,1,128]{2,1,0:T(1,128)}), f32[64,1,128]{2,1,0:T(1,128)S(1)}, u32[]{:S(2)}, u32[]{:S(2)}) async-start(f32[64,1,128]{2,1,0:T(1,128)} %reshape.391), calls=%async_computation.1 | async-start | bytes 65536 | tf_op jit(solution)/shard_map/all_to_all | solution.py:134
  111.0 31.6 %all-to-all-start.2 = ((f32[8,128,128]{2,0,1:T(8,128)}), f32[8,128,128]{2,0,1:T(8,128)S(1)}, u32[]{:S(2)}, u32[]{:S(2)}) async-start(f32[8,128,128]{2,0,1:T(8,128)} %copy.147), calls=%async_computation.2 | async-start | bytes 1048576 | tf_op jit(solution)/shard_map/all_to_all | solution.py:150
  142.6 14.0 %copy-start.3 = (f32[8,128,128]{2,0,1:T(8,128)}, f32[8,128,128]{2,0,1:T(8,128)S(1)}, u32[]{:S(2)}) copy-start(f32[8,128,128]{2,0,1:T(8,128)S(1)} %all-to-all-done.2) | copy-start | bytes 1572868
  142.6 37.2 %all-to-all-start.3 = ((f32[8,128,128]{2,0,1:T(8,128)}), f32[8,128,128]{2,0,1:T(8,128)S(1)}, u32[]{:S(2)}, u32[]{:S(2)}) async-start(f32[8,128,128]{2,0,1:T(8,128)} %copy.150), calls=%async_computation.3 | async-start | bytes 1048576 | tf_op jit(solution)/shard_map/all_to_all | solution.py:151
  179.9 2.8 copy-start.4
  183.6 0.8 copy-start.1
  183.6 1.7 copy-start.2
  187.6 17.7 %all-to-all-start.4 = ((f32[512,2,128]{2,1,0:T(2,128)}), f32[512,2,128]{2,1,0:T(2,128)S(1)}, u32[]{:S(2)}, u32[]{:S(2)}) async-start(f32[512,2,128]{2,1,0:T(2,128)} %reshape.321), calls=%async_computation.4 | async-start | bytes 1048576 | tf_op jit(solution)/shard_map/all_to_all | solution.py:155
  205.3 14.5 %all-to-all-start.5 = ((f32[512,2,128]{2,1,0:T(2,128)}), f32[512,2,128]{2,1,0:T(2,128)}, u32[]{:S(2)}, u32[]{:S(2)}) async-start(f32[512,2,128]{2,1,0:T(2,128)} %reshape.322), calls=%async_computation.5 | async-start | bytes 1048576 | tf_op jit(solution)/shard_map/all_to_all | solution.py:156
  237.8 11.4 %all-to-all-start.7 = ((bf16[8,2,8192]{2,1,0:T(2,128)(2,1)}), bf16[8,2,8192]{2,1,0:T(2,128)(2,1)}, u32[]{:S(2)}, u32[]{:S(2)}) async-start(bf16[8,2,8192]{2,1,0:T(2,128)(2,1)} %reshape.393), calls=%async_computation.7 | async-start | bytes 524288 | tf_op jit(solution)/shard_map/all_to_all | solution.py:172
  249.2 10.9 %all-to-all-start.6 = ((bf16[8,2,8192]{2,1,0:T(2,128)(2,1)}), bf16[8,2,8192]{2,1,0:T(2,128)(2,1)S(1)}, u32[]{:S(2)}, u32[]{:S(2)}) async-start(bf16[8,2,8192]{2,1,0:T(2,128)(2,1)} %reshape.395), calls=%async_computation.6 | async-start | bytes 524288 | tf_op jit(solution)/shard_map/all_to_all | solution.py:169
  268.2 36.1 %all-to-all-start.9 = ((f32[512,2,128]{2,1,0:T(2,128)}), f32[512,2,128]{2,1,0:T(2,128)}, u32[]{:S(2)}, u32[]{:S(2)}) async-start(f32[512,2,128]{2,1,0:T(2,128)} %reshape.326), calls=%async_computation.9 | async-start | bytes 1048576 | tf_op jit(solution)/shard_map/all_to_all | solution.py:181
  276.3 36.9 %copy-start.5 = (bf16[64,128]{1,0:T(8,128)(2,1)S(1)}, bf16[64,128]{1,0:T(8,128)(2,1)}, u32[]{:S(2)}) copy-start(bf16[64,128]{1,0:T(8,128)(2,1)} %param.7) | copy-start | bytes 49156
  276.3 50.8 %copy-start.6 = (s32[64,1]{0,1:T(1,128)S(1)}, s32[64,1]{0,1:T(1,128)}, u32[]{:S(2)}) copy-start(s32[64,1]{0,1:T(1,128)} %param.10) | copy-start | bytes 772
  304.2 38.0 %all-to-all-start.8 = ((f32[512,2,128]{2,1,0:T(2,128)}), f32[512,2,128]{2,1,0:T(2,128)S(1)}, u32[]{:S(2)}, u32[]{:S(2)}) async-start(f32[512,2,128]{2,1,0:T(2,128)} %reshape.325), calls=%async_computation.8 | async-start | bytes 1048576 | tf_op jit(solution)/shard_map/all_to_all | solution.py:180
  345.0 60.4 %copy-start.7 = (s32[64,1]{0,1:T(1,128)S(1)}, s32[64,1]{0,1:T(1,128)}, u32[]{:S(2)}) copy-start(s32[64,1]{0,1:T(1,128)} %param.11) | copy-start | bytes 772
  396.5 22.2 %all-to-all-start.10 = ((bf16[64,2,64]{2,1,0:T(2,128)(2,1)}), bf16[64,2,64]{2,1,0:T(2,128)(2,1)S(1)}, u32[]{:S(2)}, u32[]{:S(2)}) async-start(bf16[64,2,64]{2,1,0:T(2,128)(2,1)} %convert_element_type.204), calls=%async_computation.10 | async-start | bytes 65536 | tf_op jit(solution)/shard_map/all_to_all | solution.py:187
where the time goes:
time: 430 us; the launch traced here: 421 us
  waiting for transfers between devices  134 us (31%)
  starting transfers between devices  85.7 us (20%)
  local copies, waits for them, and re-layouts  80.8 us (19%)
  other arithmetic  59.3 us (14%)
  matrix products  47 us (11%)
  blocking collectives  13.9 us (3%)
    scatter-add x1, other arithmetic, per_device(): grid = jnp.zeros((cells_x * depth * cells_y,), jnp.float32).at[cells.resh...  53.5 us
    gather x1, local copies, waits for them, and re-layouts, per_device(): sampled = potential.reshape(-1)[cells].astype(jnp.bfloat16)  50.7 us
    all_to_all x1, waiting for transfers between devices, per_device(): lax.all_to_all(wave_im, 'slab', split_axis=0, concat_axis=1, tiled=True)  25.6 us
    all_to_all x1, waiting for transfers between devices, per_device(): lax.all_to_all(wave_re, 'slab', split_axis=1, concat_axis=0, tiled=True)  23 us
    all_to_all x1, starting transfers between devices, per_device(): lax.all_to_all(send_corner, 'slab', split_axis=0, concat_axis=0, tiled=True)  19.3 us
    all_to_all x1, waiting for transfers between devices, per_device(): lax.all_to_all(wave_im, 'slab', split_axis=1, concat_axis=0, tiled=True)  18.8 us
    all_gather x1, blocking collectives, per_device(): group_values = lax.all_gather(coefficients, 'pencil', axis=0, tiled=True)  13.9 us
    all_to_all x1, waiting for transfers between devices, per_device(): lax.all_to_all(sampled, 'slab', split_axis=0, concat_axis=0, tiled=True)  13.2 us
  transfers between devices with their start and end apart: 11, of which 11 were waited for; matrix products, arithmetic and copies ran while one was open for 9% of the time, Pallas kernels for 0%

commit v1 on v0

v1 whole, which is shorter than its diff:
```python
import math

import jax
import jax.numpy as jnp
import numpy as np
from jax import lax
from jax.experimental import pallas as pl
from jax.experimental.pallas import tpu as pltpu
from jax.sharding import PartitionSpec as P

SLABS = 64
PENCILS = 8
BOX = 64
FUNCS = 128
STENCIL = 64
CX = 8
CY = 128
NX = 512
NY = 1024
NZ = 128
GROUP = BOX * PENCILS
ROWS = 24
LINES = NX // PENCILS
MORE = LINES + 8
BOXES = SLABS * BOX
TILE = 256

F32 = jnp.float32
BF16 = jnp.bfloat16
NT = (((1,), (1,)), ((), ()))
NN = (((1,), (0,)), ((), ()))


def halves(table):
    table = np.asarray(table, np.float32)
    high = table.astype(BF16)
    low = (table - high.astype(np.float32)).astype(BF16)
    return high, low


def x_table():
    phase = np.outer(np.arange(NX), np.arange(NX)) % NX * (2.0 * math.pi / NX)
    return np.concatenate([np.cos(phase), np.sin(phase)], 0)


def y_tables():
    phase = np.outer(np.arange(CY), np.arange(CY)) % CY * (2.0 * math.pi / CY)
    c, s = np.cos(phase), np.sin(phase)
    forward = np.block([[c, -s], [s, c]])
    inverse = np.block([[c, s], [-s, c]])
    turn = np.outer(np.arange(PENCILS), np.arange(CY)) * (2.0 * math.pi / NY)
    turn = np.concatenate([np.cos(turn), np.sin(turn)], 0).astype(np.float32)
    return forward, inverse, turn


def cosine_coefficients():
    fit = np.polynomial.chebyshev.Chebyshev.interpolate(
        lambda w: np.cos(2.0 * math.pi * np.sqrt(w)), 9, domain=[0.0, 0.25]
    )
    return [float(v) for v in fit.convert(kind=np.polynomial.Polynomial).coef]


COSINE = cosine_coefficients()


def cosine_of(step):
    u = (step.astype(F32) - (NZ // 2)) * (1.0 / NZ)
    w = u * u
    total = jnp.full_like(w, COSINE[-1])
    for value in COSINE[-2::-1]:
        total = total * w + value
    return -total


def iota(shape, axis):
    return lax.broadcasted_iota(jnp.int32, shape, axis)


def dot(a, b, dims=NN):
    return lax.dot_general(a, b, dims, preferred_element_type=F32)


def split(value):
    high = value.astype(BF16)
    return high, (value - high.astype(F32)).astype(BF16)


def project_kernel(meta_ref, coef_ref, proj_ref, send_ref, phase_ref, value_ref):
    coef = coef_ref[...]
    twice = jnp.concatenate([coef, coef], 0)
    lane = iota((STENCIL, 128), 1) & (BOX - 1)
    total = jnp.zeros((STENCIL, 128), F32)
    per = TILE // STENCIL
    for block in range(BOX // per):
        part = dot(proj_ref[block * TILE : (block + 1) * TILE, :], twice, NT)
        for t in range(per):
            total = jnp.where(
                lane == block * per + t, part[t * STENCIL : (t + 1) * STENCIL], total
            )
    value_ref[...] = total

    depth = meta_ref[0:1, :]
    second = (iota((SLABS, 128), 1) >= BOX).astype(jnp.int32)
    wave = iota((SLABS, 128), 0)
    for k in range(4):
        z = depth + k
        step = jnp.where(wave == 0, second * (NZ // 2) * z, wave * z + second * (NZ // 4))
        phase_ref[k] = cosine_of(step & (NZ - 1))

    turn = meta_ref[1:2, :] & 3
    row = iota((16, 128), 0) & 3
    parts = []
    for k in range(4):
        value = value_ref[pl.ds(k, 16, stride=4), :]
        out = value
        for m in range(1, 4):
            moved = jnp.where(row >= m, pltpu.roll(value, m, 0), pltpu.roll(value, m + 12, 0))
            out = jnp.where(turn == m, moved, out)
        parts.append(out)
    places = meta_ref[8:16, :].astype(F32)
    places = jnp.where(iota((8, 128), 1) < BOX, places * (1.0 / CX) - (SLABS // 2), places)
    for wave in range(SLABS):
        total = phase_ref[0, wave : wave + 1, :] * parts[0]
        for k in range(1, 4):
            total = total + phase_ref[k, wave : wave + 1, :] * parts[k]
        send_ref[wave] = jnp.concatenate([total, places], 0).astype(BF16)


def spread_kernel(place_ref, recv_ref, high_ref, low_ref, send_ref, pos_ref, row_ref, hot_ref):
    left = iota((ROWS, 128), 1) < BOX
    x_cells = iota((NX, 128), 0).astype(F32)
    y_cells = (iota((16, 8, 128), 0) * 8 + iota((16, 8, 128), 1)).astype(F32)
    upper = iota((8, 128), 0) < 4

    def fill(step, carry):
        for near in range(2):
            pair = step * 2 + near
            first = recv_ref[pair * 2].astype(F32)
            other = recv_ref[pair * 2 + 1].astype(F32)
            real = jnp.where(left, first, pltpu.roll(other, BOX, 1))
            imag = jnp.where(left, pltpu.roll(first, BOX, 1), other)
            x_place = (real[16:17] + (SLABS // 2)) * CX
            y_place = imag[16:17]
            pos_ref[pair] = jnp.concatenate(
                [x_place, y_place, jnp.zeros((6, 128), F32)], 0
            )
            start = pl.multiple_of(pair * 128, 128)
            away = y_cells - y_place[None]
            inside = (away >= 0.0) & (away < 4.0)
            for i in range(4):
                for c, source in enumerate((real, imag)):
                    block = source[8 * (i // 2) : 8 * (i // 2) + 8]
                    moved = pltpu.roll(block, 4, 0)
                    both = jnp.where(upper, block, moved) if i % 2 == 0 else jnp.where(upper, moved, block)
                    rows = jnp.where(inside, both[None], 0.0).reshape(CY, 128).astype(BF16)
                    row_ref[(2 * i + c) * CY : (2 * i + c + 1) * CY, pl.ds(start, 128)] = rows
            hot_ref[:, pl.ds(start, 128)] = jnp.where(x_cells == x_place, 1.0, 0.0).astype(BF16)
        return carry

    lax.fori_loop(0, SLABS // 4, fill, 0)
    plane = dot(row_ref[0 : 2 * CY, :], hot_ref[...], NT)
    for i in range(1, 4):
        part = dot(row_ref[2 * CY * i : 2 * CY * (i + 1), :], hot_ref[...], NT)
        plane = plane + pltpu.roll(part, i, 1)
    high, low = split(plane)
    table = high_ref[...]
    wave = dot(table, high, NT) + dot(table, low, NT) + dot(low_ref[...], high, NT)
    ac, bc = wave[:NX, :CY], wave[:NX, CY:]
    as_, bs = wave[NX:, :CY], wave[NX:, CY:]

    def put(real, imag):
        real = real.astype(BF16)
        imag = imag.astype(BF16)
        for r in range(PENCILS):
            send_ref[r, 0:LINES, :] = real[r * LINES : (r + 1) * LINES]
            send_ref[r, LINES : 2 * LINES, :] = imag[r * LINES : (r + 1) * LINES]

    @pl.when(place_ref[0] > 0)
    def _():
        put(ac + bs, bc - as_)

    @pl.when(place_ref[0] == 0)
    def _():
        line = iota((NX, CY), 0)
        real = jnp.where(line <= NX // 2, ac, bc)
        imag = jnp.where(line < NX // 2, -as_, -bs)
        put(real, jnp.where((line == 0) | (line == NX // 2), bc, imag))


def quarter(a, b, c, d, sign):
    def add(p, q):
        return (p[0] + q[0], p[1] + q[1])

    def sub(p, q):
        return (p[0] - q[0], p[1] - q[1])

    first, second, third, fourth = add(a, c), sub(a, c), add(b, d), sub(b, d)
    fourth = (-fourth[1], fourth[0]) if sign > 0 else (fourth[1], -fourth[0])
    return [add(first, third), add(second, fourth), sub(first, third), sub(second, fourth)]


def eighth(parts, sign):
    even = quarter(parts[0], parts[2], parts[4], parts[6], sign)
    odd = quarter(parts[1], parts[3], parts[5], parts[7], sign)
    root = math.sqrt(0.5)
    a, b = odd[1]
    odd[1] = ((a - sign * b) * root, (b + sign * a) * root)
    a, b = odd[2]
    odd[2] = (-sign * b, sign * a)
    a, b = odd[3]
    odd[3] = ((-a - sign * b) * root, (sign * a - b) * root)
    return [(e[0] + o[0], e[1] + o[1]) for e, o in zip(even, odd)] + [
        (e[0] - o[0], e[1] - o[1]) for e, o in zip(even, odd)
    ]


def times(value, table):
    high, low = split(value)
    return dot(high, table[0]) + dot(low, table[0]) + dot(high, table[1])


def line_kernel(place_ref, recv_ref, spec_ref, turn_ref, forward_ref, inverse_ref, send_ref):
    special = place_ref[1]
    top = (iota((8, CY), 0) == 0) & (special > 0)
    parts = []
    for q in range(PENCILS):
        real = recv_ref[q, 0:LINES, :].astype(F32)
        imag = recv_ref[q, LINES : 2 * LINES, :].astype(F32)
        first = imag[0:8]
        real = jnp.concatenate([real, jnp.where(top, first, 0.0)], 0)
        imag = jnp.concatenate(
            [jnp.where(top, 0.0, first), imag[8:], jnp.zeros((8, CY), F32)], 0
        )
        parts.append((real, imag))
    parts = eighth(parts, -1)
    lines = []
    for k in range(PENCILS):
        real, imag = parts[k]
        if k > 0:
            c = turn_ref[k : k + 1, :]
            s = turn_ref[PENCILS + k : PENCILS + k + 1, :]
            real, imag = real * c + imag * s, imag * c - real * s
        lines.append(jnp.concatenate([real, imag], 1))
    wave = times(jnp.concatenate(lines, 0), (forward_ref[0], forward_ref[1]))
    spec = spec_ref[...]
    wave = wave * jnp.concatenate([spec, spec], 1)
    wave = times(wave, (inverse_ref[0], inverse_ref[1]))
    parts = []
    for k in range(PENCILS):
        real = wave[k * MORE : (k + 1) * MORE, :CY]
        imag = wave[k * MORE : (k + 1) * MORE, CY:]
        if k > 0:
            c = turn_ref[k : k + 1, :]
            s = turn_ref[PENCILS + k : PENCILS + k + 1, :]
            real, imag = real * c - imag * s, imag * c + real * s
        parts.append((real, imag))
    parts = eighth(parts, 1)
    for q in range(PENCILS):
        real, imag = parts[q]
        send_ref[q] = jnp.concatenate(
            [
                real[0:8] - imag[LINES:],
                real[8:LINES],
                imag[0:8] + real[LINES:],
                imag[8:LINES],
            ],
            0,
        ).astype(BF16)


def sample_kernel(place_ref, pos_ref, recv_ref, high_ref, low_ref, send_ref, left_ref, wave_ref):
    real = jnp.concatenate([recv_ref[r, 0:LINES, :] for r in range(PENCILS)], 0)
    imag = jnp.concatenate([recv_ref[r, LINES : 2 * LINES, :] for r in range(PENCILS)], 0)

    @pl.when(place_ref[0] > 0)
    def _():
        wave_ref[0:NX, 0:CY] = real
        wave_ref[0:NX, CY:] = imag
        wave_ref[NX:, 0:CY] = -imag
        wave_ref[NX:, CY:] = real

    @pl.when(place_ref[0] == 0)
    def _():
        re = real.astype(F32)
        im = imag.astype(F32)
        line = iota((NX, CY), 0)
        ends = (line == 0) | (line == NX // 2)
        low = line < NX // 2
        wave_ref[0:NX, 0:CY] = jnp.where(
            ends, re, jnp.where(low, 2.0 * re, 0.0)
        ).astype(BF16)
        wave_ref[0:NX, CY:] = jnp.where(ends, im, jnp.where(low, 0.0, 2.0 * re)).astype(BF16)
        wave_ref[NX:, 0:CY] = jnp.where(
            ends, 0.0, jnp.where(low, -2.0 * im, 0.0)
        ).astype(BF16)
        wave_ref[NX:, CY:] = jnp.where(ends, 0.0, jnp.where(low, 0.0, -2.0 * im)).astype(BF16)

    cosine, sine = wave_ref[0:NX, :], wave_ref[NX:, :]
    plane = dot(high_ref[0:NX, :], cosine) + dot(high_ref[NX:, :], sine)
    plane = plane + dot(low_ref[0:NX, :], cosine) + dot(low_ref[NX:, :], sine)
    plane = plane.T
    for i in range(4):
        moved = plane if i == 0 else pltpu.roll(plane, NX - i, 1)
        left_ref[2 * CY * i : 2 * CY * (i + 1), :] = moved.astype(BF16)

    x_cells = iota((NX, 128), 0).astype(F32)
    y_cells = (iota((16, 8, 128), 0) * 8 + iota((16, 8, 128), 1)).astype(F32)
    upper = iota((8, 128), 0) < 4
    side = iota((16, 128), 1) < BOX

    def gather(step, carry):
        pairs = [step * 2, step * 2 + 1]
        hot, inside = [], []
        for pair in pairs:
            place = pos_ref[pair]
            hot.append(jnp.where(x_cells == place[0:1], 1.0, 0.0).astype(BF16))
            away = y_cells - place[1:2][None]
            inside.append((away >= 0.0) & (away < 4.0))
        hot = jnp.concatenate(hot, 1)
        found = [[[], []], [[], []]]
        for i in range(4):
            part = dot(left_ref[2 * CY * i : 2 * CY * (i + 1), :], hot)
            for near in range(2):
                for c in range(2):
                    block = part[c * CY : (c + 1) * CY, near * 128 : (near + 1) * 128]
                    block = jnp.where(inside[near], block.reshape(16, 8, 128), 0.0)
                    block = jnp.sum(block, axis=0)
                    found[near][c].append(block + pltpu.roll(block, 4, 0))
        for near in range(2):
            real, imag = [
                jnp.concatenate(
                    [jnp.where(upper, f[0], f[1]), jnp.where(upper, f[2], f[3])], 0
                )
                for f in found[near]
            ]
            pair = pairs[near]
            send_ref[pair * 2] = jnp.where(side, real, pltpu.roll(imag, BOX, 1)).astype(BF16)
            send_ref[pair * 2 + 1] = jnp.where(side, pltpu.roll(real, BOX, 1), imag).astype(BF16)
        return carry

    lax.fori_loop(0, SLABS // 4, gather, 0)


def finish_kernel(meta_ref, phase_ref, recv_ref, proj_ref, close_ref, out_ref, value_ref, wide_ref):
    totals = [jnp.zeros((16, 128), F32) for _ in range(4)]
    for wave in range(SLABS):
        value = recv_ref[wave].astype(F32)
        for k in range(4):
            totals[k] = totals[k] + phase_ref[k, wave : wave + 1, :] * value
    turn = meta_ref[1:2, :] & 3
    row = iota((16, 128), 0) & 3
    for k in range(4):
        value = totals[k] + pltpu.roll(totals[k], BOX, 1)
        out = value
        for m in range(1, 4):
            moved = jnp.where(
                row + m < 4, pltpu.roll(value, 16 - m, 0), pltpu.roll(value, 4 - m, 0)
            )
            out = jnp.where(turn == m, moved, out)
        value_ref[pl.ds(k, 16, stride=4), :] = out
    value = value_ref[...].astype(BF16).astype(F32)
    value = jnp.concatenate([value, value], 0).T[0:BOX]
    box = iota((BOX, 128), 0)
    half = (iota((BOX, 128), 1) >= STENCIL).astype(jnp.int32)
    for m in range(BOX // 2):
        wide_ref[:, 128 * m : 128 * (m + 1)] = jnp.where(
            box == 2 * m + half, value, 0.0
        ).astype(BF16)
    out_ref[...] = dot(wide_ref[...], proj_ref[...]) + close_ref[...]


def near_kernel(ids_ref, group_ref, near_ref, out_ref):
    hot = jnp.where(iota((BOX, GROUP), 1) == ids_ref[...], 1.0, 0.0).astype(BF16)
    partner = dot(hot, group_ref[...]).astype(BF16)
    twice = jnp.concatenate([partner, partner], 0)
    lane = iota((FUNCS, 128), 1) & (BOX - 1)

    def step(index, total):
        start = pl.multiple_of(index * 512, 512)
        part = dot(near_ref[pl.ds(start, 512), :], twice, NT)
        for t in range(4):
            total = jnp.where(lane == index * 4 + t, part[t * FUNCS : (t + 1) * FUNCS], total)
        return total

    total = lax.fori_loop(0, BOX // 4, step, jnp.zeros((FUNCS, 128), F32))
    out_ref[...] = total.T[0:BOX]


VMEM = pl.BlockSpec(memory_space=pltpu.VMEM)
SMEM = pl.BlockSpec(memory_space=pltpu.SMEM)


def call(kernel, shapes, specs, scratch=(), limit=32, flops=0, moved=0):
    return pl.pallas_call(
        kernel,
        out_shape=shapes,
        in_specs=specs,
        out_specs=jax.tree.map(lambda _: VMEM, shapes),
        scratch_shapes=list(scratch),
        compiler_params=pltpu.CompilerParams(vmem_limit_bytes=limit * 1024 * 1024),
        cost_estimate=pl.CostEstimate(flops=flops, bytes_accessed=moved, transcendentals=0),
    )


def struct(*shape, kind=F32):
    return jax.ShapeDtypeStruct(shape, kind)


def project(meta, coefficients, flat):
    return call(
        project_kernel,
        (struct(SLABS, ROWS, 128, kind=BF16), struct(4, SLABS, 128)),
        [VMEM] * 3,
        [pltpu.VMEM((STENCIL, 128), F32)],
        flops=2 * BOXES * FUNCS * 128,
        moved=2 << 20,
    )(meta, coefficients, flat)


def spread(place, received, high, low):
    return call(
        spread_kernel,
        (struct(PENCILS, 2 * LINES, CY, kind=BF16), struct(SLABS // 2, 8, 128)),
        [SMEM] + [VMEM] * 3,
        [pltpu.VMEM((8 * CY, BOXES), BF16), pltpu.VMEM((NX, BOXES), BF16)],
        limit=48,
        flops=2 * BOXES * NX * 8 * CY,
        moved=4 << 20,
    )(place, received, high, low)


def lines(place, received, spec, turn, forward, inverse):
    return call(
        line_kernel,
        struct(PENCILS, 2 * LINES, CY, kind=BF16),
        [SMEM] + [VMEM] * 5,
        flops=2 * 6 * PENCILS * MORE * 256 * 256,
        moved=2 << 20,
    )(place, received, spec, turn, forward, inverse)


def sample(place, pos, received, high, low):
    return call(
        sample_kernel,
        struct(SLABS, 16, 128, kind=BF16),
        [SMEM] + [VMEM] * 4,
        [pltpu.VMEM((8 * CY, NX), BF16), pltpu.VMEM((2 * NX, 2 * CY), BF16)],
        limit=32,
        flops=2 * BOXES * NX * 8 * CY,
        moved=4 << 20,
    )(place, pos, received, high, low)


def finish(meta, phase, received, flat, close):
    return call(
        finish_kernel,
        struct(BOX, FUNCS),
        [VMEM] * 5,
        [pltpu.VMEM((STENCIL, 128), F32), pltpu.VMEM((BOX, BOX * STENCIL), BF16)],
        flops=2 * BOX * BOXES * FUNCS,
        moved=2 << 20,
    )(meta, phase, received, flat, close)


def near(ids, group, blocks):
    return call(
        near_kernel,
        struct(BOX, FUNCS),
        [VMEM] * 3,
        flops=2 * BOX * FUNCS * FUNCS * 128,
        moved=3 << 20,
    )(ids, group, blocks)


def arrange(spectrum, slab, pencil):
    first, second = spectrum[:, 0, :], spectrum[:, 1, :]
    chosen = jnp.where((slab == 0) & (pencil >= PENCILS // 2), second, first)
    head = jnp.where((slab == 0) & (pencil == PENCILS // 2), first[0:1], chosen[0:1])
    rows = jnp.concatenate([head, chosen[1:], jnp.broadcast_to(second[0:1], (8, NY))], 0)
    rows = rows * jnp.where(slab == 0, 1.0, 2.0) * (1.0 / (NX * NY * NZ))
    return rows.reshape(MORE, CY, PENCILS).transpose(2, 0, 1).reshape(PENCILS * MORE, CY)


def describe(anchors, grid_slab):
    def twice(row):
        return jnp.concatenate([row, row])[None]

    x_place = grid_slab[:, 0] * CX + anchors[0]
    place = jnp.concatenate([x_place, anchors[1]])[None]
    return jnp.concatenate(
        [
            twice(anchors[2]),
            twice(anchors[1]),
            jnp.zeros((6, 128), jnp.int32),
            place,
            jnp.zeros((7, 128), jnp.int32),
        ],
        0,
    )


def per_device(coefficients, projection, near_blocks, near_ids, grid_slab, anchors, spectrum):
    slab = lax.axis_index("slab")
    pencil = lax.axis_index("pencil")
    special = (slab == 0) & (pencil % (PENCILS // 2) == 0)
    place = jnp.stack([slab, special.astype(jnp.int32)]).astype(jnp.int32)
    flat = projection.reshape(BOX * STENCIL, FUNCS)
    meta = describe(anchors, grid_slab)
    x_high, x_low = halves(x_table())
    forward, inverse, turn = y_tables()
    forward, inverse = np.stack(halves(forward)), np.stack(halves(inverse))

    send, phase = project(meta, coefficients, flat)
    received = lax.all_to_all(send, "slab", split_axis=0, concat_axis=0, tiled=True)
    spec = arrange(spectrum, slab, pencil)
    group = lax.all_gather(coefficients, "pencil", axis=0, tiled=True)
    close = near(near_ids & (GROUP - 1), group, near_blocks.reshape(BOX * FUNCS, FUNCS))
    send, pos = spread(place, received, x_high, x_low)
    received = lax.all_to_all(send, "pencil", split_axis=0, concat_axis=0, tiled=True)
    send = lines(place, received, spec, turn, forward, inverse)
    received = lax.all_to_all(send, "pencil", split_axis=0, concat_axis=0, tiled=True)
    send = sample(place, pos, received, x_high, x_low)
    received = lax.all_to_all(send, "slab", split_axis=0, concat_axis=0, tiled=True)
    return finish(meta, phase, received, flat, close)


def solution(mesh):
    placed = (
        P(("slab", "pencil"), None),
        P(("slab", "pencil"), None, None),
        P(("slab", "pencil"), None, None, None),
        P(("slab", "pencil"), None),
        P(("slab", "pencil"), None),
        P(None, ("slab", "pencil")),
        P("pencil", "slab", None),
    )
    return jax.shard_map(
        per_device,
        mesh=mesh,
        in_specs=placed,
        out_specs=P(("slab", "pencil"), None),
        check_vma=False,
    )
```

time: 430 us -> 131 us (0.30)
  the two profiles are of different devices: /device:TPU:1 before, /device:TPU:8 now
where the time goes in v1:
time: 131 us; the launch traced here: 130 us
  waiting for transfers between devices  32.2 us (25%)
  Pallas kernels  30.9 us (24%)
  starting transfers between devices  29.9 us (23%)
  blocking collectives  22.7 us (17%)
  local copies, waits for them, and re-layouts  9.67 us (7%)
  other arithmetic  4.49 us (3%)
    all_to_all x2, waiting for transfers between devices, per_device(): lax.all_to_all(send, 'slab', split_axis=0, concat_axis=0, tiled=True)  28.8 us
    all_to_all x2, starting transfers between devices, per_device(): lax.all_to_all(send, 'slab', split_axis=0, concat_axis=0, tiled=True)  25.6 us
    pallas_call x1, Pallas kernels, spread(): call(spread_kernel, (struct(PENCILS, 2 * LINES, CY, kind=BF16), struct(SL...  13 us
    all_gather x1, blocking collectives, per_device(): group = lax.all_gather(coefficients, 'pencil', axis=0, tiled=True)  12.8 us
    pallas_call x1, Pallas kernels, sample(): call(sample_kernel, struct(SLABS, 16, 128, kind=BF16), [SMEM] + [VMEM] *...  10.2 us
    all_to_all x1, blocking collectives, per_device(): lax.all_to_all(send, 'pencil', split_axis=0, concat_axis=0, tiled=True)  9.95 us
    unnamed x33, local copies, waits for them, and re-layouts  6.78 us
    all_to_all x1, starting transfers between devices, per_device(): lax.all_to_all(send, 'pencil', split_axis=0, concat_axis=0, tiled=True)  4.3 us
  transfers between devices with their start and end apart: 3, of which 3 were waited for; matrix products, arithmetic and copies ran while one was open for 4% of the time, Pallas kernels for 3%

profile of v1, /device:TPU:8, one launch (start us, length us, event | category | flops | bytes accessed | tf_op | source)
XLA Modules:
  0.0 130.0 jit_solution(9363112485822826488)
XLA Ops:
  0.0 0.8 slice_bitcast_fusion
  0.8 0.7 bitcast_add_fusion
  1.4 0.1 add_bitcast_fusion
  1.5 0.1 add_bitcast_fusion.2
  1.6 0.0 copy-start
  1.6 1.2 copy-done
  2.9 0.7 copy-done.6
  3.6 1.4 %shard_map.118 = (bf16[64,24,128]{2,1,0:T(8,128)(2,1)}, f32[4,64,128]{2,1,0:T(8,128)S(1)}) custom-call(s32[16,128]{1,0:T(8,128)S(1)} %concatenate.23.meta_ref, bf16[64,128]{1,0:T(8,128)(2,1)S(1)} %copy-done.6, bf16[4096,128]{1,0:T(8,128)(2,1)S(1)} %bitcast.22), custom_call_target="tpu_custom_call" | custom-call | flops 134217728 | bytes 2097152 | tf_op jit(solution)/shard_map/pallas_call | solution.py:410
  5.0 0.6 copy-done.4
  5.6 18.7 %all-to-all-start = ((bf16[64,24,128]{2,1,0:T(8,128)(2,1)}), bf16[64,24,128]{2,1,0:T(8,128)(2,1)S(1)}, u32[]{:S(2)}, u32[]{:S(2)}) async-start(bf16[64,24,128]{2,1,0:T(8,128)(2,1)} %get-tuple-element.10), calls=%async_computation | async-start | bytes 786432 | tf_op jit(solution)/shard_map/all_to_all | solution.py:514
  24.4 1.6 %broadcast_select_fusion = f32[64,1,1024]{2,1,0:T(1,128)S(1)} fusion(pred[]{:T(512)S(6)} %and.25, f32[64,2,1024]{2,1,0:T(2,128)} %param.18), kind=kLoop, calls=%fused_computation.3 | loop fusion | flops 65536 | bytes 786433 | tf_op jit(solution)/shard_map/jit(_where)/select_n | solution.py:477
  26.1 0.1 pad_add_fusion.place_ref
  26.1 24.5 %all-to-all-done.recv_ref = bf16[64,24,128]{2,1,0:T(8,128)(2,1)S(1)} async-done(((bf16[64,24,128]{2,1,0:T(8,128)(2,1)}), bf16[64,24,128]{2,1,0:T(8,128)(2,1)S(1)}, u32[]{:S(2)}, u32[]{:S(2)}) %all-to-all-start) | async-done | bytes 393248 | tf_op jit(solution)/shard_map/all_to_all | solution.py:514
  50.6 0.0 copy-done.8
  50.6 0.0 copy-done.10
  50.6 13.0 %shard_map.119 = (bf16[8,128,128]{2,1,0:T(8,128)(2,1)}, f32[32,8,128]{2,1,0:T(8,128)S(1)}) custom-call(s32[2]{0:T(128)S(1)} %pad_add_fusion.place_ref, bf16[64,24,128]{2,1,0:T(8,128)(2,1)S(1)} %all-to-all-done.recv_ref, bf16[1024,512]{1,0:T(8,128)(2,1)S(1)} %copy-done.10, bf16[1024,512]{1,0:T(8,128)(2,1)S(1)} %copy-done.8), custom_call_target="tpu_custom_call" | custom-call | flops 4294967296 | bytes 4194304 | tf_op jit(solution)/shard_map/pallas_call | solution.py:421
  63.6 4.3 %all-to-all-start.1 = ((bf16[8,128,128]{2,1,0:T(8,128)(2,1)}), bf16[8,128,128]{2,1,0:T(8,128)(2,1)S(1)}, u32[]{:S(2)}, u32[]{:S(2)}) async-start(bf16[8,128,128]{2,1,0:T(8,128)(2,1)} %get-tuple-element.12), calls=%async_computation.1 | async-start | bytes 524288 | tf_op jit(solution)/shard_map/all_to_all | solution.py:519
  67.9 0.8 fusion.2
  68.7 0.1 broadcast_in_dim.27
  68.8 0.2 copy.21
  69.0 0.0 copy-start.12
  69.1 0.0 copy-start.13
  69.1 0.0 copy-start.14
  69.1 0.3 concatenate.27
  69.4 0.2 broadcast_in_dim.28
  69.6 1.2 fusion.1
  70.8 1.2 copy.23
  72.0 3.4 %all-to-all-done.1.recv_ref = bf16[8,128,128]{2,1,0:T(8,128)(2,1)S(1)} async-done(((bf16[8,128,128]{2,1,0:T(8,128)(2,1)}), bf16[8,128,128]{2,1,0:T(8,128)(2,1)S(1)}, u32[]{:S(2)}, u32[]{:S(2)}) %all-to-all-start.1) | async-done | bytes 262176 | tf_op jit(solution)/shard_map/all_to_all | solution.py:519
  75.5 0.0 copy-done.12
  75.5 0.0 copy-done.13
  75.5 0.0 copy-done.14
  75.5 1.7 %shard_map.120 = bf16[8,128,128]{2,1,0:T(8,128)(2,1)S(1)} custom-call(s32[2]{0:T(128)S(1)} %pad_add_fusion.place_ref, bf16[8,128,128]{2,1,0:T(8,128)(2,1)S(1)} %all-to-all-done.1.recv_ref, f32[576,128]{1,0:T(8,128)S(1)} %bitcast.25, f32[16,128]{1,0:T(8,128)S(1)} %copy-done.14, bf16[2,256,256]{2,1,0:T(8,128)(2,1)S(1)} %copy-done.13, ...), custom_call_target="tpu_custom_call" | custom-call | flops 452984832 | bytes 2097152 | tf_op jit(solution)/shard_map/pallas_call | solution.py:433
  77.2 9.9 %all_to_all.20.recv_ref = bf16[8,128,128]{2,1,0:T(8,128)(2,1)S(1)} all-to-all(bf16[8,128,128]{2,1,0:T(8,128)(2,1)S(1)} %shard_map.120), channel_id=1, replica_groups=mesh['slab'=64,'pencil'=8] {'pencil'}, dimensions={0} | all-to-all | bytes 524288 | tf_op jit(solution)/shard_map/all_to_all | solution.py:521
  87.1 1.2 copy-done.9
  88.3 1.2 copy-done.11
  89.6 10.2 %shard_map.121 = bf16[64,16,128]{2,1,0:T(8,128)(2,1)S(1)} custom-call(s32[2]{0:T(128)S(1)} %pad_add_fusion.place_ref, f32[32,8,128]{2,1,0:T(8,128)S(1)} %get-tuple-element.11.pos_ref, bf16[8,128,128]{2,1,0:T(8,128)(2,1)S(1)} %all_to_all.20.recv_ref, bf16[1024,512]{1,0:T(8,128)(2,1)S(1)} %copy-done.11, bf16[1024,512]{1,0:T(8,128)(2,1)S(1)} %copy-done.9), custom_call_target="tpu_custom_call" | custom-call | flops 4294967296 | bytes 4194304 | tf_op jit(solution)/shard_map/pallas_call | solution.py:443
  99.7 0.7 copy-done.3
  100.4 6.8 %all-to-all-start.3 = ((bf16[64,16,128]{2,1,0:T(8,128)(2,1)}), bf16[64,16,128]{2,1,0:T(8,128)(2,1)S(1)}, u32[]{:S(2)}, u32[]{:S(2)}) async-start(bf16[64,16,128]{2,1,0:T(8,128)(2,1)} %copy-done.3), calls=%async_computation.3 | async-start | bytes 524288 | tf_op jit(solution)/shard_map/all_to_all | solution.py:523
  107.3 0.0 copy-done.15
  107.3 0.1 copy.24
  107.4 0.0 copy-done.7
  107.4 12.8 %all_gather.3.group_ref = bf16[512,128]{1,0:T(8,128)(2,1)S(1)} all-gather(bf16[64,128]{1,0:T(8,128)(2,1)S(1)} %copy-done.7), channel_id=1, replica_groups=mesh['slab'=64,'pencil'=8] {'pencil'}, dimensions={0}, use_global_device_ids=true | all-gather | bytes 147456 | tf_op jit(solution)/shard_map/all_gather | solution.py:516
  120.2 0.0 copy-done.2
  120.2 3.3 %shard_map.122.close_ref = f32[64,128]{1,0:T(8,128)S(1)} custom-call(s32[64,1]{1,0:T(8,128)S(1)} %broadcast_and_fusion.ids_ref, bf16[512,128]{1,0:T(8,128)(2,1)S(1)} %all_gather.3.group_ref, bf16[8192,128]{1,0:T(8,128)(2,1)S(1)} %bitcast.24), custom_call_target="tpu_custom_call" | custom-call | flops 268435456 | bytes 3145728 | tf_op jit(solution)/shard_map/pallas_call | solution.py:466
  123.5 4.3 %all-to-all-done.3.recv_ref = bf16[64,16,128]{2,1,0:T(8,128)(2,1)S(1)} async-done(((bf16[64,16,128]{2,1,0:T(8,128)(2,1)}), bf16[64,16,128]{2,1,0:T(8,128)(2,1)S(1)}, u32[]{:S(2)}, u32[]{:S(2)}) %all-to-all-start.3) | async-done | bytes 262176 | tf_op jit(solution)/shard_map/all_to_all | solution.py:523
  127.8 0.0 copy-done.1
  127.8 0.9 copy-done.5
  128.7 1.3 shard_map.123
  (17 shorter events, 0.1 us)
Async XLA Ops:
  1.6 1.2 copy-start
  2.9 0.7 copy-start.6
  3.6 47.0 %copy-start.8 = (bf16[1024,512]{1,0:T(8,128)(2,1)S(1)}, bf16[1024,512]{1,0:T(8,128)(2,1)}, u32[]{:S(2)}) copy-start(bf16[1024,512]{1,0:T(8,128)(2,1)} %constant.46.clone.low_ref) | copy-start | bytes 3145732
  3.6 47.0 %copy-start.10 = (bf16[1024,512]{1,0:T(8,128)(2,1)S(1)}, bf16[1024,512]{1,0:T(8,128)(2,1)}, u32[]{:S(2)}) copy-start(bf16[1024,512]{1,0:T(8,128)(2,1)} %constant.45.clone.high_ref) | copy-start | bytes 3145732
  5.0 0.6 copy-start.4
  5.6 44.9 %all-to-all-start = ((bf16[64,24,128]{2,1,0:T(8,128)(2,1)}), bf16[64,24,128]{2,1,0:T(8,128)(2,1)S(1)}, u32[]{:S(2)}, u32[]{:S(2)}) async-start(bf16[64,24,128]{2,1,0:T(8,128)(2,1)} %get-tuple-element.10), calls=%async_computation | async-start | bytes 786432 | tf_op jit(solution)/shard_map/all_to_all | solution.py:514
  63.6 11.8 %all-to-all-start.1 = ((bf16[8,128,128]{2,1,0:T(8,128)(2,1)}), bf16[8,128,128]{2,1,0:T(8,128)(2,1)S(1)}, u32[]{:S(2)}, u32[]{:S(2)}) async-start(bf16[8,128,128]{2,1,0:T(8,128)(2,1)} %get-tuple-element.12), calls=%async_computation.1 | async-start | bytes 524288 | tf_op jit(solution)/shard_map/all_to_all | solution.py:519
  69.0 6.4 %copy-start.12 = (bf16[2,256,256]{2,1,0:T(8,128)(2,1)S(1)}, bf16[2,256,256]{2,1,0:T(8,128)(2,1)}, u32[]{:S(2)}) copy-start(bf16[2,256,256]{2,1,0:T(8,128)(2,1)} %constant.49.clone.inverse_ref) | copy-start | bytes 786436
  69.1 6.4 %copy-start.13 = (bf16[2,256,256]{2,1,0:T(8,128)(2,1)S(1)}, bf16[2,256,256]{2,1,0:T(8,128)(2,1)}, u32[]{:S(2)}) copy-start(bf16[2,256,256]{2,1,0:T(8,128)(2,1)} %constant.48.clone.forward_ref) | copy-start | bytes 786436
  69.1 6.4 %copy-start.14 = (f32[16,128]{1,0:T(8,128)S(1)}, f32[16,128]{1,0:T(8,128)}, u32[]{:S(2)}) copy-start(f32[16,128]{1,0:T(8,128)} %constant.47.clone.turn_ref) | copy-start | bytes 24580
  87.1 1.2 copy-start.9
  88.3 1.2 copy-start.11
  89.6 17.7 %copy-start.15 = (s32[64,1]{0,1:T(1,128)S(1)}, s32[64,1]{0,1:T(1,128)}, u32[]{:S(2)}) copy-start(s32[64,1]{0,1:T(1,128)} %param.15) | copy-start | bytes 772
  89.6 17.8 %copy-start.7 = (bf16[64,128]{1,0:T(8,128)(2,1)S(1)}, bf16[64,128]{1,0:T(8,128)(2,1)}, u32[]{:S(2)}) copy-start(bf16[64,128]{1,0:T(8,128)(2,1)} %coef_ref.1) | copy-start | bytes 49156
  89.6 30.6 %copy-start.2 = (bf16[64,1,128,128]{3,2,1,0:T(8,128)(2,1)S(1)}, bf16[64,1,128,128]{3,2,1,0:T(8,128)(2,1)}, u32[]{:S(2)}) copy-start(bf16[64,1,128,128]{3,2,1,0:T(8,128)(2,1)} %param.14) | copy-start | bytes 6291460
  99.7 0.7 copy-start.3
  100.4 27.4 %copy-start.1 = (bf16[64,64,128]{2,1,0:T(8,128)(2,1)S(1)}, bf16[64,64,128]{2,1,0:T(8,128)(2,1)}, u32[]{:S(2)}) copy-start(bf16[64,64,128]{2,1,0:T(8,128)(2,1)} %param.13) | copy-start | bytes 3145732
  100.4 27.4 %all-to-all-start.3 = ((bf16[64,16,128]{2,1,0:T(8,128)(2,1)}), bf16[64,16,128]{2,1,0:T(8,128)(2,1)S(1)}, u32[]{:S(2)}, u32[]{:S(2)}) async-start(bf16[64,16,128]{2,1,0:T(8,128)(2,1)} %copy-done.3), calls=%async_computation.3 | async-start | bytes 524288 | tf_op jit(solution)/shard_map/all_to_all | solution.py:523
  127.8 0.9 copy-start.5

commit v2 on v1

v2 whole, which is shorter than its diff:
```python
import math

import jax
import jax.numpy as jnp
import numpy as np
from jax import lax
from jax.experimental import pallas as pl
from jax.experimental.pallas import tpu as pltpu
from jax.sharding import PartitionSpec as P

SLABS = 64
PENCILS = 8
BOX = 64
FUNCS = 128
STENCIL = 64
CX = 8
CY = 128
NX = 512
NY = 1024
NZ = 128
GROUP = BOX * PENCILS
ROWS = 24
LINES = NX // PENCILS
MORE = LINES + 8
BOXES = SLABS * BOX
TILE = 256
WINDOW = 48
SHIFT = SLABS - WINDOW
SPAN = CX * WINDOW

F32 = jnp.float32
BF16 = jnp.bfloat16
NT = (((1,), (1,)), ((), ()))
NN = (((1,), (0,)), ((), ()))


def halves(table):
    table = np.asarray(table, np.float32)
    high = table.astype(BF16)
    low = (table - high.astype(np.float32)).astype(BF16)
    return high, low


def x_table():
    half, offset, slab = np.meshgrid(
        np.arange(2), np.arange(CX), np.arange(WINDOW), indexing="ij"
    )
    cells = (CX * (slab + SHIFT * half) + offset).reshape(-1)
    phase = np.outer(np.arange(NX), cells) % NX * (2.0 * math.pi / NX)
    return np.concatenate([np.cos(phase), np.sin(phase)], 0)


def y_tables():
    phase = np.outer(np.arange(CY), np.arange(CY)) % CY * (2.0 * math.pi / CY)
    c, s = np.cos(phase), np.sin(phase)
    forward = np.block([[c, -s], [s, c]])
    inverse = np.block([[c, s], [-s, c]])
    turn = np.outer(np.arange(PENCILS), np.arange(CY)) * (2.0 * math.pi / NY)
    turn = np.concatenate([np.cos(turn), np.sin(turn)], 0).astype(np.float32)
    return forward, inverse, turn


def cosine_coefficients():
    fit = np.polynomial.chebyshev.Chebyshev.interpolate(
        lambda w: np.cos(2.0 * math.pi * np.sqrt(w)), 9, domain=[0.0, 0.25]
    )
    return [float(v) for v in fit.convert(kind=np.polynomial.Polynomial).coef]


COSINE = cosine_coefficients()


def cosine_of(step):
    u = (step.astype(F32) - (NZ // 2)) * (1.0 / NZ)
    w = u * u
    total = jnp.full_like(w, COSINE[-1])
    for value in COSINE[-2::-1]:
        total = total * w + value
    return -total


def iota(shape, axis):
    return lax.broadcasted_iota(jnp.int32, shape, axis)


def dot(a, b, dims=NN):
    return lax.dot_general(a, b, dims, preferred_element_type=F32)


def split(value):
    high = value.astype(BF16)
    return high, (value - high.astype(F32)).astype(BF16)


def swap(first, other, width):
    even = iota(first.shape, 1) & width == 0
    return (
        jnp.where(even, first, pltpu.roll(other, width, 1)),
        jnp.where(even, pltpu.roll(first, 128 - width, 1), other),
    )


def regroup(tiles):
    a, c = swap(tiles[0], tiles[2], 64)
    b, d = swap(tiles[1], tiles[3], 64)
    return swap(a, b, 32) + swap(c, d, 32)


def ungroup(tiles):
    a, b = swap(tiles[0], tiles[1], 32)
    c, d = swap(tiles[2], tiles[3], 32)
    first, third = swap(a, c, 64)
    second, fourth = swap(b, d, 64)
    return first, second, third, fourth


def project_kernel(
    anchor_hbm, slab_hbm, coef_hbm, proj_hbm,
    send_ref, phase_ref, turn_ref, back_ref,
    value_ref, anchor_ref, slab_ref, coef_ref, proj_ref, sems,
):
    count = 4
    size = BOX * STENCIL // count
    small = [
        pltpu.make_async_copy(source, target, sems.at[n])
        for n, (source, target) in enumerate(
            ((slab_hbm, slab_ref), (anchor_hbm, anchor_ref), (coef_hbm, coef_ref))
        )
    ]
    for copy in small:
        copy.start()
    large = [
        pltpu.make_async_copy(
            proj_hbm.at[n * size : (n + 1) * size, :],
            proj_ref.at[n * size : (n + 1) * size, :],
            sems.at[3 + n],
        )
        for n in range(count)
    ]
    for copy in large:
        copy.start()
    for copy in small:
        copy.wait()

    slab = slab_ref[...].astype(F32)
    box = iota((1, BOX), 1).astype(F32)
    key = slab * BOX + box
    key = jnp.concatenate([key, key], 1)
    column = jnp.broadcast_to(key, (128, 128)).T[0:BOX]
    rank = jnp.sum(jnp.where(column < key, 1.0, 0.0), axis=0, keepdims=True)
    column = jnp.broadcast_to(rank, (128, 128)).T[0:BOX]
    lane = (iota((BOX, 128), 1) & (BOX - 1)).astype(F32)
    chosen = column == lane
    order = jnp.sum(
        jnp.where(chosen, iota((BOX, 128), 0).astype(F32), 0.0), axis=0, keepdims=True
    )
    row = iota((128, 128), 0)
    hot = jnp.where((row & (BOX - 1)).astype(F32) == rank, 1.0, 0.0)
    back_ref[...] = jnp.where(row < BOX, hot, 0.0).astype(BF16)
    twice = dot(hot.astype(BF16)[:, 0:BOX], coef_ref[...]).astype(BF16)
    table = jnp.concatenate(
        [anchor_ref[...].astype(F32), slab, jnp.zeros((4, BOX), F32)], 0
    ).astype(BF16)
    table = dot(table, jnp.where(chosen, 1.0, 0.0).astype(BF16))
    later = (iota((1, 128), 1) & (BOX // 2) > 0).astype(F32)
    code = table[0:1] * WINDOW + table[3:4] - later * SHIFT
    y_place = table[1:2]
    depth = table[2:3].astype(jnp.int32)
    turn_ref[...] = jnp.broadcast_to(y_place, (8, 128))

    second = (iota((SLABS, 128), 1) >= BOX).astype(jnp.int32)
    wave = iota((SLABS, 128), 0)
    for k in range(4):
        z = depth + k
        step = jnp.where(wave == 0, second * (NZ // 2) * z, wave * z + second * (NZ // 4))
        phase_ref[k] = cosine_of(step & (NZ - 1))

    total = jnp.zeros((STENCIL, 128), F32)
    per = TILE // STENCIL
    for block in range(BOX // per):
        if block * count % (BOX // per) == 0:
            large[block * count // (BOX // per)].wait()
        part = dot(proj_ref[block * TILE : (block + 1) * TILE, :], twice, NT)
        for t in range(per):
            mine = order == float(block * per + t)
            total = jnp.where(mine, part[t * STENCIL : (t + 1) * STENCIL], total)
    value_ref[...] = total

    turn = y_place.astype(jnp.int32) & 3
    row = iota((16, 128), 0) & 3
    parts = []
    for k in range(4):
        value = value_ref[pl.ds(k, 16, stride=4), :]
        out = value
        for m in range(1, 4):
            moved = jnp.where(row >= m, pltpu.roll(value, m, 0), pltpu.roll(value, m + 12, 0))
            out = jnp.where(turn == m, moved, out)
        parts.append(out)
    places = jnp.where(iota((8, 128), 1) < BOX, code, y_place)
    for wave in range(SLABS):
        total = phase_ref[0, wave : wave + 1, :] * parts[0]
        for k in range(1, 4):
            total = total + phase_ref[k, wave : wave + 1, :] * parts[k]
        send_ref[wave] = jnp.concatenate([total, places], 0).astype(BF16)


def spread_kernel(place_ref, recv_ref, table_ref, send_ref, pos_ref, row_ref, hot_ref):
    cells = iota((TILE, 128), 0).astype(F32)
    y_cells = iota((CY, 128), 0).astype(F32)
    upper = iota((8, 128), 0) < 4

    groups = []
    for step in range(SLABS // 4):
        tiles = regroup([recv_ref[step * 4 + n].astype(F32) for n in range(4)])
        groups.append(((tiles[0], tiles[2]), (tiles[1], tiles[3])))
        places = [tile[16:17] for pair in groups[-1] for tile in pair]
        pos_ref[step] = jnp.concatenate(places + [jnp.zeros((4, 128), F32)], 0)

    def fill(step, half):
        real, imag = groups[step][half]
        code, y_place = real[16:17], imag[16:17]
        start = half * (BOXES // 2) + step * 128
        away = y_cells - y_place
        inside = jnp.where((away >= 0.0) & (away < 4.0), 1.0, 0.0).astype(BF16)
        inside = inside.reshape(8, 16, 128)
        for i in range(4):
            for c, source in enumerate((real, imag)):
                block = source[8 * (i // 2) : 8 * (i // 2) + 8]
                moved = pltpu.roll(block, 4, 0)
                pair = (block, moved) if i % 2 == 0 else (moved, block)
                both = jnp.where(upper, pair[0], pair[1])
                both = jnp.concatenate([both, both], 0).astype(BF16)
                rows = (inside * both[None]).reshape(CY, 128)
                row_ref[(2 * i + c) * CY : (2 * i + c + 1) * CY, start : start + 128] = rows
        hot_ref[:, start : start + 128] = jnp.where(cells == code, 1.0, 0.0).astype(BF16)

    planes = []
    for half in range(2):
        for step in range(SLABS // 4):
            fill(step, half)
        lanes = slice(half * (BOXES // 2), (half + 1) * (BOXES // 2))
        plane = None
        for i in range(4):
            part = dot(row_ref[2 * CY * i : 2 * CY * (i + 1), lanes], hot_ref[:, lanes], NT)
            part = jnp.concatenate([part, jnp.zeros((2 * CY, SPAN - TILE), F32)], 1)
            plane = part if i == 0 else plane + pltpu.roll(part, WINDOW * i, 1)
        planes.append(plane)
    wave = dot(table_ref[...], jnp.concatenate(planes, 1).astype(BF16), NT)
    ac, bc = wave[:NX, :CY], wave[:NX, CY:]
    as_, bs = wave[NX:, :CY], wave[NX:, CY:]

    def put(real, imag):
        real = real.astype(BF16)
        imag = imag.astype(BF16)
        for r in range(PENCILS):
            send_ref[r, 0:LINES, :] = real[r * LINES : (r + 1) * LINES]
            send_ref[r, LINES : 2 * LINES, :] = imag[r * LINES : (r + 1) * LINES]

    @pl.when(place_ref[0] > 0)
    def _():
        put(ac + bs, bc - as_)

    @pl.when(place_ref[0] == 0)
    def _():
        line = iota((NX, CY), 0)
        real = jnp.where(line <= NX // 2, ac, bc)
        imag = jnp.where(line < NX // 2, -as_, -bs)
        put(real, jnp.where((line == 0) | (line == NX // 2), bc, imag))


def quarter(a, b, c, d, sign):
    def add(p, q):
        return (p[0] + q[0], p[1] + q[1])

    def sub(p, q):
        return (p[0] - q[0], p[1] - q[1])

    first, second, third, fourth = add(a, c), sub(a, c), add(b, d), sub(b, d)
    fourth = (-fourth[1], fourth[0]) if sign > 0 else (fourth[1], -fourth[0])
    return [add(first, third), add(second, fourth), sub(first, third), sub(second, fourth)]


def eighth(parts, sign):
    even = quarter(parts[0], parts[2], parts[4], parts[6], sign)
    odd = quarter(parts[1], parts[3], parts[5], parts[7], sign)
    root = math.sqrt(0.5)
    a, b = odd[1]
    odd[1] = ((a - sign * b) * root, (b + sign * a) * root)
    a, b = odd[2]
    odd[2] = (-sign * b, sign * a)
    a, b = odd[3]
    odd[3] = ((-a - sign * b) * root, (sign * a - b) * root)
    return [(e[0] + o[0], e[1] + o[1]) for e, o in zip(even, odd)] + [
        (e[0] - o[0], e[1] - o[1]) for e, o in zip(even, odd)
    ]


def times(value, table):
    high, low = split(value)
    return dot(high, table[0]) + dot(low, table[0]) + dot(high, table[1])


def line_kernel(place_ref, recv_ref, spec_ref, turn_ref, forward_ref, inverse_ref, send_ref):
    special = place_ref[1]
    top = (iota((8, CY), 0) == 0) & (special > 0)
    parts = []
    for q in range(PENCILS):
        real = recv_ref[q, 0:LINES, :].astype(F32)
        imag = recv_ref[q, LINES : 2 * LINES, :].astype(F32)
        first = imag[0:8]
        real = jnp.concatenate([real, jnp.where(top, first, 0.0)], 0)
        imag = jnp.concatenate(
            [jnp.where(top, 0.0, first), imag[8:], jnp.zeros((8, CY), F32)], 0
        )
        parts.append((real, imag))
    parts = eighth(parts, -1)
    lines = []
    for k in range(PENCILS):
        real, imag = parts[k]
        if k > 0:
            c = turn_ref[k : k + 1, :]
            s = turn_ref[PENCILS + k : PENCILS + k + 1, :]
            real, imag = real * c + imag * s, imag * c - real * s
        lines.append(jnp.concatenate([real, imag], 1))
    wave = times(jnp.concatenate(lines, 0), (forward_ref[0], forward_ref[1]))
    spec = spec_ref[...]
    wave = wave * jnp.concatenate([spec, spec], 1)
    wave = times(wave, (inverse_ref[0], inverse_ref[1]))
    parts = []
    for k in range(PENCILS):
        real = wave[k * MORE : (k + 1) * MORE, :CY]
        imag = wave[k * MORE : (k + 1) * MORE, CY:]
        if k > 0:
            c = turn_ref[k : k + 1, :]
            s = turn_ref[PENCILS + k : PENCILS + k + 1, :]
            real, imag = real * c - imag * s, imag * c + real * s
        parts.append((real, imag))
    parts = eighth(parts, 1)
    for q in range(PENCILS):
        real, imag = parts[q]
        send_ref[q] = jnp.concatenate(
            [
                real[0:8] - imag[LINES:],
                real[8:LINES],
                imag[0:8] + real[LINES:],
                imag[8:LINES],
            ],
            0,
        ).astype(BF16)


def sample_kernel(place_ref, pos_ref, recv_ref, table_ref, send_ref, left_ref, wave_ref):
    real = jnp.concatenate([recv_ref[r, 0:LINES, :] for r in range(PENCILS)], 0)
    imag = jnp.concatenate([recv_ref[r, LINES : 2 * LINES, :] for r in range(PENCILS)], 0)
    real = real.astype(F32).T
    imag = imag.astype(F32).T

    def put(first, second, third, fourth):
        wave_ref[0:CY, 0:NX] = first.astype(BF16)
        wave_ref[0:CY, NX:] = second.astype(BF16)
        wave_ref[CY:, 0:NX] = third.astype(BF16)
        wave_ref[CY:, NX:] = fourth.astype(BF16)

    @pl.when(place_ref[0] > 0)
    def _():
        put(real, -imag, imag, real)

    @pl.when(place_ref[0] == 0)
    def _():
        line = iota((CY, NX), 1)
        ends = (line == 0) | (line == NX // 2)
        low = line < NX // 2
        put(
            jnp.where(ends, real, jnp.where(low, 2.0 * real, 0.0)),
            jnp.where(ends, 0.0, jnp.where(low, -2.0 * imag, 0.0)),
            jnp.where(ends, imag, jnp.where(low, 0.0, 2.0 * real)),
            jnp.where(ends, 0.0, jnp.where(low, 0.0, -2.0 * imag)),
        )

    plane = dot(wave_ref[...], table_ref[...])
    for half in range(2):
        part = plane[:, half * SPAN : (half + 1) * SPAN]
        for i in range(4):
            moved = part if i == 0 else pltpu.roll(part, SPAN - WINDOW * i, 1)
            left_ref[half, 2 * CY * i : 2 * CY * (i + 1), :] = moved[:, :TILE].astype(BF16)

    cells = iota((TILE, 128), 0).astype(F32)
    y_cells = (iota((16, 8, 128), 0) * 8 + iota((16, 8, 128), 1)).astype(F32)
    upper = iota((8, 128), 0) < 4

    def gather(step):
        quads = [step * 2, step * 2 + 1]
        found = {}
        for half in range(2):
            hot, inside = [], []
            for quad in quads:
                place = pos_ref[quad]
                code, y_place = place[2 * half : 2 * half + 1], place[2 * half + 1 : 2 * half + 2]
                hot.append(jnp.where(cells == code, 1.0, 0.0).astype(BF16))
                away = y_cells - y_place[None]
                inside.append((away >= 0.0) & (away < 4.0))
            hot = jnp.concatenate(hot, 1)
            for i in range(4):
                part = dot(left_ref[half, 2 * CY * i : 2 * CY * (i + 1), :], hot)
                for near in range(2):
                    for c in range(2):
                        block = part[c * CY : (c + 1) * CY, near * 128 : (near + 1) * 128]
                        block = jnp.where(inside[near], block.reshape(16, 8, 128), 0.0)
                        block = jnp.sum(block, axis=0)
                        found[near, c, half, i] = block + pltpu.roll(block, 4, 0)
        for near in range(2):
            tiles = []
            for c in range(2):
                for half in range(2):
                    f = [found[near, c, half, i] for i in range(4)]
                    tiles.append(
                        jnp.concatenate(
                            [jnp.where(upper, f[0], f[1]), jnp.where(upper, f[2], f[3])], 0
                        )
                    )
            for n, tile in enumerate(ungroup(tiles)):
                send_ref[quads[near] * 4 + n] = tile.astype(BF16)

    for step in range(SLABS // 8):
        gather(step)


def finish_kernel(
    turn_ref, back_ref, phase_ref, recv_ref, close_ref, proj_ref, out_ref, value_ref, wide_ref
):
    totals = [jnp.zeros((16, 128), F32) for _ in range(4)]
    for wave in range(SLABS):
        value = recv_ref[wave].astype(F32)
        for k in range(4):
            totals[k] = totals[k] + phase_ref[k, wave : wave + 1, :] * value
    turn = turn_ref[0:1, :].astype(jnp.int32) & 3
    row = iota((16, 128), 0) & 3
    for k in range(4):
        value = totals[k] + pltpu.roll(totals[k], BOX, 1)
        out = value
        for m in range(1, 4):
            moved = jnp.where(
                row + m < 4, pltpu.roll(value, 16 - m, 0), pltpu.roll(value, 4 - m, 0)
            )
            out = jnp.where(turn == m, moved, out)
        value_ref[pl.ds(k, 16, stride=4), :] = out
    value = dot(value_ref[...].astype(BF16), back_ref[...])
    value = jnp.concatenate([value, value], 0).T[0:BOX]
    box = iota((BOX, 128), 0)
    half = (iota((BOX, 128), 1) >= STENCIL).astype(jnp.int32)
    for m in range(BOX // 2):
        wide_ref[:, 128 * m : 128 * (m + 1)] = jnp.where(
            box == 2 * m + half, value, 0.0
        ).astype(BF16)
    out_ref[...] = dot(wide_ref[...], proj_ref[...]) + close_ref[...]


def near_kernel(ids_ref, group_ref, near_ref, out_ref):
    hot = jnp.where(iota((BOX, GROUP), 1) == ids_ref[...], 1.0, 0.0).astype(BF16)
    partner = dot(hot, group_ref[...]).astype(BF16)
    twice = jnp.concatenate([partner, partner], 0)
    lane = iota((FUNCS, 128), 1) & (BOX - 1)

    def step(index, total):
        start = pl.multiple_of(index * 512, 512)
        part = dot(near_ref[pl.ds(start, 512), :], twice, NT)
        for t in range(4):
            total = jnp.where(lane == index * 4 + t, part[t * FUNCS : (t + 1) * FUNCS], total)
        return total

    total = lax.fori_loop(0, BOX // 4, step, jnp.zeros((FUNCS, 128), F32))
    out_ref[...] = total.T[0:BOX]


VMEM = pl.BlockSpec(memory_space=pltpu.VMEM)
SMEM = pl.BlockSpec(memory_space=pltpu.SMEM)
HBM = pl.BlockSpec(memory_space=pltpu.HBM)


def call(kernel, shapes, specs, scratch=(), limit=32, flops=0, moved=0):
    return pl.pallas_call(
        kernel,
        out_shape=shapes,
        in_specs=specs,
        out_specs=jax.tree.map(lambda _: VMEM, shapes),
        scratch_shapes=list(scratch),
        compiler_params=pltpu.CompilerParams(vmem_limit_bytes=limit * 1024 * 1024),
        cost_estimate=pl.CostEstimate(flops=flops, bytes_accessed=moved, transcendentals=0),
    )


def resident(*arrays):
    return [pltpu.with_memory_space_constraint(a, pltpu.HBM) for a in arrays]


def struct(*shape, kind=F32):
    return jax.ShapeDtypeStruct(shape, kind)


def project(anchors, slabs, coefficients, flat):
    return call(
        project_kernel,
        (
            struct(SLABS, ROWS, 128, kind=BF16),
            struct(4, SLABS, 128),
            struct(8, 128),
            struct(128, 128, kind=BF16),
        ),
        [HBM] * 4,
        [
            pltpu.VMEM((STENCIL, 128), F32),
            pltpu.VMEM(anchors.shape, jnp.int32),
            pltpu.VMEM(slabs.shape, jnp.int32),
            pltpu.VMEM(coefficients.shape, BF16),
            pltpu.VMEM(flat.shape, BF16),
            pltpu.SemaphoreType.DMA((7,)),
        ],
        limit=8,
        flops=2 * BOXES * FUNCS * 128,
        moved=2 << 20,
    )(*resident(anchors, slabs, coefficients, flat))


def spread(place, received, table):
    return call(
        spread_kernel,
        (struct(PENCILS, 2 * LINES, CY, kind=BF16), struct(SLABS // 4, 8, 128)),
        [SMEM] + [VMEM] * 2,
        [pltpu.VMEM((8 * CY, BOXES), BF16), pltpu.VMEM((TILE, BOXES), BF16)],
        limit=28,
        flops=2 * BOXES * TILE * 8 * CY,
        moved=4 << 20,
    )(place, received, table)


def lines(place, received, spec, turn, forward, inverse):
    return call(
        line_kernel,
        struct(PENCILS, 2 * LINES, CY, kind=BF16),
        [SMEM] + [VMEM] * 5,
        limit=12,
        flops=2 * 6 * PENCILS * MORE * 256 * 256,
        moved=2 << 20,
    )(place, received, spec, turn, forward, inverse)


def sample(place, pos, received, table):
    return call(
        sample_kernel,
        struct(SLABS, 16, 128, kind=BF16),
        [SMEM] + [VMEM] * 3,
        [pltpu.VMEM((2, 8 * CY, TILE), BF16), pltpu.VMEM((2 * CY, 2 * NX), BF16)],
        limit=16,
        flops=2 * BOXES * TILE * 8 * CY,
        moved=4 << 20,
    )(place, pos, received, table)


def finish(turn, back, phase, received, close, flat):
    return call(
        finish_kernel,
        struct(BOX, FUNCS),
        [VMEM] * 6,
        [pltpu.VMEM((STENCIL, 128), F32), pltpu.VMEM((BOX, BOX * STENCIL), BF16)],
        limit=8,
        flops=2 * BOX * BOXES * FUNCS,
        moved=2 << 20,
    )(turn, back, phase, received, close, flat)


def near(ids, group, blocks):
    return call(
        near_kernel,
        struct(BOX, FUNCS),
        [VMEM] * 3,
        limit=8,
        flops=2 * BOX * FUNCS * FUNCS * 128,
        moved=3 << 20,
    )(ids, group, blocks)


def arrange(spectrum, slab, pencil):
    first, second = spectrum[:, 0, :], spectrum[:, 1, :]
    chosen = jnp.where((slab == 0) & (pencil >= PENCILS // 2), second, first)
    head = jnp.where((slab == 0) & (pencil == PENCILS // 2), first[0:1], chosen[0:1])
    rows = jnp.concatenate([head, chosen[1:], jnp.broadcast_to(second[0:1], (8, NY))], 0)
    rows = rows * jnp.where(slab == 0, 1.0, 2.0) * (1.0 / (NX * NY * NZ))
    return rows.reshape(MORE, CY, PENCILS).transpose(2, 0, 1).reshape(PENCILS * MORE, CY)


def per_device(coefficients, projection, near_blocks, near_ids, grid_slab, anchors, spectrum):
    slab = lax.axis_index("slab")
    pencil = lax.axis_index("pencil")
    special = (slab == 0) & (pencil % (PENCILS // 2) == 0)
    place = jnp.stack([slab, special.astype(jnp.int32)]).astype(jnp.int32)
    flat = projection.reshape(BOX * STENCIL, FUNCS)
    table = jnp.asarray(x_table().astype(BF16))
    forward, inverse, turn = y_tables()
    forward, inverse = np.stack(halves(forward)), np.stack(halves(inverse))

    send, phase, turned, back = project(anchors, grid_slab.reshape(1, BOX), coefficients, flat)
    received = lax.all_to_all(send, "slab", split_axis=0, concat_axis=0, tiled=True)
    spec = arrange(spectrum, slab, pencil)
    group = lax.all_gather(coefficients, "pencil", axis=0, tiled=True)
    close = near(near_ids & (GROUP - 1), group, near_blocks.reshape(BOX * FUNCS, FUNCS))
    received, spec, place = lax.optimization_barrier((received, spec, place))
    send, pos = spread(place, received, table)
    received = lax.all_to_all(send, "pencil", split_axis=0, concat_axis=0, tiled=True)
    send = lines(place, received, spec, turn, forward, inverse)
    received = lax.all_to_all(send, "pencil", split_axis=0, concat_axis=0, tiled=True)
    send = sample(place, pos, received, table)
    received = lax.all_to_all(send, "slab", split_axis=0, concat_axis=0, tiled=True)
    return finish(turned, back, phase, received, close, flat)


def solution(mesh):
    placed = (
        P(("slab", "pencil"), None),
        P(("slab", "pencil"), None, None),
        P(("slab", "pencil"), None, None, None),
        P(("slab", "pencil"), None),
        P(("slab", "pencil"), None),
        P(None, ("slab", "pencil")),
        P("pencil", "slab", None),
    )
    return jax.shard_map(
        per_device,
        mesh=mesh,
        in_specs=placed,
        out_specs=P(("slab", "pencil"), None),
        check_vma=False,
    )
```

time: 131 us -> 112 us (0.85)
  Pallas kernels: 30.9 us -> 18.7 us
  blocking collectives: 22.7 us -> 34.5 us
  waiting for transfers between devices: 32.2 us -> 25.1 us
  starting transfers between devices: 29.9 us -> 25.6 us
  local copies, waits for them, and re-layouts: 9.67 us -> 6.23 us
  other arithmetic: 4.49 us -> 1.52 us
    all_to_all x1 -> x2, blocking collectives: 9.95 us -> 21.7 us  [per_device(): lax.all_to_all(send, 'pencil', split_axis=0, concat_axis=0, tiled=True)]
    pallas_call x1, Pallas kernels: 13 us -> 5.21 us  [spread(): call(spread_kernel, (struct(PENCILS, 2 * LINES, CY, kind=BF16), struct(SL...]
    pallas_call x1, Pallas kernels: 10.2 us -> 3.89 us  [sample(): call(sample_kernel, struct(SLABS, 16, 128, kind=BF16), [SMEM] + [VMEM] *...]
    unnamed x33 -> x27, local copies, waits for them, and re-layouts: 6.78 us -> 2.4 us
    all_to_all x1 -> x0, starting transfers between devices: 4.3 us -> none  [per_device(): lax.all_to_all(send, 'pencil', split_axis=0, concat_axis=0, tiled=True)]
    all_to_all x2, waiting for transfers between devices: 28.8 us -> 25.1 us  [per_device(): lax.all_to_all(send, 'slab', split_axis=0, concat_axis=0, tiled=True)]
    all_to_all x1 -> x0, waiting for transfers between devices: 3.44 us -> none  [per_device(): lax.all_to_all(send, 'pencil', split_axis=0, concat_axis=0, tiled=True)]
    pallas_call x1, Pallas kernels: 1.41 us -> 3.18 us  [project(): call(project_kernel, (struct(SLABS, ROWS, 128, kind=BF16), struct(4, SLAB...]
  transfers between devices with their start and end apart: 3 -> 2, of which waited for: 3 -> 2; matrix products, arithmetic and copies ran while one was open for 4% -> 5% of each run, Pallas kernels for 3% -> 3%
where the time goes in v2:
time: 112 us
  blocking collectives  34.5 us (31%)
  starting transfers between devices  25.6 us (23%)
  waiting for transfers between devices  25.1 us (22%)
  Pallas kernels  18.7 us (17%)
  local copies, waits for them, and re-layouts  6.23 us (6%)
  other arithmetic  1.52 us (1%)
    all_to_all x2, starting transfers between devices, per_device(): lax.all_to_all(send, 'slab', split_axis=0, concat_axis=0, tiled=True)  25.6 us
    all_to_all x2, waiting for transfers between devices, per_device(): lax.all_to_all(send, 'slab', split_axis=0, concat_axis=0, tiled=True)  25.1 us
    all_to_all x2, blocking collectives, per_device(): lax.all_to_all(send, 'pencil', split_axis=0, concat_axis=0, tiled=True)  21.7 us
    all_gather x1, blocking collectives, per_device(): group = lax.all_gather(coefficients, 'pencil', axis=0, tiled=True)  12.8 us
    pallas_call x1, Pallas kernels, spread(): call(spread_kernel, (struct(PENCILS, 2 * LINES, CY, kind=BF16), struct(SL...  5.21 us
    pallas_call x1, Pallas kernels, sample(): call(sample_kernel, struct(SLABS, 16, 128, kind=BF16), [SMEM] + [VMEM] *...  3.89 us
    pallas_call x1, Pallas kernels, near(): call(near_kernel, struct(BOX, FUNCS), [VMEM] * 3, limit=8, flops=2 * BOX...  3.33 us
    pallas_call x1, Pallas kernels, project(): call(project_kernel, (struct(SLABS, ROWS, 128, kind=BF16), struct(4, SLAB...  3.18 us
  transfers between devices with their start and end apart: 2, of which 2 were waited for; matrix products, arithmetic and copies ran while one was open for 5% of the time, Pallas kernels for 3%

profile of v2, /device:TPU:8, one launch (start us, length us, event | category | flops | bytes accessed | tf_op | source)
XLA Modules:
  0.0 111.7 jit_solution(7095354905648602285)
XLA Ops:
  0.0 0.0 copy-start.10
  0.0 3.2 %shard_map.109 = (bf16[64,24,128]{2,1,0:T(8,128)(2,1)}, f32[4,64,128]{2,1,0:T(8,128)S(1)}, f32[8,128]{1,0:T(8,128)S(1)}, bf16[128,128]{1,0:T(8,128)(2,1)S(1)}) custom-call(s32[3,64]{1,0:T(4,128)} %anchor_hbm.1, s32[1,64]{1,0:T(1,128)} %bitcast.14, bf16[64,128]{1,0:T(8,128)(2,1)} %coef_hbm.1, bf16[4096,128]{1,0:T(8,128)(2,1)} %bitcast.9), custom_call_target="tpu_custom_call" | custom-call | flops 134217728 | bytes 2097152 | tf_op jit(solution)/shard_map/pallas_call | solution.py:501
  3.2 0.0 copy-start.3
  3.2 0.6 copy-done.3
  3.8 18.7 %all-to-all-start = ((bf16[64,24,128]{2,1,0:T(8,128)(2,1)}), bf16[64,24,128]{2,1,0:T(8,128)(2,1)S(1)}, u32[]{:S(2)}, u32[]{:S(2)}) async-start(bf16[64,24,128]{2,1,0:T(8,128)(2,1)} %get-tuple-element.17), calls=%async_computation | async-start | bytes 786432 | tf_op jit(solution)/shard_map/all_to_all | solution.py:602
  22.6 0.0 copy-done.10
  22.6 0.3 broadcast_select_fusion
  22.9 0.7 slice.31
  23.7 0.1 broadcast_in_dim.7
  23.8 0.3 concatenate.11
  24.1 0.0 copy-start.5
  24.1 1.3 %copy.20 = f32[63,1,1024]{0,2,1:T(8,128)S(1)} copy(f32[63,1,1024]{2,1,0:T(1,128)} %slice.31) | data formatting | bytes 516096 | tf_op jit(solution)/shard_map/slice | solution.py:586
  25.4 0.2 broadcast_in_dim.8
  25.6 1.1 %fusion.1 = f32[8,72,128]{1,0,2:T(8,128)} fusion(f32[8,128,8]{0,2,1:T(8,128)S(1)} %broadcast_in_dim.8, f32[63,128,8]{0,2,1:T(8,128)S(1)} %bitcast.13, f32[1,128,8]{0,2,1:T(8,128)S(1)} %concatenate.11, f32[]{:T(128)S(6)} %select_n.33), kind=kLoop, calls=%fused_computation.2 | loop fusion | flops 294912 | bytes 589828 | tf_op jit(solution)/shard_map/transpose | solution.py:588
  26.7 1.2 %copy.22 = f32[8,72,128]{2,1,0:T(8,128)S(1)} copy(f32[8,72,128]{1,0,2:T(8,128)} %fusion.1) | data formatting | bytes 589824 | tf_op jit(solution)/shard_map/transpose | solution.py:588
  28.0 0.1 pad_add_fusion.place_ref
  28.0 20.8 %all-to-all-done.recv_ref = bf16[64,24,128]{2,1,0:T(8,128)(2,1)S(1)} async-done(((bf16[64,24,128]{2,1,0:T(8,128)(2,1)}), bf16[64,24,128]{2,1,0:T(8,128)(2,1)S(1)}, u32[]{:S(2)}, u32[]{:S(2)}) %all-to-all-start) | async-done | bytes 393248 | tf_op jit(solution)/shard_map/all_to_all | solution.py:602
  48.8 0.0 copy-done.5
  48.8 0.0 copy-start.7
  48.8 0.0 copy-start.8
  48.8 0.0 copy-start.9
  48.8 5.2 %shard_map.110 = (bf16[8,128,128]{2,1,0:T(8,128)(2,1)S(1)}, f32[16,8,128]{2,1,0:T(8,128)S(1)}) custom-call(s32[2]{0:T(128)S(1)} %pad_add_fusion.place_ref, bf16[64,24,128]{2,1,0:T(8,128)(2,1)S(1)} %all-to-all-done.recv_ref, bf16[1024,768]{1,0:T(8,128)(2,1)S(1)} %copy-done.5), custom_call_target="tpu_custom_call" | custom-call | flops 2147483648 | bytes 4194304 | tf_op jit(solution)/shard_map/pallas_call | solution.py:525
  54.0 0.0 copy-start.6
  54.0 11.8 %all_to_all.20.recv_ref = bf16[8,128,128]{2,1,0:T(8,128)(2,1)S(1)} all-to-all(bf16[8,128,128]{2,1,0:T(8,128)(2,1)S(1)} %get-tuple-element.21), channel_id=1, replica_groups=mesh['slab'=64,'pencil'=8] {'pencil'}, dimensions={0} | all-to-all | bytes 524288 | tf_op jit(solution)/shard_map/all_to_all | solution.py:608
  65.8 0.0 copy-done.7
  65.8 0.0 copy-done.8
  65.8 0.0 copy-done.9
  65.8 1.7 %shard_map.111 = bf16[8,128,128]{2,1,0:T(8,128)(2,1)S(1)} custom-call(s32[2]{0:T(128)S(1)} %pad_add_fusion.place_ref, bf16[8,128,128]{2,1,0:T(8,128)(2,1)S(1)} %all_to_all.20.recv_ref, f32[576,128]{1,0:T(8,128)S(1)} %bitcast.12, f32[16,128]{1,0:T(8,128)S(1)} %copy-done.9, bf16[2,256,256]{2,1,0:T(8,128)(2,1)S(1)} %copy-done.7, bf16[2,256,256]{2,1,0:T(8,128)(2,1)S(1)} %copy-done.8), custom_call_target="tpu_custom_call" | custom-call | flops 452984832 | bytes 2097152 | tf_op jit(solution)/shard_map/pallas_call | solution.py:537
  67.5 9.9 %all_to_all.21.recv_ref = bf16[8,128,128]{2,1,0:T(8,128)(2,1)S(1)} all-to-all(bf16[8,128,128]{2,1,0:T(8,128)(2,1)S(1)} %shard_map.111), channel_id=1, replica_groups=mesh['slab'=64,'pencil'=8] {'pencil'}, dimensions={0} | all-to-all | bytes 524288 | tf_op jit(solution)/shard_map/all_to_all | solution.py:610
  77.5 0.0 copy-done.6
  77.5 0.0 copy-start.12
  77.5 0.0 copy-start.11
  77.5 0.0 copy-start.1
  77.5 3.9 %shard_map.112 = bf16[64,16,128]{2,1,0:T(8,128)(2,1)S(1)} custom-call(s32[2]{0:T(128)S(1)} %pad_add_fusion.place_ref, f32[16,8,128]{2,1,0:T(8,128)S(1)} %get-tuple-element.20.pos_ref, bf16[8,128,128]{2,1,0:T(8,128)(2,1)S(1)} %all_to_all.21.recv_ref, bf16[1024,768]{1,0:T(8,128)(2,1)S(1)} %copy-done.6), custom_call_target="tpu_custom_call" | custom-call | flops 2147483648 | bytes 4194304 | tf_op jit(solution)/shard_map/pallas_call | solution.py:548
  81.4 0.0 copy-start.2
  81.4 0.7 copy-done.2
  82.1 0.0 copy-start
  82.1 6.8 %all-to-all-start.3 = ((bf16[64,16,128]{2,1,0:T(8,128)(2,1)}), bf16[64,16,128]{2,1,0:T(8,128)(2,1)S(1)}, u32[]{:S(2)}, u32[]{:S(2)}) async-start(bf16[64,16,128]{2,1,0:T(8,128)(2,1)} %copy-done.2), calls=%async_computation.3 | async-start | bytes 524288 | tf_op jit(solution)/shard_map/all_to_all | solution.py:612
  88.9 0.0 copy-done.12
  88.9 0.1 copy.23
  89.0 0.0 copy-done.11
  89.0 12.8 %all_gather.3.group_ref = bf16[512,128]{1,0:T(8,128)(2,1)S(1)} all-gather(bf16[64,128]{1,0:T(8,128)(2,1)S(1)} %copy-done.11), channel_id=1, replica_groups=mesh['slab'=64,'pencil'=8] {'pencil'}, dimensions={0}, use_global_device_ids=true | all-gather | bytes 147456 | tf_op jit(solution)/shard_map/all_gather | solution.py:604
  101.8 0.0 copy-done.1
  101.8 3.3 %shard_map.113.close_ref = f32[64,128]{1,0:T(8,128)S(1)} custom-call(s32[64,1]{1,0:T(8,128)S(1)} %broadcast_and_fusion.ids_ref, bf16[512,128]{1,0:T(8,128)(2,1)S(1)} %all_gather.3.group_ref, bf16[8192,128]{1,0:T(8,128)(2,1)S(1)} %bitcast.11), custom_call_target="tpu_custom_call" | custom-call | flops 268435456 | bytes 3145728 | tf_op jit(solution)/shard_map/pallas_call | solution.py:572
  105.1 4.3 %all-to-all-done.3.recv_ref = bf16[64,16,128]{2,1,0:T(8,128)(2,1)S(1)} async-done(((bf16[64,16,128]{2,1,0:T(8,128)(2,1)}), bf16[64,16,128]{2,1,0:T(8,128)(2,1)S(1)}, u32[]{:S(2)}, u32[]{:S(2)}) %all-to-all-start.3) | async-done | bytes 262176 | tf_op jit(solution)/shard_map/all_to_all | solution.py:612
  109.5 0.0 copy-done
  109.5 0.9 copy-done.4
  110.4 1.4 %shard_map.114 = f32[64,128]{1,0:T(8,128)} custom-call(f32[8,128]{1,0:T(8,128)S(1)} %get-tuple-element.14.turn_ref, bf16[128,128]{1,0:T(8,128)(2,1)S(1)} %get-tuple-element.15.back_ref, f32[4,64,128]{2,1,0:T(8,128)S(1)} %copy-done.4, bf16[64,16,128]{2,1,0:T(8,128)(2,1)S(1)} %all-to-all-done.3.recv_ref, f32[64,128]{1,0:T(8,128)S(1)} %shard_map.113.close_ref, ...), custom_call_target="tpu_custom_call" | custom-call | flops 67108864 | bytes 2097152 | tf_op jit(solution)/shard_map/pallas_call | solution.py:560
  (3 shorter events, 0.0 us)
Async XLA Ops:
  0.0 22.6 %copy-start.10 = (f32[64,2,1024]{2,1,0:T(2,128)S(1)}, f32[64,2,1024]{2,1,0:T(2,128)}, u32[]{:S(2)}) copy-start(f32[64,2,1024]{2,1,0:T(2,128)} %param.17) | copy-start | bytes 1572868
  3.2 0.7 copy-start.3
  3.8 44.9 %all-to-all-start = ((bf16[64,24,128]{2,1,0:T(8,128)(2,1)}), bf16[64,24,128]{2,1,0:T(8,128)(2,1)S(1)}, u32[]{:S(2)}, u32[]{:S(2)}) async-start(bf16[64,24,128]{2,1,0:T(8,128)(2,1)} %get-tuple-element.17), calls=%async_computation | async-start | bytes 786432 | tf_op jit(solution)/shard_map/all_to_all | solution.py:602
  24.1 24.7 %copy-start.5 = (bf16[1024,768]{1,0:T(8,128)(2,1)S(1)}, bf16[1024,768]{1,0:T(8,128)(2,1)}, u32[]{:S(2)}) copy-start(bf16[1024,768]{1,0:T(8,128)(2,1)} %constant.39.clone.table_ref) | copy-start | bytes 4718596
  48.8 17.0 %copy-start.7 = (bf16[2,256,256]{2,1,0:T(8,128)(2,1)S(1)}, bf16[2,256,256]{2,1,0:T(8,128)(2,1)}, u32[]{:S(2)}) copy-start(bf16[2,256,256]{2,1,0:T(8,128)(2,1)} %constant.41.clone.forward_ref) | copy-start | bytes 786436
  48.8 17.0 %copy-start.8 = (bf16[2,256,256]{2,1,0:T(8,128)(2,1)S(1)}, bf16[2,256,256]{2,1,0:T(8,128)(2,1)}, u32[]{:S(2)}) copy-start(bf16[2,256,256]{2,1,0:T(8,128)(2,1)} %constant.42.clone.inverse_ref) | copy-start | bytes 786436
  48.8 17.0 %copy-start.9 = (f32[16,128]{1,0:T(8,128)S(1)}, f32[16,128]{1,0:T(8,128)}, u32[]{:S(2)}) copy-start(f32[16,128]{1,0:T(8,128)} %constant.40.clone.turn_ref) | copy-start | bytes 24580
  54.0 23.4 %copy-start.6 = (bf16[1024,768]{1,0:T(8,128)(2,1)S(1)}, bf16[1024,768]{1,0:T(8,128)(2,1)}, u32[]{:S(2)}) copy-start(bf16[1024,768]{1,0:T(8,128)(2,1)} %constant.39.clone.table_ref) | copy-start | bytes 4718596
  77.5 11.5 %copy-start.12 = (s32[64,1]{0,1:T(1,128)S(1)}, s32[64,1]{0,1:T(1,128)}, u32[]{:S(2)}) copy-start(s32[64,1]{0,1:T(1,128)} %param.14) | copy-start | bytes 772
  77.5 11.6 %copy-start.11 = (bf16[64,128]{1,0:T(8,128)(2,1)S(1)}, bf16[64,128]{1,0:T(8,128)(2,1)}, u32[]{:S(2)}) copy-start(bf16[64,128]{1,0:T(8,128)(2,1)} %coef_hbm.1) | copy-start | bytes 49156
  77.5 24.3 %copy-start.1 = (bf16[64,1,128,128]{3,2,1,0:T(8,128)(2,1)S(1)}, bf16[64,1,128,128]{3,2,1,0:T(8,128)(2,1)}, u32[]{:S(2)}) copy-start(bf16[64,1,128,128]{3,2,1,0:T(8,128)(2,1)} %param.13) | copy-start | bytes 6291460
  81.4 0.7 copy-start.2
  82.1 27.4 %copy-start = (bf16[64,64,128]{2,1,0:T(8,128)(2,1)S(1)}, bf16[64,64,128]{2,1,0:T(8,128)(2,1)}, u32[]{:S(2)}) copy-start(bf16[64,64,128]{2,1,0:T(8,128)(2,1)} %param.12) | copy-start | bytes 3145732
  82.1 27.4 %all-to-all-start.3 = ((bf16[64,16,128]{2,1,0:T(8,128)(2,1)}), bf16[64,16,128]{2,1,0:T(8,128)(2,1)S(1)}, u32[]{:S(2)}, u32[]{:S(2)}) async-start(bf16[64,16,128]{2,1,0:T(8,128)(2,1)} %copy-done.2), calls=%async_computation.3 | async-start | bytes 524288 | tf_op jit(solution)/shard_map/all_to_all | solution.py:612
  109.5 0.9 copy-start.4

commit v3 on v2

--- a/solution.py
+++ b/solution.py
@@ -19,10 +19,12 @@
 NY = 1024
 NZ = 128
 GROUP = BOX * PENCILS
-ROWS = 24
+ROWS = 18
 LINES = NX // PENCILS
 MORE = LINES + 8
 BOXES = SLABS * BOX
+SMALL = 8 + 128
+SIDE = BOX + 128
 TILE = 256
 WINDOW = 48
 SHIFT = SLABS - WINDOW
@@ -114,10 +116,19 @@
     return first, second, third, fourth
 
 
+def phases(depth, phase_ref):
+    second = (iota((SLABS, 128), 1) >= BOX).astype(jnp.int32)
+    wave = iota((SLABS, 128), 0)
+    for k in range(4):
+        z = depth + k
+        step = jnp.where(wave == 0, second * (NZ // 2) * z, wave * z + second * (NZ // 4))
+        phase_ref[k * SLABS : (k + 1) * SLABS] = cosine_of(step & (NZ - 1))
+
+
 def project_kernel(
     anchor_hbm, slab_hbm, coef_hbm, proj_hbm,
-    send_ref, phase_ref, turn_ref, back_ref,
-    value_ref, anchor_ref, slab_ref, coef_ref, proj_ref, sems,
+    send_hbm, small_hbm,
+    send_ref, small_ref, phase_ref, value_ref, anchor_ref, slab_ref, coef_ref, proj_ref, sems,
 ):
     count = 4
     size = BOX * STENCIL // count
@@ -156,7 +167,6 @@
     )
     row = iota((128, 128), 0)
     hot = jnp.where((row & (BOX - 1)).astype(F32) == rank, 1.0, 0.0)
-    back_ref[...] = jnp.where(row < BOX, hot, 0.0).astype(BF16)
     twice = dot(hot.astype(BF16)[:, 0:BOX], coef_ref[...]).astype(BF16)
     table = jnp.concatenate(
         [anchor_ref[...].astype(F32), slab, jnp.zeros((4, BOX), F32)], 0
@@ -166,14 +176,11 @@
     code = table[0:1] * WINDOW + table[3:4] - later * SHIFT
     y_place = table[1:2]
     depth = table[2:3].astype(jnp.int32)
-    turn_ref[...] = jnp.broadcast_to(y_place, (8, 128))
-
-    second = (iota((SLABS, 128), 1) >= BOX).astype(jnp.int32)
-    wave = iota((SLABS, 128), 0)
-    for k in range(4):
-        z = depth + k
-        step = jnp.where(wave == 0, second * (NZ // 2) * z, wave * z + second * (NZ // 4))
-        phase_ref[k] = cosine_of(step & (NZ - 1))
+    small_ref[0:8] = jnp.concatenate([y_place, table[2:3], jnp.zeros((6, 128), F32)], 0)
+    small_ref[8:] = jnp.where(row < BOX, hot, 0.0)
+    notes = pltpu.make_async_copy(small_ref, small_hbm, sems.at[11])
+    notes.start()
+    phases(depth, phase_ref)
 
     total = jnp.zeros((STENCIL, 128), F32)
     per = TILE // STENCIL
@@ -196,12 +203,29 @@
             moved = jnp.where(row >= m, pltpu.roll(value, m, 0), pltpu.roll(value, m + 12, 0))
             out = jnp.where(turn == m, moved, out)
         parts.append(out)
-    places = jnp.where(iota((8, 128), 1) < BOX, code, y_place)
+    places = jnp.where(iota((8, 128), 1) < BOX, code, y_place)[0 : ROWS - 16]
+    size = SLABS // count
+    copies = []
     for wave in range(SLABS):
-        total = phase_ref[0, wave : wave + 1, :] * parts[0]
+        total = phase_ref[wave : wave + 1, :] * parts[0]
         for k in range(1, 4):
-            total = total + phase_ref[k, wave : wave + 1, :] * parts[k]
-        send_ref[wave] = jnp.concatenate([total, places], 0).astype(BF16)
+            row = k * SLABS + wave
+            total = total + phase_ref[row : row + 1, :] * parts[k]
+        total = jnp.concatenate([total, places], 0).reshape(ROWS // 2, 2, 128)
+        send_ref[wave] = total.astype(BF16)
+        if wave % size == size - 1:
+            n = wave // size
+            copies.append(
+                pltpu.make_async_copy(
+                    send_ref.at[n * size : (n + 1) * size],
+                    send_hbm.at[n * size : (n + 1) * size],
+                    sems.at[7 + n],
+                )
+            )
+            copies[-1].start()
+    for copy in copies:
+        copy.wait()
+    notes.wait()
 
 
 def spread_kernel(place_ref, recv_ref, table_ref, send_ref, pos_ref, row_ref, hot_ref):
@@ -211,7 +235,11 @@
 
     groups = []
     for step in range(SLABS // 4):
-        tiles = regroup([recv_ref[step * 4 + n].astype(F32) for n in range(4)])
+        tiles = []
+        for n in range(4):
+            tile = recv_ref[step * 4 + n].astype(F32).reshape(ROWS, 128)
+            tiles.append(jnp.concatenate([tile, jnp.zeros((24 - ROWS, 128), F32)], 0))
+        tiles = regroup(tiles)
         groups.append(((tiles[0], tiles[2]), (tiles[1], tiles[3])))
         places = [tile[16:17] for pair in groups[-1] for tile in pair]
         pos_ref[step] = jnp.concatenate(places + [jnp.zeros((4, 128), F32)], 0)
@@ -349,7 +377,7 @@
         ).astype(BF16)
 
 
-def sample_kernel(place_ref, pos_ref, recv_ref, table_ref, send_ref, left_ref, wave_ref):
+def sample_kernel(place_ref, pos_ref, recv_ref, table_ref, send_hbm, left_ref, wave_ref, send_ref, sems):
     real = jnp.concatenate([recv_ref[r, 0:LINES, :] for r in range(PENCILS)], 0)
     imag = jnp.concatenate([recv_ref[r, LINES : 2 * LINES, :] for r in range(PENCILS)], 0)
     real = real.astype(F32).T
@@ -421,19 +449,27 @@
             for n, tile in enumerate(ungroup(tiles)):
                 send_ref[quads[near] * 4 + n] = tile.astype(BF16)
 
+    copies = []
     for step in range(SLABS // 8):
         gather(step)
+        rows = slice(step * 8, (step + 1) * 8)
+        copies.append(pltpu.make_async_copy(send_ref.at[rows], send_hbm.at[rows], sems.at[step]))
+        copies[-1].start()
+    for copy in copies:
+        copy.wait()
 
 
 def finish_kernel(
-    turn_ref, back_ref, phase_ref, recv_ref, close_ref, proj_ref, out_ref, value_ref, wide_ref
+    phase_ref, side_hbm, recv_ref, proj_ref, out_ref, value_ref, wide_ref, side_ref, sem
 ):
+    copy = pltpu.make_async_copy(side_hbm, side_ref, sem)
+    copy.start()
     totals = [jnp.zeros((16, 128), F32) for _ in range(4)]
     for wave in range(SLABS):
         value = recv_ref[wave].astype(F32)
         for k in range(4):
-            totals[k] = totals[k] + phase_ref[k, wave : wave + 1, :] * value
-    turn = turn_ref[0:1, :].astype(jnp.int32) & 3
+            totals[k] = totals[k] + phase_ref[k * SLABS + wave : k * SLABS + wave + 1, :] * value
+    turn = phase_ref[4 * SLABS : 4 * SLABS + 1, :].astype(jnp.int32) & 3
     row = iota((16, 128), 0) & 3
     for k in range(4):
         value = totals[k] + pltpu.roll(totals[k], BOX, 1)
@@ -444,7 +480,8 @@
             )
             out = jnp.where(turn == m, moved, out)
         value_ref[pl.ds(k, 16, stride=4), :] = out
-    value = dot(value_ref[...].astype(BF16), back_ref[...])
+    copy.wait()
+    value = dot(value_ref[...].astype(BF16), side_ref[BOX:].astype(BF16))
     value = jnp.concatenate([value, value], 0).T[0:BOX]
     box = iota((BOX, 128), 0)
     half = (iota((BOX, 128), 1) >= STENCIL).astype(jnp.int32)
@@ -452,10 +489,13 @@
         wide_ref[:, 128 * m : 128 * (m + 1)] = jnp.where(
             box == 2 * m + half, value, 0.0
         ).astype(BF16)
-    out_ref[...] = dot(wide_ref[...], proj_ref[...]) + close_ref[...]
-
-
-def near_kernel(ids_ref, group_ref, near_ref, out_ref):
+    out_ref[...] = dot(wide_ref[...], proj_ref[...]) + side_ref[0:BOX]
+
+
+def near_kernel(ids_ref, small_ref, group_ref, near_ref, phase_ref, side_hbm, side_ref, sem):
+    phases(small_ref[1:2, :].astype(jnp.int32), phase_ref)
+    phase_ref[4 * SLABS :] = small_ref[0:8]
+    side_ref[BOX:] = small_ref[8:]
     hot = jnp.where(iota((BOX, GROUP), 1) == ids_ref[...], 1.0, 0.0).astype(BF16)
     partner = dot(hot, group_ref[...]).astype(BF16)
     twice = jnp.concatenate([partner, partner], 0)
@@ -469,7 +509,10 @@
         return total
 
     total = lax.fori_loop(0, BOX // 4, step, jnp.zeros((FUNCS, 128), F32))
-    out_ref[...] = total.T[0:BOX]
+    side_ref[0:BOX] = total.T[0:BOX]
+    copy = pltpu.make_async_copy(side_ref, side_hbm, sem)
+    copy.start()
+    copy.wait()
 
 
 VMEM = pl.BlockSpec(memory_space=pltpu.VMEM)
@@ -477,20 +520,20 @@
 HBM = pl.BlockSpec(memory_space=pltpu.HBM)
 
 
-def call(kernel, shapes, specs, scratch=(), limit=32, flops=0, moved=0):
+def call(kernel, shapes, specs, scratch=(), outs=None, limit=32, flops=0, moved=0):
     return pl.pallas_call(
         kernel,
         out_shape=shapes,
         in_specs=specs,
-        out_specs=jax.tree.map(lambda _: VMEM, shapes),
+        out_specs=outs or jax.tree.map(lambda _: VMEM, shapes),
         scratch_shapes=list(scratch),
         compiler_params=pltpu.CompilerParams(vmem_limit_bytes=limit * 1024 * 1024),
         cost_estimate=pl.CostEstimate(flops=flops, bytes_accessed=moved, transcendentals=0),
     )
 
 
-def resident(*arrays):
-    return [pltpu.with_memory_space_constraint(a, pltpu.HBM) for a in arrays]
+def resident(*arrays, space=pltpu.HBM):
+    return [pltpu.with_memory_space_constraint(a, space) for a in arrays]
 
 
 def struct(*shape, kind=F32):
@@ -501,20 +544,22 @@
     return call(
         project_kernel,
         (
-            struct(SLABS, ROWS, 128, kind=BF16),
-            struct(4, SLABS, 128),
-            struct(8, 128),
-            struct(128, 128, kind=BF16),
+            pltpu.HBM((SLABS, ROWS // 2, 2, 128), BF16),
+            pltpu.HBM((SMALL, 128), F32),
         ),
         [HBM] * 4,
         [
+            pltpu.VMEM((SLABS, ROWS // 2, 2, 128), BF16),
+            pltpu.VMEM((SMALL, 128), F32),
+            pltpu.VMEM((4 * SLABS, 128), F32),
             pltpu.VMEM((STENCIL, 128), F32),
             pltpu.VMEM(anchors.shape, jnp.int32),
             pltpu.VMEM(slabs.shape, jnp.int32),
             pltpu.VMEM(coefficients.shape, BF16),
             pltpu.VMEM(flat.shape, BF16),
-            pltpu.SemaphoreType.DMA((7,)),
+            pltpu.SemaphoreType.DMA((12,)),
         ],
+        outs=(HBM, HBM),
         limit=8,
         flops=2 * BOXES * FUNCS * 128,
         moved=2 << 20,
@@ -547,36 +592,49 @@
 def sample(place, pos, received, table):
     return call(
         sample_kernel,
-        struct(SLABS, 16, 128, kind=BF16),
+        pltpu.HBM((SLABS, 16, 128), BF16),
         [SMEM] + [VMEM] * 3,
-        [pltpu.VMEM((2, 8 * CY, TILE), BF16), pltpu.VMEM((2 * CY, 2 * NX), BF16)],
+        [
+            pltpu.VMEM((2, 8 * CY, TILE), BF16),
+            pltpu.VMEM((2 * CY, 2 * NX), BF16),
+            pltpu.VMEM((SLABS, 16, 128), BF16),
+            pltpu.SemaphoreType.DMA((SLABS // 8,)),
+        ],
+        outs=HBM,
         limit=16,
         flops=2 * BOXES * TILE * 8 * CY,
         moved=4 << 20,
     )(place, pos, received, table)
 
 
-def finish(turn, back, phase, received, close, flat):
+def finish(phase, side, received, flat):
     return call(
         finish_kernel,
         struct(BOX, FUNCS),
-        [VMEM] * 6,
-        [pltpu.VMEM((STENCIL, 128), F32), pltpu.VMEM((BOX, BOX * STENCIL), BF16)],
+        [VMEM, HBM, VMEM, VMEM],
+        [
+            pltpu.VMEM((STENCIL, 128), F32),
+            pltpu.VMEM((BOX, BOX * STENCIL), BF16),
+            pltpu.VMEM((SIDE, 128), F32),
+            pltpu.SemaphoreType.DMA,
+        ],
         limit=8,
         flops=2 * BOX * BOXES * FUNCS,
         moved=2 << 20,
-    )(turn, back, phase, received, close, flat)
-
-
-def near(ids, group, blocks):
+    )(*resident(phase, space=pltpu.VMEM), *resident(side), received, flat)
+
+
+def near(ids, small, group, blocks):
     return call(
         near_kernel,
-        struct(BOX, FUNCS),
-        [VMEM] * 3,
+        (pltpu.VMEM((4 * SLABS + 8, 128), F32), pltpu.HBM((SIDE, 128), F32)),
+        [VMEM] * 4,
+        [pltpu.VMEM((SIDE, 128), F32), pltpu.SemaphoreType.DMA],
+        outs=(VMEM, HBM),
         limit=8,
         flops=2 * BOX * FUNCS * FUNCS * 128,
         moved=3 << 20,
-    )(ids, group, blocks)
+    )(ids, small, group, blocks)
 
 
 def arrange(spectrum, slab, pencil):
@@ -598,19 +656,21 @@
     forward, inverse, turn = y_tables()
     forward, inverse = np.stack(halves(forward)), np.stack(halves(inverse))
 
-    send, phase, turned, back = project(anchors, grid_slab.reshape(1, BOX), coefficients, flat)
+    send, small = project(anchors, grid_slab.reshape(1, BOX), coefficients, flat)
     received = lax.all_to_all(send, "slab", split_axis=0, concat_axis=0, tiled=True)
     spec = arrange(spectrum, slab, pencil)
-    group = lax.all_gather(coefficients, "pencil", axis=0, tiled=True)
-    close = near(near_ids & (GROUP - 1), group, near_blocks.reshape(BOX * FUNCS, FUNCS))
     received, spec, place = lax.optimization_barrier((received, spec, place))
     send, pos = spread(place, received, table)
     received = lax.all_to_all(send, "pencil", split_axis=0, concat_axis=0, tiled=True)
     send = lines(place, received, spec, turn, forward, inverse)
     received = lax.all_to_all(send, "pencil", split_axis=0, concat_axis=0, tiled=True)
     send = sample(place, pos, received, table)
+    send, own = lax.optimization_barrier((send, coefficients))
     received = lax.all_to_all(send, "slab", split_axis=0, concat_axis=0, tiled=True)
-    return finish(turned, back, phase, received, close, flat)
+    group = lax.all_gather(own, "pencil", axis=0, tiled=True)
+    blocks = near_blocks.reshape(BOX * FUNCS, FUNCS)
+    phase, side = near(near_ids & (GROUP - 1), small, group, blocks)
+    return finish(phase, side, received, flat)
 
 
 def solution(mesh):

time: 112 us -> 108 us (0.964)
  waiting for transfers between devices: 25.1 us -> 20.9 us
  local copies, waits for them, and re-layouts: 6.23 us -> 2.09 us
  Pallas kernels: 18.7 us -> 21.2 us
  other arithmetic: 1.52 us -> 2.86 us
    all_to_all x2, waiting for transfers between devices: 25.1 us -> 20.9 us  [per_device(): lax.all_to_all(send, 'slab', split_axis=0, concat_axis=0, tiled=True)]
    pallas_call x4, Pallas kernels: 11.8 us -> 14.2 us  [the longest x1 4.76 us: sample(): call(sample_kernel, pltpu.HBM((SLABS, 16, 128), BF16), [SMEM] + [VMEM] *...]
    slice x2, local copies, waits for them, and re-layouts: 2 us -> 0.25 us  [arrange(): chosen[1:]]
    unnamed x27 -> x21, local copies, waits for them, and re-layouts: 2.4 us -> 1.02 us
    select_n x1, other arithmetic: 0.27 us -> 1.62 us  [arrange(): chosen = jnp.where((slab == 0) & (pencil >= PENCILS // 2), second, first)]
  transfers between devices with their start and end apart: 2 -> 2, of which waited for: 2 -> 2; matrix products, arithmetic and copies ran while one was open for 5% -> 4% of each run, Pallas kernels for 3% -> 4%
where the time goes in v3:
time: 108 us; the launch traced here: 107 us
  blocking collectives  34.5 us (32%)
  starting transfers between devices  25.5 us (24%)
  Pallas kernels  21.2 us (20%)
  waiting for transfers between devices  20.9 us (19%)
  other arithmetic  2.86 us (3%)
  local copies, waits for them, and re-layouts  2.09 us (2%)
    all_to_all x2, starting transfers between devices, per_device(): lax.all_to_all(send, 'slab', split_axis=0, concat_axis=0, tiled=True)  25.5 us
    all_to_all x2, blocking collectives, per_device(): lax.all_to_all(send, 'pencil', split_axis=0, concat_axis=0, tiled=True)  21.7 us
    all_to_all x2, waiting for transfers between devices, per_device(): lax.all_to_all(send, 'slab', split_axis=0, concat_axis=0, tiled=True)  20.9 us
    all_gather x1, blocking collectives, per_device(): group = lax.all_gather(own, 'pencil', axis=0, tiled=True)  12.8 us
    pallas_call x1, Pallas kernels, spread(): call(spread_kernel, (struct(PENCILS, 2 * LINES, CY, kind=BF16), struct(SL...  5.31 us
    pallas_call x1, Pallas kernels, sample(): call(sample_kernel, pltpu.HBM((SLABS, 16, 128), BF16), [SMEM] + [VMEM] *...  4.76 us
    pallas_call x1, Pallas kernels, near(): call(near_kernel, (pltpu.VMEM((4 * SLABS + 8, 128), F32), pltpu.HBM((SIDE...  4.04 us
    pallas_call x1, Pallas kernels, project(): call(project_kernel, (pltpu.HBM((SLABS, ROWS // 2, 2, 128), BF16), pltpu....  3.22 us
  transfers between devices with their start and end apart: 2, of which 2 were waited for; matrix products, arithmetic and copies ran while one was open for 4% of the time, Pallas kernels for 4%

profile of v3, /device:TPU:8, one launch (start us, length us, event | category | flops | bytes accessed | tf_op | source)
XLA Modules:
  0.0 107.4 jit_solution(8633000564339532042)
XLA Ops:
  0.0 3.2 %shard_map.109 = (bf16[64,9,2,128]{3,2,1,0:T(2,128)(2,1)}, f32[136,128]{1,0:T(8,128)}) custom-call(s32[3,64]{1,0:T(4,128)} %anchor_hbm.1, s32[1,64]{1,0:T(1,128)} %bitcast.14, bf16[64,128]{1,0:T(8,128)(2,1)} %coef_hbm.1, bf16[4096,128]{1,0:T(8,128)(2,1)} %bitcast.9), custom_call_target="tpu_custom_call" | custom-call | flops 134217728 | bytes 2097152 | tf_op jit(solution)/shard_map/pallas_call | solution.py:544
  3.2 18.7 %all-to-all-start = ((bf16[64,9,2,128]{3,2,1,0:T(2,128)(2,1)}), bf16[64,9,2,128]{3,2,1,0:T(2,128)(2,1)S(1)}, u32[]{:S(2)}, u32[]{:S(2)}) async-start(bf16[64,9,2,128]{3,2,1,0:T(2,128)(2,1)} %get-tuple-element.17), calls=%async_computation | async-start | bytes 589824 | tf_op jit(solution)/shard_map/all_to_all | solution.py:660
  22.0 1.6 %broadcast_select_fusion = f32[64,1,1024]{2,1,0:T(1,128)S(1)} fusion(pred[]{:T(512)S(6)} %and.25, f32[64,2,1024]{2,1,0:T(2,128)} %param.17), kind=kLoop, calls=%fused_computation.3 | loop fusion | flops 65536 | bytes 786433 | tf_op jit(solution)/shard_map/jit(_where)/select_n | solution.py:642
  23.7 0.8 fusion.2
  24.5 0.1 broadcast_in_dim.7
  24.6 0.3 concatenate.11
  24.9 0.0 copy-start.3
  24.9 0.2 copy.22
  25.2 0.2 broadcast_in_dim.8
  25.4 0.3 fusion.1
  25.7 0.2 copy.24
  25.9 0.1 pad_add_fusion.place_ref
  26.0 18.2 %all-to-all-done.recv_ref = bf16[64,9,2,128]{3,2,1,0:T(2,128)(2,1)S(1)} async-done(((bf16[64,9,2,128]{3,2,1,0:T(2,128)(2,1)}), bf16[64,9,2,128]{3,2,1,0:T(2,128)(2,1)S(1)}, u32[]{:S(2)}, u32[]{:S(2)}) %all-to-all-start) | async-done | bytes 294944 | tf_op jit(solution)/shard_map/all_to_all | solution.py:660
  44.2 0.0 copy-done.3
  44.2 0.0 copy-start.5
  44.2 0.0 copy-start.6
  44.2 0.0 copy-start.7
  44.2 5.3 %shard_map.110 = (bf16[8,128,128]{2,1,0:T(8,128)(2,1)S(1)}, f32[16,8,128]{2,1,0:T(8,128)S(1)}) custom-call(s32[2]{0:T(128)S(1)} %pad_add_fusion.place_ref, bf16[64,9,2,128]{3,2,1,0:T(2,128)(2,1)S(1)} %all-to-all-done.recv_ref, bf16[1024,768]{1,0:T(8,128)(2,1)S(1)} %copy-done.3), custom_call_target="tpu_custom_call" | custom-call | flops 2147483648 | bytes 4194304 | tf_op jit(solution)/shard_map/pallas_call | solution.py:570
  49.6 0.0 copy-start.4
  49.6 11.8 %all_to_all.20.recv_ref = bf16[8,128,128]{2,1,0:T(8,128)(2,1)S(1)} all-to-all(bf16[8,128,128]{2,1,0:T(8,128)(2,1)S(1)} %get-tuple-element.21), channel_id=1, replica_groups=mesh['slab'=64,'pencil'=8] {'pencil'}, dimensions={0} | all-to-all | bytes 524288 | tf_op jit(solution)/shard_map/all_to_all | solution.py:664
  61.3 0.0 copy-done.5
  61.3 0.0 copy-done.6
  61.3 0.0 copy-done.7
  61.3 1.7 %shard_map.111 = bf16[8,128,128]{2,1,0:T(8,128)(2,1)S(1)} custom-call(s32[2]{0:T(128)S(1)} %pad_add_fusion.place_ref, bf16[8,128,128]{2,1,0:T(8,128)(2,1)S(1)} %all_to_all.20.recv_ref, f32[576,128]{1,0:T(8,128)S(1)} %bitcast.12, f32[16,128]{1,0:T(8,128)S(1)} %copy-done.7, bf16[2,256,256]{2,1,0:T(8,128)(2,1)S(1)} %copy-done.5, bf16[2,256,256]{2,1,0:T(8,128)(2,1)S(1)} %copy-done.6), custom_call_target="tpu_custom_call" | custom-call | flops 452984832 | bytes 2097152 | tf_op jit(solution)/shard_map/pallas_call | solution.py:582
  63.0 9.9 %all_to_all.21.recv_ref = bf16[8,128,128]{2,1,0:T(8,128)(2,1)S(1)} all-to-all(bf16[8,128,128]{2,1,0:T(8,128)(2,1)S(1)} %shard_map.111), channel_id=1, replica_groups=mesh['slab'=64,'pencil'=8] {'pencil'}, dimensions={0} | all-to-all | bytes 524288 | tf_op jit(solution)/shard_map/all_to_all | solution.py:666
  73.0 0.0 copy-done.4
  73.0 0.0 copy-start.9
  73.0 0.0 copy-start.8
  73.0 0.0 copy-start.1
  73.0 4.8 %shard_map.112 = bf16[64,16,128]{2,1,0:T(8,128)(2,1)} custom-call(s32[2]{0:T(128)S(1)} %pad_add_fusion.place_ref, f32[16,8,128]{2,1,0:T(8,128)S(1)} %get-tuple-element.20.pos_ref, bf16[8,128,128]{2,1,0:T(8,128)(2,1)S(1)} %all_to_all.21.recv_ref, bf16[1024,768]{1,0:T(8,128)(2,1)S(1)} %copy-done.4), custom_call_target="tpu_custom_call" | custom-call | flops 2147483648 | bytes 4194304 | tf_op jit(solution)/shard_map/pallas_call | solution.py:593
  77.8 0.0 copy-start
  77.8 6.7 %all-to-all-start.3 = ((bf16[64,16,128]{2,1,0:T(8,128)(2,1)}), bf16[64,16,128]{2,1,0:T(8,128)(2,1)S(1)}, u32[]{:S(2)}, u32[]{:S(2)}) async-start(bf16[64,16,128]{2,1,0:T(8,128)(2,1)} %shard_map.112), calls=%async_computation.3 | async-start | bytes 524288 | tf_op jit(solution)/shard_map/all_to_all | solution.py:669
  84.5 0.0 copy-done.9
  84.5 0.1 copy.20
  84.6 0.0 copy-done.8
  84.6 12.8 %all_gather.3.group_ref = bf16[512,128]{1,0:T(8,128)(2,1)S(1)} all-gather(bf16[64,128]{1,0:T(8,128)(2,1)S(1)} %copy-done.8), channel_id=1, replica_groups=mesh['slab'=64,'pencil'=8] {'pencil'}, dimensions={0}, use_global_device_ids=true | all-gather | bytes 147456 | tf_op jit(solution)/shard_map/all_gather | solution.py:670
  97.4 0.0 copy-done.1
  97.4 0.0 copy-start.2
  97.4 0.9 copy-done.2
  98.3 4.0 %shard_map.113 = (f32[264,128]{1,0:T(8,128)S(1)}, f32[192,128]{1,0:T(8,128)}) custom-call(s32[64,1]{1,0:T(8,128)S(1)} %broadcast_and_fusion.ids_ref, f32[136,128]{1,0:T(8,128)S(1)} %copy-done.2, bf16[512,128]{1,0:T(8,128)(2,1)S(1)} %all_gather.3.group_ref, bf16[8192,128]{1,0:T(8,128)(2,1)S(1)} %bitcast.11), custom_call_target="tpu_custom_call" | custom-call | flops 268435456 | bytes 3145728 | tf_op jit(solution)/shard_map/pallas_call | solution.py:628
  102.3 2.7 %all-to-all-done.3.recv_ref = bf16[64,16,128]{2,1,0:T(8,128)(2,1)S(1)} async-done(((bf16[64,16,128]{2,1,0:T(8,128)(2,1)}), bf16[64,16,128]{2,1,0:T(8,128)(2,1)S(1)}, u32[]{:S(2)}, u32[]{:S(2)}) %all-to-all-start.3) | async-done | bytes 262176 | tf_op jit(solution)/shard_map/all_to_all | solution.py:669
  105.0 0.0 copy-done
  105.0 2.2 %shard_map.114 = f32[64,128]{1,0:T(8,128)} custom-call(f32[264,128]{1,0:T(8,128)S(1)} %get-tuple-element.24.phase_ref, f32[192,128]{1,0:T(8,128)} %get-tuple-element.25.side_hbm, bf16[64,16,128]{2,1,0:T(8,128)(2,1)S(1)} %all-to-all-done.3.recv_ref, bf16[4096,128]{1,0:T(8,128)(2,1)S(1)} %bitcast.10), custom_call_target="tpu_custom_call" | custom-call | flops 67108864 | bytes 2097152 | tf_op jit(solution)/shard_map/pallas_call | solution.py:611
  (2 shorter events, 0.0 us)
Async XLA Ops:
  3.2 41.0 %all-to-all-start = ((bf16[64,9,2,128]{3,2,1,0:T(2,128)(2,1)}), bf16[64,9,2,128]{3,2,1,0:T(2,128)(2,1)S(1)}, u32[]{:S(2)}, u32[]{:S(2)}) async-start(bf16[64,9,2,128]{3,2,1,0:T(2,128)(2,1)} %get-tuple-element.17), calls=%async_computation | async-start | bytes 589824 | tf_op jit(solution)/shard_map/all_to_all | solution.py:660
  24.9 19.3 %copy-start.3 = (bf16[1024,768]{1,0:T(8,128)(2,1)S(1)}, bf16[1024,768]{1,0:T(8,128)(2,1)}, u32[]{:S(2)}) copy-start(bf16[1024,768]{1,0:T(8,128)(2,1)} %constant.39.clone.table_ref) | copy-start | bytes 4718596
  44.2 17.1 %copy-start.5 = (bf16[2,256,256]{2,1,0:T(8,128)(2,1)S(1)}, bf16[2,256,256]{2,1,0:T(8,128)(2,1)}, u32[]{:S(2)}) copy-start(bf16[2,256,256]{2,1,0:T(8,128)(2,1)} %constant.41.clone.forward_ref) | copy-start | bytes 786436
  44.2 17.1 %copy-start.6 = (bf16[2,256,256]{2,1,0:T(8,128)(2,1)S(1)}, bf16[2,256,256]{2,1,0:T(8,128)(2,1)}, u32[]{:S(2)}) copy-start(bf16[2,256,256]{2,1,0:T(8,128)(2,1)} %constant.42.clone.inverse_ref) | copy-start | bytes 786436
  44.2 17.1 %copy-start.7 = (f32[16,128]{1,0:T(8,128)S(1)}, f32[16,128]{1,0:T(8,128)}, u32[]{:S(2)}) copy-start(f32[16,128]{1,0:T(8,128)} %constant.40.clone.turn_ref) | copy-start | bytes 24580
  49.6 23.4 %copy-start.4 = (bf16[1024,768]{1,0:T(8,128)(2,1)S(1)}, bf16[1024,768]{1,0:T(8,128)(2,1)}, u32[]{:S(2)}) copy-start(bf16[1024,768]{1,0:T(8,128)(2,1)} %constant.39.clone.table_ref) | copy-start | bytes 4718596
  73.0 11.5 %copy-start.9 = (s32[64,1]{0,1:T(1,128)S(1)}, s32[64,1]{0,1:T(1,128)}, u32[]{:S(2)}) copy-start(s32[64,1]{0,1:T(1,128)} %param.14) | copy-start | bytes 772
  73.0 11.6 %copy-start.8 = (bf16[64,128]{1,0:T(8,128)(2,1)S(1)}, bf16[64,128]{1,0:T(8,128)(2,1)}, u32[]{:S(2)}) copy-start(bf16[64,128]{1,0:T(8,128)(2,1)} %coef_hbm.1) | copy-start | bytes 49156
  73.0 24.4 %copy-start.1 = (bf16[64,1,128,128]{3,2,1,0:T(8,128)(2,1)S(1)}, bf16[64,1,128,128]{3,2,1,0:T(8,128)(2,1)}, u32[]{:S(2)}) copy-start(bf16[64,1,128,128]{3,2,1,0:T(8,128)(2,1)} %param.13) | copy-start | bytes 6291460
  77.8 27.3 %copy-start = (bf16[64,64,128]{2,1,0:T(8,128)(2,1)S(1)}, bf16[64,64,128]{2,1,0:T(8,128)(2,1)}, u32[]{:S(2)}) copy-start(bf16[64,64,128]{2,1,0:T(8,128)(2,1)} %param.12) | copy-start | bytes 3145732
  77.8 27.2 %all-to-all-start.3 = ((bf16[64,16,128]{2,1,0:T(8,128)(2,1)}), bf16[64,16,128]{2,1,0:T(8,128)(2,1)S(1)}, u32[]{:S(2)}, u32[]{:S(2)}) async-start(bf16[64,16,128]{2,1,0:T(8,128)(2,1)} %shard_map.112), calls=%async_computation.3 | async-start | bytes 524288 | tf_op jit(solution)/shard_map/all_to_all | solution.py:669
  97.4 0.9 copy-start.2

commit v4 on v3

--- a/solution.py
+++ b/solution.py
@@ -130,8 +130,6 @@
     send_hbm, small_hbm,
     send_ref, small_ref, phase_ref, value_ref, anchor_ref, slab_ref, coef_ref, proj_ref, sems,
 ):
-    count = 4
-    size = BOX * STENCIL // count
     small = [
         pltpu.make_async_copy(source, target, sems.at[n])
         for n, (source, target) in enumerate(
@@ -140,16 +138,8 @@
     ]
     for copy in small:
         copy.start()
-    large = [
-        pltpu.make_async_copy(
-            proj_hbm.at[n * size : (n + 1) * size, :],
-            proj_ref.at[n * size : (n + 1) * size, :],
-            sems.at[3 + n],
-        )
-        for n in range(count)
-    ]
-    for copy in large:
-        copy.start()
+    large = pltpu.make_async_copy(proj_hbm, proj_ref, sems.at[3])
+    large.start()
     for copy in small:
         copy.wait()
 
@@ -178,19 +168,16 @@
     depth = table[2:3].astype(jnp.int32)
     small_ref[0:8] = jnp.concatenate([y_place, table[2:3], jnp.zeros((6, 128), F32)], 0)
     small_ref[8:] = jnp.where(row < BOX, hot, 0.0)
-    notes = pltpu.make_async_copy(small_ref, small_hbm, sems.at[11])
+    notes = pltpu.make_async_copy(small_ref, small_hbm, sems.at[8])
     notes.start()
     phases(depth, phase_ref)
 
+    large.wait()
+    every = dot(proj_ref[...], twice, NT)
     total = jnp.zeros((STENCIL, 128), F32)
-    per = TILE // STENCIL
-    for block in range(BOX // per):
-        if block * count % (BOX // per) == 0:
-            large[block * count // (BOX // per)].wait()
-        part = dot(proj_ref[block * TILE : (block + 1) * TILE, :], twice, NT)
-        for t in range(per):
-            mine = order == float(block * per + t)
-            total = jnp.where(mine, part[t * STENCIL : (t + 1) * STENCIL], total)
+    for n in range(BOX):
+        part = every[n * STENCIL : (n + 1) * STENCIL]
+        total = jnp.where(order == float(n), part, total)
     value_ref[...] = total
 
     turn = y_place.astype(jnp.int32) & 3
@@ -204,7 +191,7 @@
             out = jnp.where(turn == m, moved, out)
         parts.append(out)
     places = jnp.where(iota((8, 128), 1) < BOX, code, y_place)[0 : ROWS - 16]
-    size = SLABS // count
+    size = SLABS // 4
     copies = []
     for wave in range(SLABS):
         total = phase_ref[wave : wave + 1, :] * parts[0]
@@ -219,7 +206,7 @@
                 pltpu.make_async_copy(
                     send_ref.at[n * size : (n + 1) * size],
                     send_hbm.at[n * size : (n + 1) * size],
-                    sems.at[7 + n],
+                    sems.at[4 + n],
                 )
             )
             copies[-1].start()
@@ -262,15 +249,24 @@
                 row_ref[(2 * i + c) * CY : (2 * i + c + 1) * CY, start : start + 128] = rows
         hot_ref[:, start : start + 128] = jnp.where(cells == code, 1.0, 0.0).astype(BF16)
 
+    count = 4
+    steps = SLABS // 4 // count
+    size = BOXES // 2 // count
+    parts = [[None] * 4 for _ in range(2)]
+    for run in range(count):
+        for half in range(2):
+            for step in range(run * steps, (run + 1) * steps):
+                fill(step, half)
+            start = half * (BOXES // 2) + run * size
+            lanes = slice(start, start + size)
+            for i in range(4):
+                part = dot(row_ref[2 * CY * i : 2 * CY * (i + 1), lanes], hot_ref[:, lanes], NT)
+                parts[half][i] = part if run == 0 else parts[half][i] + part
     planes = []
     for half in range(2):
-        for step in range(SLABS // 4):
-            fill(step, half)
-        lanes = slice(half * (BOXES // 2), (half + 1) * (BOXES // 2))
         plane = None
         for i in range(4):
-            part = dot(row_ref[2 * CY * i : 2 * CY * (i + 1), lanes], hot_ref[:, lanes], NT)
-            part = jnp.concatenate([part, jnp.zeros((2 * CY, SPAN - TILE), F32)], 1)
+            part = jnp.concatenate([parts[half][i], jnp.zeros((2 * CY, SPAN - TILE), F32)], 1)
             plane = part if i == 0 else plane + pltpu.roll(part, WINDOW * i, 1)
         planes.append(plane)
     wave = dot(table_ref[...], jnp.concatenate(planes, 1).astype(BF16), NT)
@@ -557,7 +553,7 @@
             pltpu.VMEM(slabs.shape, jnp.int32),
             pltpu.VMEM(coefficients.shape, BF16),
             pltpu.VMEM(flat.shape, BF16),
-            pltpu.SemaphoreType.DMA((12,)),
+            pltpu.SemaphoreType.DMA((9,)),
         ],
         outs=(HBM, HBM),
         limit=8,

time: 108 us -> 107 us (level)
  no operation moved by 1% of the time
where the time goes in v4:
time: 107 us; the launch traced here: 106 us
  blocking collectives  34.5 us (32%)
  starting transfers between devices  25.5 us (24%)
  waiting for transfers between devices  20.9 us (20%)
  Pallas kernels  20.2 us (19%)
  other arithmetic  2.86 us (3%)
  local copies, waits for them, and re-layouts  2.09 us (2%)
    all_to_all x2, starting transfers between devices, per_device(): lax.all_to_all(send, 'slab', split_axis=0, concat_axis=0, tiled=True)  25.5 us
    all_to_all x2, blocking collectives, per_device(): lax.all_to_all(send, 'pencil', split_axis=0, concat_axis=0, tiled=True)  21.7 us
    all_to_all x2, waiting for transfers between devices, per_device(): lax.all_to_all(send, 'slab', split_axis=0, concat_axis=0, tiled=True)  20.9 us
    all_gather x1, blocking collectives, per_device(): group = lax.all_gather(own, 'pencil', axis=0, tiled=True)  12.8 us
    pallas_call x1, Pallas kernels, spread(): call(spread_kernel, (struct(PENCILS, 2 * LINES, CY, kind=BF16), struct(SL...  4.95 us
    pallas_call x1, Pallas kernels, sample(): call(sample_kernel, pltpu.HBM((SLABS, 16, 128), BF16), [SMEM] + [VMEM] *...  4.58 us
    pallas_call x1, Pallas kernels, near(): call(near_kernel, (pltpu.VMEM((4 * SLABS + 8, 128), F32), pltpu.HBM((SIDE...  4.04 us
    pallas_call x1, Pallas kernels, project(): call(project_kernel, (pltpu.HBM((SLABS, ROWS // 2, 2, 128), BF16), pltpu....  2.77 us
  transfers between devices with their start and end apart: 2, of which 2 were waited for; matrix products, arithmetic and copies ran while one was open for 4% of the time, Pallas kernels for 4%

profile of v4, /device:TPU:8, one launch (start us, length us, event | category | flops | bytes accessed | tf_op | source)
XLA Modules:
  0.0 106.2 jit_solution(8290180801182439669)
XLA Ops:
  0.0 2.8 %shard_map.109 = (bf16[64,9,2,128]{3,2,1,0:T(2,128)(2,1)}, f32[136,128]{1,0:T(8,128)}) custom-call(s32[3,64]{1,0:T(4,128)} %anchor_hbm.1, s32[1,64]{1,0:T(1,128)} %bitcast.14, bf16[64,128]{1,0:T(8,128)(2,1)} %coef_hbm.1, bf16[4096,128]{1,0:T(8,128)(2,1)} %bitcast.9), custom_call_target="tpu_custom_call" | custom-call | flops 134217728 | bytes 2097152 | tf_op jit(solution)/shard_map/pallas_call | solution.py:540
  2.8 18.7 %all-to-all-start = ((bf16[64,9,2,128]{3,2,1,0:T(2,128)(2,1)}), bf16[64,9,2,128]{3,2,1,0:T(2,128)(2,1)S(1)}, u32[]{:S(2)}, u32[]{:S(2)}) async-start(bf16[64,9,2,128]{3,2,1,0:T(2,128)(2,1)} %get-tuple-element.17), calls=%async_computation | async-start | bytes 589824 | tf_op jit(solution)/shard_map/all_to_all | solution.py:656
  21.6 1.6 %broadcast_select_fusion = f32[64,1,1024]{2,1,0:T(1,128)S(1)} fusion(pred[]{:T(512)S(6)} %and.25, f32[64,2,1024]{2,1,0:T(2,128)} %param.17), kind=kLoop, calls=%fused_computation.3 | loop fusion | flops 65536 | bytes 786433 | tf_op jit(solution)/shard_map/jit(_where)/select_n | solution.py:638
  23.2 0.8 fusion.2
  24.0 0.1 broadcast_in_dim.7
  24.1 0.3 concatenate.11
  24.5 0.0 copy-start.3
  24.5 0.2 copy.22
  24.7 0.2 broadcast_in_dim.8
  24.9 0.3 fusion.1
  25.3 0.2 copy.24
  25.5 0.1 pad_add_fusion.place_ref
  25.5 18.2 %all-to-all-done.recv_ref = bf16[64,9,2,128]{3,2,1,0:T(2,128)(2,1)S(1)} async-done(((bf16[64,9,2,128]{3,2,1,0:T(2,128)(2,1)}), bf16[64,9,2,128]{3,2,1,0:T(2,128)(2,1)S(1)}, u32[]{:S(2)}, u32[]{:S(2)}) %all-to-all-start) | async-done | bytes 294944 | tf_op jit(solution)/shard_map/all_to_all | solution.py:656
  43.8 0.0 copy-done.3
  43.8 0.0 copy-start.5
  43.8 0.0 copy-start.6
  43.8 0.0 copy-start.7
  43.8 4.9 %shard_map.110 = (bf16[8,128,128]{2,1,0:T(8,128)(2,1)S(1)}, f32[16,8,128]{2,1,0:T(8,128)S(1)}) custom-call(s32[2]{0:T(128)S(1)} %pad_add_fusion.place_ref, bf16[64,9,2,128]{3,2,1,0:T(2,128)(2,1)S(1)} %all-to-all-done.recv_ref, bf16[1024,768]{1,0:T(8,128)(2,1)S(1)} %copy-done.3), custom_call_target="tpu_custom_call" | custom-call | flops 2147483648 | bytes 4194304 | tf_op jit(solution)/shard_map/pallas_call | solution.py:566
  48.7 0.0 copy-start.4
  48.8 11.8 %all_to_all.20.recv_ref = bf16[8,128,128]{2,1,0:T(8,128)(2,1)S(1)} all-to-all(bf16[8,128,128]{2,1,0:T(8,128)(2,1)S(1)} %get-tuple-element.21), channel_id=1, replica_groups=mesh['slab'=64,'pencil'=8] {'pencil'}, dimensions={0} | all-to-all | bytes 524288 | tf_op jit(solution)/shard_map/all_to_all | solution.py:660
  60.5 0.0 copy-done.5
  60.5 0.0 copy-done.6
  60.5 0.0 copy-done.7
  60.5 1.7 %shard_map.111 = bf16[8,128,128]{2,1,0:T(8,128)(2,1)S(1)} custom-call(s32[2]{0:T(128)S(1)} %pad_add_fusion.place_ref, bf16[8,128,128]{2,1,0:T(8,128)(2,1)S(1)} %all_to_all.20.recv_ref, f32[576,128]{1,0:T(8,128)S(1)} %bitcast.12, f32[16,128]{1,0:T(8,128)S(1)} %copy-done.7, bf16[2,256,256]{2,1,0:T(8,128)(2,1)S(1)} %copy-done.5, bf16[2,256,256]{2,1,0:T(8,128)(2,1)S(1)} %copy-done.6), custom_call_target="tpu_custom_call" | custom-call | flops 452984832 | bytes 2097152 | tf_op jit(solution)/shard_map/pallas_call | solution.py:578
  62.2 9.9 %all_to_all.21.recv_ref = bf16[8,128,128]{2,1,0:T(8,128)(2,1)S(1)} all-to-all(bf16[8,128,128]{2,1,0:T(8,128)(2,1)S(1)} %shard_map.111), channel_id=1, replica_groups=mesh['slab'=64,'pencil'=8] {'pencil'}, dimensions={0} | all-to-all | bytes 524288 | tf_op jit(solution)/shard_map/all_to_all | solution.py:662
  72.2 0.0 copy-done.4
  72.2 0.0 copy-start.9
  72.2 0.0 copy-start.8
  72.2 0.0 copy-start.1
  72.2 4.6 %shard_map.112 = bf16[64,16,128]{2,1,0:T(8,128)(2,1)} custom-call(s32[2]{0:T(128)S(1)} %pad_add_fusion.place_ref, f32[16,8,128]{2,1,0:T(8,128)S(1)} %get-tuple-element.20.pos_ref, bf16[8,128,128]{2,1,0:T(8,128)(2,1)S(1)} %all_to_all.21.recv_ref, bf16[1024,768]{1,0:T(8,128)(2,1)S(1)} %copy-done.4), custom_call_target="tpu_custom_call" | custom-call | flops 2147483648 | bytes 4194304 | tf_op jit(solution)/shard_map/pallas_call | solution.py:589
  76.8 0.0 copy-start
  76.8 6.7 %all-to-all-start.3 = ((bf16[64,16,128]{2,1,0:T(8,128)(2,1)}), bf16[64,16,128]{2,1,0:T(8,128)(2,1)S(1)}, u32[]{:S(2)}, u32[]{:S(2)}) async-start(bf16[64,16,128]{2,1,0:T(8,128)(2,1)} %shard_map.112), calls=%async_computation.3 | async-start | bytes 524288 | tf_op jit(solution)/shard_map/all_to_all | solution.py:665
  83.5 0.0 copy-done.9
  83.5 0.1 copy.20
  83.6 0.0 copy-done.8
  83.7 12.8 %all_gather.3.group_ref = bf16[512,128]{1,0:T(8,128)(2,1)S(1)} all-gather(bf16[64,128]{1,0:T(8,128)(2,1)S(1)} %copy-done.8), channel_id=1, replica_groups=mesh['slab'=64,'pencil'=8] {'pencil'}, dimensions={0}, use_global_device_ids=true | all-gather | bytes 147456 | tf_op jit(solution)/shard_map/all_gather | solution.py:666
  96.4 0.0 copy-done.1
  96.4 0.0 copy-start.2
  96.4 0.9 copy-done.2
  97.3 4.0 %shard_map.113 = (f32[264,128]{1,0:T(8,128)S(1)}, f32[192,128]{1,0:T(8,128)}) custom-call(s32[64,1]{1,0:T(8,128)S(1)} %broadcast_and_fusion.ids_ref, f32[136,128]{1,0:T(8,128)S(1)} %copy-done.2, bf16[512,128]{1,0:T(8,128)(2,1)S(1)} %all_gather.3.group_ref, bf16[8192,128]{1,0:T(8,128)(2,1)S(1)} %bitcast.11), custom_call_target="tpu_custom_call" | custom-call | flops 268435456 | bytes 3145728 | tf_op jit(solution)/shard_map/pallas_call | solution.py:624
  101.3 2.7 %all-to-all-done.3.recv_ref = bf16[64,16,128]{2,1,0:T(8,128)(2,1)S(1)} async-done(((bf16[64,16,128]{2,1,0:T(8,128)(2,1)}), bf16[64,16,128]{2,1,0:T(8,128)(2,1)S(1)}, u32[]{:S(2)}, u32[]{:S(2)}) %all-to-all-start.3) | async-done | bytes 262176 | tf_op jit(solution)/shard_map/all_to_all | solution.py:665
  104.1 0.0 copy-done
  104.1 2.2 %shard_map.114 = f32[64,128]{1,0:T(8,128)} custom-call(f32[264,128]{1,0:T(8,128)S(1)} %get-tuple-element.24.phase_ref, f32[192,128]{1,0:T(8,128)} %get-tuple-element.25.side_hbm, bf16[64,16,128]{2,1,0:T(8,128)(2,1)S(1)} %all-to-all-done.3.recv_ref, bf16[4096,128]{1,0:T(8,128)(2,1)S(1)} %bitcast.10), custom_call_target="tpu_custom_call" | custom-call | flops 67108864 | bytes 2097152 | tf_op jit(solution)/shard_map/pallas_call | solution.py:607
  (2 shorter events, 0.0 us)
Async XLA Ops:
  2.8 41.0 %all-to-all-start = ((bf16[64,9,2,128]{3,2,1,0:T(2,128)(2,1)}), bf16[64,9,2,128]{3,2,1,0:T(2,128)(2,1)S(1)}, u32[]{:S(2)}, u32[]{:S(2)}) async-start(bf16[64,9,2,128]{3,2,1,0:T(2,128)(2,1)} %get-tuple-element.17), calls=%async_computation | async-start | bytes 589824 | tf_op jit(solution)/shard_map/all_to_all | solution.py:656
  24.5 19.3 %copy-start.3 = (bf16[1024,768]{1,0:T(8,128)(2,1)S(1)}, bf16[1024,768]{1,0:T(8,128)(2,1)}, u32[]{:S(2)}) copy-start(bf16[1024,768]{1,0:T(8,128)(2,1)} %constant.39.clone.table_ref) | copy-start | bytes 4718596
  43.8 16.8 %copy-start.5 = (bf16[2,256,256]{2,1,0:T(8,128)(2,1)S(1)}, bf16[2,256,256]{2,1,0:T(8,128)(2,1)}, u32[]{:S(2)}) copy-start(bf16[2,256,256]{2,1,0:T(8,128)(2,1)} %constant.41.clone.forward_ref) | copy-start | bytes 786436
  43.8 16.8 %copy-start.6 = (bf16[2,256,256]{2,1,0:T(8,128)(2,1)S(1)}, bf16[2,256,256]{2,1,0:T(8,128)(2,1)}, u32[]{:S(2)}) copy-start(bf16[2,256,256]{2,1,0:T(8,128)(2,1)} %constant.42.clone.inverse_ref) | copy-start | bytes 786436
  43.8 16.8 %copy-start.7 = (f32[16,128]{1,0:T(8,128)S(1)}, f32[16,128]{1,0:T(8,128)}, u32[]{:S(2)}) copy-start(f32[16,128]{1,0:T(8,128)} %constant.40.clone.turn_ref) | copy-start | bytes 24580
  48.7 23.5 %copy-start.4 = (bf16[1024,768]{1,0:T(8,128)(2,1)S(1)}, bf16[1024,768]{1,0:T(8,128)(2,1)}, u32[]{:S(2)}) copy-start(bf16[1024,768]{1,0:T(8,128)(2,1)} %constant.39.clone.table_ref) | copy-start | bytes 4718596
  72.2 11.3 %copy-start.9 = (s32[64,1]{0,1:T(1,128)S(1)}, s32[64,1]{0,1:T(1,128)}, u32[]{:S(2)}) copy-start(s32[64,1]{0,1:T(1,128)} %param.14) | copy-start | bytes 772
  72.2 11.4 %copy-start.8 = (bf16[64,128]{1,0:T(8,128)(2,1)S(1)}, bf16[64,128]{1,0:T(8,128)(2,1)}, u32[]{:S(2)}) copy-start(bf16[64,128]{1,0:T(8,128)(2,1)} %coef_hbm.1) | copy-start | bytes 49156
  72.2 24.2 %copy-start.1 = (bf16[64,1,128,128]{3,2,1,0:T(8,128)(2,1)S(1)}, bf16[64,1,128,128]{3,2,1,0:T(8,128)(2,1)}, u32[]{:S(2)}) copy-start(bf16[64,1,128,128]{3,2,1,0:T(8,128)(2,1)} %param.13) | copy-start | bytes 6291460
  76.8 27.3 %copy-start = (bf16[64,64,128]{2,1,0:T(8,128)(2,1)S(1)}, bf16[64,64,128]{2,1,0:T(8,128)(2,1)}, u32[]{:S(2)}) copy-start(bf16[64,64,128]{2,1,0:T(8,128)(2,1)} %param.12) | copy-start | bytes 3145732
  76.8 27.2 %all-to-all-start.3 = ((bf16[64,16,128]{2,1,0:T(8,128)(2,1)}), bf16[64,16,128]{2,1,0:T(8,128)(2,1)S(1)}, u32[]{:S(2)}, u32[]{:S(2)}) async-start(bf16[64,16,128]{2,1,0:T(8,128)(2,1)} %shard_map.112), calls=%async_computation.3 | async-start | bytes 524288 | tf_op jit(solution)/shard_map/all_to_all | solution.py:665
  96.4 0.9 copy-start.2

commit v5 on v4

--- a/solution.py
+++ b/solution.py
@@ -24,7 +24,10 @@
 MORE = LINES + 8
 BOXES = SLABS * BOX
 SMALL = 8 + 128
-SIDE = BOX + 128
+NOTES = 2 * SLABS
+ORDER = NOTES + 8
+CLOSE = ORDER + BOX
+SIDE = CLOSE + BOX
 TILE = 256
 WINDOW = 48
 SHIFT = SLABS - WINDOW
@@ -116,10 +119,10 @@
     return first, second, third, fourth
 
 
-def phases(depth, phase_ref):
+def phases(depth, phase_ref, count):
     second = (iota((SLABS, 128), 1) >= BOX).astype(jnp.int32)
     wave = iota((SLABS, 128), 0)
-    for k in range(4):
+    for k in range(count):
         z = depth + k
         step = jnp.where(wave == 0, second * (NZ // 2) * z, wave * z + second * (NZ // 4))
         phase_ref[k * SLABS : (k + 1) * SLABS] = cosine_of(step & (NZ - 1))
@@ -170,7 +173,7 @@
     small_ref[8:] = jnp.where(row < BOX, hot, 0.0)
     notes = pltpu.make_async_copy(small_ref, small_hbm, sems.at[8])
     notes.start()
-    phases(depth, phase_ref)
+    phases(depth, phase_ref, 4)
 
     large.wait()
     every = dot(proj_ref[...], twice, NT)
@@ -455,17 +458,19 @@
         copy.wait()
 
 
-def finish_kernel(
-    phase_ref, side_hbm, recv_ref, proj_ref, out_ref, value_ref, wide_ref, side_ref, sem
-):
-    copy = pltpu.make_async_copy(side_hbm, side_ref, sem)
-    copy.start()
+def finish_kernel(side_ref, recv_ref, proj_ref, out_ref, value_ref, wide_ref):
     totals = [jnp.zeros((16, 128), F32) for _ in range(4)]
     for wave in range(SLABS):
         value = recv_ref[wave].astype(F32)
-        for k in range(4):
-            totals[k] = totals[k] + phase_ref[k * SLABS + wave : k * SLABS + wave + 1, :] * value
-    turn = phase_ref[4 * SLABS : 4 * SLABS + 1, :].astype(jnp.int32) & 3
+        terms = [side_ref[k * SLABS + wave : k * SLABS + wave + 1, :] * value for k in range(2)]
+        if wave == 0:
+            twice = jnp.where(iota((16, 128), 1) < BOX, 2.0, -2.0)
+        else:
+            twice = 2.0 * math.cos(2.0 * math.pi * wave / NZ)
+        for k in range(2, 4):
+            terms.append(twice * terms[k - 1] - terms[k - 2])
+        totals = [total + term for total, term in zip(totals, terms)]
+    turn = side_ref[NOTES : NOTES + 1, :].astype(jnp.int32) & 3
     row = iota((16, 128), 0) & 3
     for k in range(4):
         value = totals[k] + pltpu.roll(totals[k], BOX, 1)
@@ -476,8 +481,8 @@
             )
             out = jnp.where(turn == m, moved, out)
         value_ref[pl.ds(k, 16, stride=4), :] = out
-    copy.wait()
-    value = dot(value_ref[...].astype(BF16), side_ref[BOX:].astype(BF16))
+    back = jnp.concatenate([side_ref[ORDER:CLOSE], jnp.zeros((BOX, 128), F32)], 0).astype(BF16)
+    value = dot(value_ref[...].astype(BF16), back)
     value = jnp.concatenate([value, value], 0).T[0:BOX]
     box = iota((BOX, 128), 0)
     half = (iota((BOX, 128), 1) >= STENCIL).astype(jnp.int32)
@@ -485,13 +490,12 @@
         wide_ref[:, 128 * m : 128 * (m + 1)] = jnp.where(
             box == 2 * m + half, value, 0.0
         ).astype(BF16)
-    out_ref[...] = dot(wide_ref[...], proj_ref[...]) + side_ref[0:BOX]
-
-
-def near_kernel(ids_ref, small_ref, group_ref, near_ref, phase_ref, side_hbm, side_ref, sem):
-    phases(small_ref[1:2, :].astype(jnp.int32), phase_ref)
-    phase_ref[4 * SLABS :] = small_ref[0:8]
-    side_ref[BOX:] = small_ref[8:]
+    out_ref[...] = dot(wide_ref[...], proj_ref[...]) + side_ref[CLOSE:]
+
+
+def near_kernel(ids_ref, small_ref, group_ref, near_ref, side_ref):
+    phases(small_ref[1:2, :].astype(jnp.int32), side_ref, 2)
+    side_ref[NOTES:CLOSE] = small_ref[0 : 8 + BOX]
     hot = jnp.where(iota((BOX, GROUP), 1) == ids_ref[...], 1.0, 0.0).astype(BF16)
     partner = dot(hot, group_ref[...]).astype(BF16)
     twice = jnp.concatenate([partner, partner], 0)
@@ -505,10 +509,7 @@
         return total
 
     total = lax.fori_loop(0, BOX // 4, step, jnp.zeros((FUNCS, 128), F32))
-    side_ref[0:BOX] = total.T[0:BOX]
-    copy = pltpu.make_async_copy(side_ref, side_hbm, sem)
-    copy.start()
-    copy.wait()
+    side_ref[CLOSE:] = total.T[0:BOX]
 
 
 VMEM = pl.BlockSpec(memory_space=pltpu.VMEM)
@@ -603,30 +604,23 @@
     )(place, pos, received, table)
 
 
-def finish(phase, side, received, flat):
+def finish(side, received, flat):
     return call(
         finish_kernel,
         struct(BOX, FUNCS),
-        [VMEM, HBM, VMEM, VMEM],
-        [
-            pltpu.VMEM((STENCIL, 128), F32),
-            pltpu.VMEM((BOX, BOX * STENCIL), BF16),
-            pltpu.VMEM((SIDE, 128), F32),
-            pltpu.SemaphoreType.DMA,
-        ],
+        [VMEM] * 3,
+        [pltpu.VMEM((STENCIL, 128), F32), pltpu.VMEM((BOX, BOX * STENCIL), BF16)],
         limit=8,
         flops=2 * BOX * BOXES * FUNCS,
         moved=2 << 20,
-    )(*resident(phase, space=pltpu.VMEM), *resident(side), received, flat)
+    )(*resident(side, space=pltpu.VMEM), received, flat)
 
 
 def near(ids, small, group, blocks):
     return call(
         near_kernel,
-        (pltpu.VMEM((4 * SLABS + 8, 128), F32), pltpu.HBM((SIDE, 128), F32)),
+        pltpu.VMEM((SIDE, 128), F32),
         [VMEM] * 4,
-        [pltpu.VMEM((SIDE, 128), F32), pltpu.SemaphoreType.DMA],
-        outs=(VMEM, HBM),
         limit=8,
         flops=2 * BOX * FUNCS * FUNCS * 128,
         moved=3 << 20,
@@ -665,8 +659,8 @@
     received = lax.all_to_all(send, "slab", split_axis=0, concat_axis=0, tiled=True)
     group = lax.all_gather(own, "pencil", axis=0, tiled=True)
     blocks = near_blocks.reshape(BOX * FUNCS, FUNCS)
-    phase, side = near(near_ids & (GROUP - 1), small, group, blocks)
-    return finish(phase, side, received, flat)
+    side = near(near_ids & (GROUP - 1), small, group, blocks)
+    return finish(side, received, flat)
 
 
 def solution(mesh):

time: 107 us -> 106 us (level)
  Pallas kernels: 20.2 us -> 18.8 us
    pallas_call x2, Pallas kernels: 6.23 us -> 4.75 us  [the longest x1 3.32 us: near(): call(near_kernel, pltpu.VMEM((SIDE, 128), F32), [VMEM] * 4, limit=8, flop...]
    all_to_all x2, waiting for transfers between devices: 20.9 us -> 19.9 us  [per_device(): lax.all_to_all(send, 'slab', split_axis=0, concat_axis=0, tiled=True)]
  transfers between devices with their start and end apart: 2 -> 2, of which waited for: 2 -> 2; matrix products, arithmetic and copies ran while one was open for 4% -> 6% of each run, Pallas kernels for 4% -> 3%
where the time goes in v5:
time: 106 us
  blocking collectives  34.5 us (33%)
  starting transfers between devices  25.4 us (24%)
  waiting for transfers between devices  19.9 us (19%)
  Pallas kernels  18.8 us (18%)
  other arithmetic  3.65 us (3%)
  local copies, waits for them, and re-layouts  3.11 us (3%)
    all_to_all x2, starting transfers between devices, per_device(): lax.all_to_all(send, 'slab', split_axis=0, concat_axis=0, tiled=True)  25.4 us
    all_to_all x2, blocking collectives, per_device(): lax.all_to_all(send, 'pencil', split_axis=0, concat_axis=0, tiled=True)  21.7 us
    all_to_all x2, waiting for transfers between devices, per_device(): lax.all_to_all(send, 'slab', split_axis=0, concat_axis=0, tiled=True)  19.9 us
    all_gather x1, blocking collectives, per_device(): group = lax.all_gather(own, 'pencil', axis=0, tiled=True)  12.8 us
    pallas_call x1, Pallas kernels, spread(): call(spread_kernel, (struct(PENCILS, 2 * LINES, CY, kind=BF16), struct(SL...  4.94 us
    pallas_call x1, Pallas kernels, sample(): call(sample_kernel, pltpu.HBM((SLABS, 16, 128), BF16), [SMEM] + [VMEM] *...  4.59 us
    pallas_call x1, Pallas kernels, near(): call(near_kernel, pltpu.VMEM((SIDE, 128), F32), [VMEM] * 4, limit=8, flop...  3.32 us
    pallas_call x1, Pallas kernels, project(): call(project_kernel, (pltpu.HBM((SLABS, ROWS // 2, 2, 128), BF16), pltpu....  2.78 us
  transfers between devices with their start and end apart: 2, of which 2 were waited for; matrix products, arithmetic and copies ran while one was open for 6% of the time, Pallas kernels for 3%

profile of v5, /device:TPU:8, one launch (start us, length us, event | category | flops | bytes accessed | tf_op | source)
XLA Modules:
  0.0 105.5 jit_solution(297493664970211947)
XLA Ops:
  0.0 2.8 %shard_map.109 = (bf16[64,9,2,128]{3,2,1,0:T(2,128)(2,1)}, f32[136,128]{1,0:T(8,128)}) custom-call(s32[3,64]{1,0:T(4,128)} %anchor_hbm.1, s32[1,64]{1,0:T(1,128)} %bitcast.14, bf16[64,128]{1,0:T(8,128)(2,1)} %coef_hbm.1, bf16[4096,128]{1,0:T(8,128)(2,1)} %bitcast.9), custom_call_target="tpu_custom_call" | custom-call | flops 134217728 | bytes 2097152 | tf_op jit(solution)/shard_map/pallas_call | solution.py:541
  2.8 18.7 %all-to-all-start = ((bf16[64,9,2,128]{3,2,1,0:T(2,128)(2,1)}), bf16[64,9,2,128]{3,2,1,0:T(2,128)(2,1)S(1)}, u32[]{:S(2)}, u32[]{:S(2)}) async-start(bf16[64,9,2,128]{3,2,1,0:T(2,128)(2,1)} %get-tuple-element.15), calls=%async_computation | async-start | bytes 589824 | tf_op jit(solution)/shard_map/all_to_all | solution.py:650
  21.6 1.6 %broadcast_select_fusion = f32[64,1,1024]{2,1,0:T(1,128)S(1)} fusion(pred[]{:T(512)S(6)} %and.25, f32[64,2,1024]{2,1,0:T(2,128)} %param.17), kind=kLoop, calls=%fused_computation.3 | loop fusion | flops 65536 | bytes 786433 | tf_op jit(solution)/shard_map/jit(_where)/select_n | solution.py:632
  23.2 0.8 fusion.2
  24.0 0.1 broadcast_in_dim.7
  24.1 0.3 concatenate.11
  24.5 0.0 copy-start.3
  24.5 0.2 copy.22
  24.7 0.2 broadcast_in_dim.8
  24.9 1.1 %fusion.1 = f32[8,72,128]{1,0,2:T(8,128)} fusion(f32[8,128,8]{0,2,1:T(8,128)S(1)} %broadcast_in_dim.8, f32[63,128,8]{0,2,1:T(8,128)S(1)} %bitcast.13, f32[1,128,8]{0,2,1:T(8,128)S(1)} %concatenate.11, f32[]{:T(128)S(6)} %select_n.33), kind=kLoop, calls=%fused_computation.2 | loop fusion | flops 294912 | bytes 589828 | tf_op jit(solution)/shard_map/transpose | solution.py:636
  26.1 1.2 %copy.24 = f32[8,72,128]{2,1,0:T(8,128)S(1)} copy(f32[8,72,128]{1,0,2:T(8,128)} %fusion.1) | data formatting | bytes 589824 | tf_op jit(solution)/shard_map/transpose | solution.py:636
  27.3 0.1 pad_add_fusion.place_ref
  27.4 16.4 %all-to-all-done.recv_ref = bf16[64,9,2,128]{3,2,1,0:T(2,128)(2,1)S(1)} async-done(((bf16[64,9,2,128]{3,2,1,0:T(2,128)(2,1)}), bf16[64,9,2,128]{3,2,1,0:T(2,128)(2,1)S(1)}, u32[]{:S(2)}, u32[]{:S(2)}) %all-to-all-start) | async-done | bytes 294944 | tf_op jit(solution)/shard_map/all_to_all | solution.py:650
  43.8 0.0 copy-done.3
  43.8 0.0 copy-start.5
  43.8 0.0 copy-start.6
  43.8 0.0 copy-start.7
  43.8 4.9 %shard_map.110 = (bf16[8,128,128]{2,1,0:T(8,128)(2,1)S(1)}, f32[16,8,128]{2,1,0:T(8,128)S(1)}) custom-call(s32[2]{0:T(128)S(1)} %pad_add_fusion.place_ref, bf16[64,9,2,128]{3,2,1,0:T(2,128)(2,1)S(1)} %all-to-all-done.recv_ref, bf16[1024,768]{1,0:T(8,128)(2,1)S(1)} %copy-done.3), custom_call_target="tpu_custom_call" | custom-call | flops 2147483648 | bytes 4194304 | tf_op jit(solution)/shard_map/pallas_call | solution.py:567
  48.7 0.0 copy-start.4
  48.8 11.8 %all_to_all.20.recv_ref = bf16[8,128,128]{2,1,0:T(8,128)(2,1)S(1)} all-to-all(bf16[8,128,128]{2,1,0:T(8,128)(2,1)S(1)} %get-tuple-element.19), channel_id=1, replica_groups=mesh['slab'=64,'pencil'=8] {'pencil'}, dimensions={0} | all-to-all | bytes 524288 | tf_op jit(solution)/shard_map/all_to_all | solution.py:654
  60.5 0.0 copy-done.5
  60.5 0.0 copy-done.6
  60.5 0.0 copy-done.7
  60.5 1.7 %shard_map.111 = bf16[8,128,128]{2,1,0:T(8,128)(2,1)S(1)} custom-call(s32[2]{0:T(128)S(1)} %pad_add_fusion.place_ref, bf16[8,128,128]{2,1,0:T(8,128)(2,1)S(1)} %all_to_all.20.recv_ref, f32[576,128]{1,0:T(8,128)S(1)} %bitcast.12, f32[16,128]{1,0:T(8,128)S(1)} %copy-done.7, bf16[2,256,256]{2,1,0:T(8,128)(2,1)S(1)} %copy-done.5, bf16[2,256,256]{2,1,0:T(8,128)(2,1)S(1)} %copy-done.6), custom_call_target="tpu_custom_call" | custom-call | flops 452984832 | bytes 2097152 | tf_op jit(solution)/shard_map/pallas_call | solution.py:579
  62.3 9.9 %all_to_all.21.recv_ref = bf16[8,128,128]{2,1,0:T(8,128)(2,1)S(1)} all-to-all(bf16[8,128,128]{2,1,0:T(8,128)(2,1)S(1)} %shard_map.111), channel_id=1, replica_groups=mesh['slab'=64,'pencil'=8] {'pencil'}, dimensions={0} | all-to-all | bytes 524288 | tf_op jit(solution)/shard_map/all_to_all | solution.py:656
  72.2 0.0 copy-done.4
  72.2 0.0 copy-start.9
  72.2 0.0 copy-start.8
  72.2 0.0 copy-start.1
  72.2 4.6 %shard_map.112 = bf16[64,16,128]{2,1,0:T(8,128)(2,1)} custom-call(s32[2]{0:T(128)S(1)} %pad_add_fusion.place_ref, f32[16,8,128]{2,1,0:T(8,128)S(1)} %get-tuple-element.18.pos_ref, bf16[8,128,128]{2,1,0:T(8,128)(2,1)S(1)} %all_to_all.21.recv_ref, bf16[1024,768]{1,0:T(8,128)(2,1)S(1)} %copy-done.4), custom_call_target="tpu_custom_call" | custom-call | flops 2147483648 | bytes 4194304 | tf_op jit(solution)/shard_map/pallas_call | solution.py:590
  76.8 0.0 copy-start
  76.8 6.7 %all-to-all-start.3 = ((bf16[64,16,128]{2,1,0:T(8,128)(2,1)}), bf16[64,16,128]{2,1,0:T(8,128)(2,1)S(1)}, u32[]{:S(2)}, u32[]{:S(2)}) async-start(bf16[64,16,128]{2,1,0:T(8,128)(2,1)} %shard_map.112), calls=%async_computation.3 | async-start | bytes 524288 | tf_op jit(solution)/shard_map/all_to_all | solution.py:659
  83.5 0.0 copy-done.9
  83.6 0.1 copy.20
  83.7 0.0 copy-done.8
  83.7 12.8 %all_gather.3.group_ref = bf16[512,128]{1,0:T(8,128)(2,1)S(1)} all-gather(bf16[64,128]{1,0:T(8,128)(2,1)S(1)} %copy-done.8), channel_id=1, replica_groups=mesh['slab'=64,'pencil'=8] {'pencil'}, dimensions={0}, use_global_device_ids=true | all-gather | bytes 147456 | tf_op jit(solution)/shard_map/all_gather | solution.py:660
  96.4 0.0 copy-done.1
  96.4 0.0 copy-start.2
  96.4 0.9 copy-done.2
  97.3 3.3 %shard_map.113.side_ref = f32[264,128]{1,0:T(8,128)S(1)} custom-call(s32[64,1]{1,0:T(8,128)S(1)} %broadcast_and_fusion.ids_ref, f32[136,128]{1,0:T(8,128)S(1)} %copy-done.2, bf16[512,128]{1,0:T(8,128)(2,1)S(1)} %all_gather.3.group_ref, bf16[8192,128]{1,0:T(8,128)(2,1)S(1)} %bitcast.11), custom_call_target="tpu_custom_call" | custom-call | flops 268435456 | bytes 3145728 | tf_op jit(solution)/shard_map/pallas_call | solution.py:620
  100.6 3.4 %all-to-all-done.3.recv_ref = bf16[64,16,128]{2,1,0:T(8,128)(2,1)S(1)} async-done(((bf16[64,16,128]{2,1,0:T(8,128)(2,1)}), bf16[64,16,128]{2,1,0:T(8,128)(2,1)S(1)}, u32[]{:S(2)}, u32[]{:S(2)}) %all-to-all-start.3) | async-done | bytes 262176 | tf_op jit(solution)/shard_map/all_to_all | solution.py:659
  104.1 0.0 copy-done
  104.1 1.4 %shard_map.114 = f32[64,128]{1,0:T(8,128)} custom-call(f32[264,128]{1,0:T(8,128)S(1)} %shard_map.113.side_ref, bf16[64,16,128]{2,1,0:T(8,128)(2,1)S(1)} %all-to-all-done.3.recv_ref, bf16[4096,128]{1,0:T(8,128)(2,1)S(1)} %bitcast.10), custom_call_target="tpu_custom_call" | custom-call | flops 67108864 | bytes 2097152 | tf_op jit(solution)/shard_map/pallas_call | solution.py:608
  (2 shorter events, 0.0 us)
Async XLA Ops:
  2.8 41.0 %all-to-all-start = ((bf16[64,9,2,128]{3,2,1,0:T(2,128)(2,1)}), bf16[64,9,2,128]{3,2,1,0:T(2,128)(2,1)S(1)}, u32[]{:S(2)}, u32[]{:S(2)}) async-start(bf16[64,9,2,128]{3,2,1,0:T(2,128)(2,1)} %get-tuple-element.15), calls=%async_computation | async-start | bytes 589824 | tf_op jit(solution)/shard_map/all_to_all | solution.py:650
  24.5 19.3 %copy-start.3 = (bf16[1024,768]{1,0:T(8,128)(2,1)S(1)}, bf16[1024,768]{1,0:T(8,128)(2,1)}, u32[]{:S(2)}) copy-start(bf16[1024,768]{1,0:T(8,128)(2,1)} %constant.39.clone.table_ref) | copy-start | bytes 4718596
  43.8 16.8 %copy-start.5 = (bf16[2,256,256]{2,1,0:T(8,128)(2,1)S(1)}, bf16[2,256,256]{2,1,0:T(8,128)(2,1)}, u32[]{:S(2)}) copy-start(bf16[2,256,256]{2,1,0:T(8,128)(2,1)} %constant.41.clone.forward_ref) | copy-start | bytes 786436
  43.8 16.8 %copy-start.6 = (bf16[2,256,256]{2,1,0:T(8,128)(2,1)S(1)}, bf16[2,256,256]{2,1,0:T(8,128)(2,1)}, u32[]{:S(2)}) copy-start(bf16[2,256,256]{2,1,0:T(8,128)(2,1)} %constant.42.clone.inverse_ref) | copy-start | bytes 786436
  43.8 16.8 %copy-start.7 = (f32[16,128]{1,0:T(8,128)S(1)}, f32[16,128]{1,0:T(8,128)}, u32[]{:S(2)}) copy-start(f32[16,128]{1,0:T(8,128)} %constant.40.clone.turn_ref) | copy-start | bytes 24580
  48.7 23.5 %copy-start.4 = (bf16[1024,768]{1,0:T(8,128)(2,1)S(1)}, bf16[1024,768]{1,0:T(8,128)(2,1)}, u32[]{:S(2)}) copy-start(bf16[1024,768]{1,0:T(8,128)(2,1)} %constant.39.clone.table_ref) | copy-start | bytes 4718596
  72.2 11.3 %copy-start.9 = (s32[64,1]{0,1:T(1,128)S(1)}, s32[64,1]{0,1:T(1,128)}, u32[]{:S(2)}) copy-start(s32[64,1]{0,1:T(1,128)} %param.14) | copy-start | bytes 772
  72.2 11.5 %copy-start.8 = (bf16[64,128]{1,0:T(8,128)(2,1)S(1)}, bf16[64,128]{1,0:T(8,128)(2,1)}, u32[]{:S(2)}) copy-start(bf16[64,128]{1,0:T(8,128)(2,1)} %coef_hbm.1) | copy-start | bytes 49156
  72.2 24.2 %copy-start.1 = (bf16[64,1,128,128]{3,2,1,0:T(8,128)(2,1)S(1)}, bf16[64,1,128,128]{3,2,1,0:T(8,128)(2,1)}, u32[]{:S(2)}) copy-start(bf16[64,1,128,128]{3,2,1,0:T(8,128)(2,1)} %param.13) | copy-start | bytes 6291460
  76.8 27.3 %copy-start = (bf16[64,64,128]{2,1,0:T(8,128)(2,1)S(1)}, bf16[64,64,128]{2,1,0:T(8,128)(2,1)}, u32[]{:S(2)}) copy-start(bf16[64,64,128]{2,1,0:T(8,128)(2,1)} %param.12) | copy-start | bytes 3145732
  76.8 27.2 %all-to-all-start.3 = ((bf16[64,16,128]{2,1,0:T(8,128)(2,1)}), bf16[64,16,128]{2,1,0:T(8,128)(2,1)S(1)}, u32[]{:S(2)}, u32[]{:S(2)}) async-start(bf16[64,16,128]{2,1,0:T(8,128)(2,1)} %shard_map.112), calls=%async_computation.3 | async-start | bytes 524288 | tf_op jit(solution)/shard_map/all_to_all | solution.py:659
  96.4 0.9 copy-start.2

commit v6 on v5

--- a/solution.py
+++ b/solution.py
@@ -90,6 +90,10 @@
 
 def dot(a, b, dims=NN):
     return lax.dot_general(a, b, dims, preferred_element_type=F32)
+
+
+def one_hot(cells, code):
+    return jnp.where(cells == code.astype(BF16), jnp.ones((), BF16), jnp.zeros((), BF16))
 
 
 def split(value):
@@ -219,7 +223,7 @@
 
 
 def spread_kernel(place_ref, recv_ref, table_ref, send_ref, pos_ref, row_ref, hot_ref):
-    cells = iota((TILE, 128), 0).astype(F32)
+    cells = iota((TILE, 128), 0).astype(F32).astype(BF16)
     y_cells = iota((CY, 128), 0).astype(F32)
     upper = iota((8, 128), 0) < 4
 
@@ -239,7 +243,7 @@
         code, y_place = real[16:17], imag[16:17]
         start = half * (BOXES // 2) + step * 128
         away = y_cells - y_place
-        inside = jnp.where((away >= 0.0) & (away < 4.0), 1.0, 0.0).astype(BF16)
+        inside = jnp.clip(2.5 - jnp.abs(away.astype(BF16) - 1.5), 0.0, 1.0)
         inside = inside.reshape(8, 16, 128)
         for i in range(4):
             for c, source in enumerate((real, imag)):
@@ -250,7 +254,7 @@
                 both = jnp.concatenate([both, both], 0).astype(BF16)
                 rows = (inside * both[None]).reshape(CY, 128)
                 row_ref[(2 * i + c) * CY : (2 * i + c + 1) * CY, start : start + 128] = rows
-        hot_ref[:, start : start + 128] = jnp.where(cells == code, 1.0, 0.0).astype(BF16)
+        hot_ref[:, start : start + 128] = one_hot(cells, code)
 
     count = 4
     steps = SLABS // 4 // count
@@ -411,7 +415,7 @@
             moved = part if i == 0 else pltpu.roll(part, SPAN - WINDOW * i, 1)
             left_ref[half, 2 * CY * i : 2 * CY * (i + 1), :] = moved[:, :TILE].astype(BF16)
 
-    cells = iota((TILE, 128), 0).astype(F32)
+    cells = iota((TILE, 128), 0).astype(F32).astype(BF16)
     y_cells = (iota((16, 8, 128), 0) * 8 + iota((16, 8, 128), 1)).astype(F32)
     upper = iota((8, 128), 0) < 4
 
@@ -423,7 +427,7 @@
             for quad in quads:
                 place = pos_ref[quad]
                 code, y_place = place[2 * half : 2 * half + 1], place[2 * half + 1 : 2 * half + 2]
-                hot.append(jnp.where(cells == code, 1.0, 0.0).astype(BF16))
+                hot.append(one_hot(cells, code))
                 away = y_cells - y_place[None]
                 inside.append((away >= 0.0) & (away < 4.0))
             hot = jnp.concatenate(hot, 1)

time: 106 us -> 106 us (level)
  no operation moved by 1% of the time
where the time goes in v6:
time: 106 us; the launch traced here: 105 us
  blocking collectives  34.5 us (33%)
  starting transfers between devices  25.5 us (24%)
  waiting for transfers between devices  19.9 us (19%)
  Pallas kernels  18.3 us (17%)
  other arithmetic  3.65 us (3%)
  local copies, waits for them, and re-layouts  3.11 us (3%)
    all_to_all x2, starting transfers between devices, per_device(): lax.all_to_all(send, 'slab', split_axis=0, concat_axis=0, tiled=True)  25.5 us
    all_to_all x2, blocking collectives, per_device(): lax.all_to_all(send, 'pencil', split_axis=0, concat_axis=0, tiled=True)  21.7 us
    all_to_all x2, waiting for transfers between devices, per_device(): lax.all_to_all(send, 'slab', split_axis=0, concat_axis=0, tiled=True)  19.9 us
    all_gather x1, blocking collectives, per_device(): group = lax.all_gather(own, 'pencil', axis=0, tiled=True)  12.8 us
    pallas_call x1, Pallas kernels, spread(): call(spread_kernel, (struct(PENCILS, 2 * LINES, CY, kind=BF16), struct(SL...  4.53 us
    pallas_call x1, Pallas kernels, sample(): call(sample_kernel, pltpu.HBM((SLABS, 16, 128), BF16), [SMEM] + [VMEM] *...  4.51 us
    pallas_call x1, Pallas kernels, near(): call(near_kernel, pltpu.VMEM((SIDE, 128), F32), [VMEM] * 4, limit=8, flop...  3.32 us
    pallas_call x1, Pallas kernels, project(): call(project_kernel, (pltpu.HBM((SLABS, ROWS // 2, 2, 128), BF16), pltpu....  2.78 us
  transfers between devices with their start and end apart: 2, of which 2 were waited for; matrix products, arithmetic and copies ran while one was open for 6% of the time, Pallas kernels for 3%

profile of v6, /device:TPU:8, one launch (start us, length us, event | category | flops | bytes accessed | tf_op | source)
XLA Modules:
  0.0 105.0 jit_solution(10907670893327768322)
XLA Ops:
  0.0 2.8 %shard_map.109 = (bf16[64,9,2,128]{3,2,1,0:T(2,128)(2,1)}, f32[136,128]{1,0:T(8,128)}) custom-call(s32[3,64]{1,0:T(4,128)} %anchor_hbm.1, s32[1,64]{1,0:T(1,128)} %bitcast.14, bf16[64,128]{1,0:T(8,128)(2,1)} %coef_hbm.1, bf16[4096,128]{1,0:T(8,128)(2,1)} %bitcast.9), custom_call_target="tpu_custom_call" | custom-call | flops 134217728 | bytes 2097152 | tf_op jit(solution)/shard_map/pallas_call | solution.py:545
  2.8 18.7 %all-to-all-start = ((bf16[64,9,2,128]{3,2,1,0:T(2,128)(2,1)}), bf16[64,9,2,128]{3,2,1,0:T(2,128)(2,1)S(1)}, u32[]{:S(2)}, u32[]{:S(2)}) async-start(bf16[64,9,2,128]{3,2,1,0:T(2,128)(2,1)} %get-tuple-element.15), calls=%async_computation | async-start | bytes 589824 | tf_op jit(solution)/shard_map/all_to_all | solution.py:654
  21.6 1.6 %broadcast_select_fusion = f32[64,1,1024]{2,1,0:T(1,128)S(1)} fusion(pred[]{:T(512)S(6)} %and.25, f32[64,2,1024]{2,1,0:T(2,128)} %param.17), kind=kLoop, calls=%fused_computation.3 | loop fusion | flops 65536 | bytes 786433 | tf_op jit(solution)/shard_map/jit(_where)/select_n | solution.py:636
  23.2 0.8 fusion.2
  24.0 0.1 broadcast_in_dim.7
  24.1 0.3 concatenate.11
  24.5 0.0 copy-start.3
  24.5 0.2 copy.22
  24.7 0.2 broadcast_in_dim.8
  24.9 1.1 %fusion.1 = f32[8,72,128]{1,0,2:T(8,128)} fusion(f32[8,128,8]{0,2,1:T(8,128)S(1)} %broadcast_in_dim.8, f32[63,128,8]{0,2,1:T(8,128)S(1)} %bitcast.13, f32[1,128,8]{0,2,1:T(8,128)S(1)} %concatenate.11, f32[]{:T(128)S(6)} %select_n.33), kind=kLoop, calls=%fused_computation.2 | loop fusion | flops 294912 | bytes 589828 | tf_op jit(solution)/shard_map/transpose | solution.py:640
  26.1 1.2 %copy.24 = f32[8,72,128]{2,1,0:T(8,128)S(1)} copy(f32[8,72,128]{1,0,2:T(8,128)} %fusion.1) | data formatting | bytes 589824 | tf_op jit(solution)/shard_map/transpose | solution.py:640
  27.3 0.1 pad_add_fusion.place_ref
  27.4 16.4 %all-to-all-done.recv_ref = bf16[64,9,2,128]{3,2,1,0:T(2,128)(2,1)S(1)} async-done(((bf16[64,9,2,128]{3,2,1,0:T(2,128)(2,1)}), bf16[64,9,2,128]{3,2,1,0:T(2,128)(2,1)S(1)}, u32[]{:S(2)}, u32[]{:S(2)}) %all-to-all-start) | async-done | bytes 294944 | tf_op jit(solution)/shard_map/all_to_all | solution.py:654
  43.8 0.0 copy-done.3
  43.8 0.0 copy-start.5
  43.8 0.0 copy-start.6
  43.8 0.0 copy-start.7
  43.8 4.5 %shard_map.110 = (bf16[8,128,128]{2,1,0:T(8,128)(2,1)S(1)}, f32[16,8,128]{2,1,0:T(8,128)S(1)}) custom-call(s32[2]{0:T(128)S(1)} %pad_add_fusion.place_ref, bf16[64,9,2,128]{3,2,1,0:T(2,128)(2,1)S(1)} %all-to-all-done.recv_ref, bf16[1024,768]{1,0:T(8,128)(2,1)S(1)} %copy-done.3), custom_call_target="tpu_custom_call" | custom-call | flops 2147483648 | bytes 4194304 | tf_op jit(solution)/shard_map/pallas_call | solution.py:571
  48.3 0.0 copy-start.4
  48.3 11.8 %all_to_all.20.recv_ref = bf16[8,128,128]{2,1,0:T(8,128)(2,1)S(1)} all-to-all(bf16[8,128,128]{2,1,0:T(8,128)(2,1)S(1)} %get-tuple-element.19), channel_id=1, replica_groups=mesh['slab'=64,'pencil'=8] {'pencil'}, dimensions={0} | all-to-all | bytes 524288 | tf_op jit(solution)/shard_map/all_to_all | solution.py:658
  60.1 0.0 copy-done.5
  60.1 0.0 copy-done.6
  60.1 0.0 copy-done.7
  60.1 1.7 %shard_map.111 = bf16[8,128,128]{2,1,0:T(8,128)(2,1)S(1)} custom-call(s32[2]{0:T(128)S(1)} %pad_add_fusion.place_ref, bf16[8,128,128]{2,1,0:T(8,128)(2,1)S(1)} %all_to_all.20.recv_ref, f32[576,128]{1,0:T(8,128)S(1)} %bitcast.12, f32[16,128]{1,0:T(8,128)S(1)} %copy-done.7, bf16[2,256,256]{2,1,0:T(8,128)(2,1)S(1)} %copy-done.5, bf16[2,256,256]{2,1,0:T(8,128)(2,1)S(1)} %copy-done.6), custom_call_target="tpu_custom_call" | custom-call | flops 452984832 | bytes 2097152 | tf_op jit(solution)/shard_map/pallas_call | solution.py:583
  61.8 9.9 %all_to_all.21.recv_ref = bf16[8,128,128]{2,1,0:T(8,128)(2,1)S(1)} all-to-all(bf16[8,128,128]{2,1,0:T(8,128)(2,1)S(1)} %shard_map.111), channel_id=1, replica_groups=mesh['slab'=64,'pencil'=8] {'pencil'}, dimensions={0} | all-to-all | bytes 524288 | tf_op jit(solution)/shard_map/all_to_all | solution.py:660
  71.8 0.0 copy-done.4
  71.8 0.0 copy-start.9
  71.8 0.0 copy-start.8
  71.8 0.0 copy-start.1
  71.8 4.5 %shard_map.112 = bf16[64,16,128]{2,1,0:T(8,128)(2,1)} custom-call(s32[2]{0:T(128)S(1)} %pad_add_fusion.place_ref, f32[16,8,128]{2,1,0:T(8,128)S(1)} %get-tuple-element.18.pos_ref, bf16[8,128,128]{2,1,0:T(8,128)(2,1)S(1)} %all_to_all.21.recv_ref, bf16[1024,768]{1,0:T(8,128)(2,1)S(1)} %copy-done.4), custom_call_target="tpu_custom_call" | custom-call | flops 2147483648 | bytes 4194304 | tf_op jit(solution)/shard_map/pallas_call | solution.py:594
  76.3 0.0 copy-start
  76.3 6.7 %all-to-all-start.3 = ((bf16[64,16,128]{2,1,0:T(8,128)(2,1)}), bf16[64,16,128]{2,1,0:T(8,128)(2,1)S(1)}, u32[]{:S(2)}, u32[]{:S(2)}) async-start(bf16[64,16,128]{2,1,0:T(8,128)(2,1)} %shard_map.112), calls=%async_computation.3 | async-start | bytes 524288 | tf_op jit(solution)/shard_map/all_to_all | solution.py:663
  83.1 0.0 copy-done.9
  83.1 0.1 copy.20
  83.2 0.0 copy-done.8
  83.2 12.8 %all_gather.3.group_ref = bf16[512,128]{1,0:T(8,128)(2,1)S(1)} all-gather(bf16[64,128]{1,0:T(8,128)(2,1)S(1)} %copy-done.8), channel_id=1, replica_groups=mesh['slab'=64,'pencil'=8] {'pencil'}, dimensions={0}, use_global_device_ids=true | all-gather | bytes 147456 | tf_op jit(solution)/shard_map/all_gather | solution.py:664
  95.9 0.0 copy-done.1
  95.9 0.0 copy-start.2
  95.9 0.9 copy-done.2
  96.8 3.3 %shard_map.113.side_ref = f32[264,128]{1,0:T(8,128)S(1)} custom-call(s32[64,1]{1,0:T(8,128)S(1)} %broadcast_and_fusion.ids_ref, f32[136,128]{1,0:T(8,128)S(1)} %copy-done.2, bf16[512,128]{1,0:T(8,128)(2,1)S(1)} %all_gather.3.group_ref, bf16[8192,128]{1,0:T(8,128)(2,1)S(1)} %bitcast.11), custom_call_target="tpu_custom_call" | custom-call | flops 268435456 | bytes 3145728 | tf_op jit(solution)/shard_map/pallas_call | solution.py:624
  100.1 3.4 %all-to-all-done.3.recv_ref = bf16[64,16,128]{2,1,0:T(8,128)(2,1)S(1)} async-done(((bf16[64,16,128]{2,1,0:T(8,128)(2,1)}), bf16[64,16,128]{2,1,0:T(8,128)(2,1)S(1)}, u32[]{:S(2)}, u32[]{:S(2)}) %all-to-all-start.3) | async-done | bytes 262176 | tf_op jit(solution)/shard_map/all_to_all | solution.py:663
  103.6 0.0 copy-done
  103.6 1.4 %shard_map.114 = f32[64,128]{1,0:T(8,128)} custom-call(f32[264,128]{1,0:T(8,128)S(1)} %shard_map.113.side_ref, bf16[64,16,128]{2,1,0:T(8,128)(2,1)S(1)} %all-to-all-done.3.recv_ref, bf16[4096,128]{1,0:T(8,128)(2,1)S(1)} %bitcast.10), custom_call_target="tpu_custom_call" | custom-call | flops 67108864 | bytes 2097152 | tf_op jit(solution)/shard_map/pallas_call | solution.py:612
  (2 shorter events, 0.0 us)
Async XLA Ops:
  2.8 41.0 %all-to-all-start = ((bf16[64,9,2,128]{3,2,1,0:T(2,128)(2,1)}), bf16[64,9,2,128]{3,2,1,0:T(2,128)(2,1)S(1)}, u32[]{:S(2)}, u32[]{:S(2)}) async-start(bf16[64,9,2,128]{3,2,1,0:T(2,128)(2,1)} %get-tuple-element.15), calls=%async_computation | async-start | bytes 589824 | tf_op jit(solution)/shard_map/all_to_all | solution.py:654
  24.5 19.3 %copy-start.3 = (bf16[1024,768]{1,0:T(8,128)(2,1)S(1)}, bf16[1024,768]{1,0:T(8,128)(2,1)}, u32[]{:S(2)}) copy-start(bf16[1024,768]{1,0:T(8,128)(2,1)} %constant.39.clone.table_ref) | copy-start | bytes 4718596
  43.8 16.3 %copy-start.5 = (bf16[2,256,256]{2,1,0:T(8,128)(2,1)S(1)}, bf16[2,256,256]{2,1,0:T(8,128)(2,1)}, u32[]{:S(2)}) copy-start(bf16[2,256,256]{2,1,0:T(8,128)(2,1)} %constant.41.clone.forward_ref) | copy-start | bytes 786436
  43.8 16.3 %copy-start.6 = (bf16[2,256,256]{2,1,0:T(8,128)(2,1)S(1)}, bf16[2,256,256]{2,1,0:T(8,128)(2,1)}, u32[]{:S(2)}) copy-start(bf16[2,256,256]{2,1,0:T(8,128)(2,1)} %constant.42.clone.inverse_ref) | copy-start | bytes 786436
  43.8 16.3 %copy-start.7 = (f32[16,128]{1,0:T(8,128)S(1)}, f32[16,128]{1,0:T(8,128)}, u32[]{:S(2)}) copy-start(f32[16,128]{1,0:T(8,128)} %constant.40.clone.turn_ref) | copy-start | bytes 24580
  48.3 23.5 %copy-start.4 = (bf16[1024,768]{1,0:T(8,128)(2,1)S(1)}, bf16[1024,768]{1,0:T(8,128)(2,1)}, u32[]{:S(2)}) copy-start(bf16[1024,768]{1,0:T(8,128)(2,1)} %constant.39.clone.table_ref) | copy-start | bytes 4718596
  71.8 11.3 %copy-start.9 = (s32[64,1]{0,1:T(1,128)S(1)}, s32[64,1]{0,1:T(1,128)}, u32[]{:S(2)}) copy-start(s32[64,1]{0,1:T(1,128)} %param.14) | copy-start | bytes 772
  71.8 11.4 %copy-start.8 = (bf16[64,128]{1,0:T(8,128)(2,1)S(1)}, bf16[64,128]{1,0:T(8,128)(2,1)}, u32[]{:S(2)}) copy-start(bf16[64,128]{1,0:T(8,128)(2,1)} %coef_hbm.1) | copy-start | bytes 49156
  71.8 24.1 %copy-start.1 = (bf16[64,1,128,128]{3,2,1,0:T(8,128)(2,1)S(1)}, bf16[64,1,128,128]{3,2,1,0:T(8,128)(2,1)}, u32[]{:S(2)}) copy-start(bf16[64,1,128,128]{3,2,1,0:T(8,128)(2,1)} %param.13) | copy-start | bytes 6291460
  76.3 27.3 %copy-start = (bf16[64,64,128]{2,1,0:T(8,128)(2,1)S(1)}, bf16[64,64,128]{2,1,0:T(8,128)(2,1)}, u32[]{:S(2)}) copy-start(bf16[64,64,128]{2,1,0:T(8,128)(2,1)} %param.12) | copy-start | bytes 3145732
  76.3 27.2 %all-to-all-start.3 = ((bf16[64,16,128]{2,1,0:T(8,128)(2,1)}), bf16[64,16,128]{2,1,0:T(8,128)(2,1)S(1)}, u32[]{:S(2)}, u32[]{:S(2)}) async-start(bf16[64,16,128]{2,1,0:T(8,128)(2,1)} %shard_map.112), calls=%async_computation.3 | async-start | bytes 524288 | tf_op jit(solution)/shard_map/all_to_all | solution.py:663
  95.9 0.9 copy-start.2
